TPU v7x, 256 devices: a whole 4x4x8 slice. The times are simulated.
256 devices in a mesh: dp: 64 (over z, y, core), rep: 4 (over x).
Axes of the slice: x: 4, y: 4, z: 8, core: 2. Of those that a mesh axis runs over, the one named last changes fastest.
Arguments:
- grads: bfloat16 [256, 4096, 512], P(('dp', 'rep')), may hold values from -1000 to 1000
- master: float32 [4096, 512], P('dp'), may hold values from -3 to 3
- first_moment: float32 [4096, 512], P('dp'), may hold values from -2 to 2
- second_moment: float32 [4096, 512], P('dp'), may hold values from 0.01 to 1
Outputs:
- weights: bfloat16 [4096, 512], replicated
- new_master: float32 [4096, 512], P('dp')
- new_first: float32 [4096, 512], P('dp')
- new_second: float32 [4096, 512], P('dp')
All inputs are finite; a program needn't handle non-finite values.
Results may differ from a plain program's by a relative error of at most 0.001.
Values may be sent and summed in bfloat16 or wider, within the bound.
No kernel may reach another device: no remote copies, remote signals or barrier semaphores. Data moves between devices by JAX's collectives and lax.ppermute only.
A program may use at most 64 MiB of HBM per device.

v0:
```python
import math

import jax
import jax.numpy as jnp
from jax import lax
from jax.sharding import Mesh
from jax.sharding import PartitionSpec as P

D_WIN = 4096
STEP = 20
DP = ("dp_0", "dp_1", "dp_2")
DP_REP = ("dp_0", "dp_1", "dp_2", "rep")


def sum_by_axis(shard, axes, dim):
    for axis in axes:
        shard = lax.psum_scatter(shard, axis, scatter_dimension=dim, tiled=True)
    return shard


def from_everyone(shard, axis):
    length = lax.axis_size(axis)
    return lax.all_to_all(
        jnp.broadcast_to(shard[None], (length, *shard.shape)), axis, 0, 0, tiled=True
    )


def of_everyone(shard, axis):
    everything = from_everyone(shard, axis)
    return jnp.sum(everything, axis=0)


def laid_out(pieces, dim):
    dims = list(pieces.shape[1:])
    dims[dim] *= pieces.shape[0]
    return jnp.moveaxis(pieces, 0, dim).reshape(dims)


def gather_in_order(shard, axes, order):
    pieces = shard[None]
    for k in order:
        pieces = lax.all_gather(pieces, axes[k], axis=0, tiled=True)
    block = [lax.axis_size(axes[k]) for k in reversed(order)]
    pieces = pieces.reshape(*block, *shard.shape)
    turned = sorted(range(len(order)), key=lambda place: order[len(order) - 1 - place])
    return pieces.transpose(*turned, *range(len(order), pieces.ndim)).reshape(-1, *shard.shape)


def whole_of(shard, axes, order, dim):
    return laid_out(gather_in_order(shard, axes, order), dim)


def adam_update(clipped, master, first_moment, second_moment):
    new_first = 0.9 * first_moment + 0.1 * clipped
    new_second = 0.95 * second_moment + 0.05 * clipped * clipped
    first_hat = new_first / (1.0 - 0.9**STEP)
    second_hat = new_second / (1.0 - 0.95**STEP)
    update = first_hat / (jnp.sqrt(second_hat) + 1e-08)
    new_master = master - 0.01 * (update + 0.1 * master)
    return (new_master, new_first, new_second)


def clip_factor(squares, width):
    threshold = 4.0 * math.sqrt(D_WIN * width)
    return jnp.minimum(1.0, threshold / (jnp.sqrt(squares) + 1e-06))


def body(grads, master, first_moment, second_moment):
    width = grads.shape[2]
    local = grads[0].astype(jnp.float32)
    owners = sum_by_axis(local, DP, 0)
    summed = of_everyone(owners, "rep")
    squares = of_everyone(jnp.sum(summed * summed), DP)
    factor = clip_factor(squares, width)
    new_master, new_first, new_second = adam_update(
        factor * summed, master, first_moment, second_moment
    )
    weights = whole_of(new_master.astype(jnp.bfloat16), DP, (1, 0, 2), 0)
    return (weights, new_master, new_first, new_second)


def solution(mesh):
    split = Mesh(mesh.devices.reshape(8, 4, 2, mesh.shape["rep"]), ("dp_0", "dp_1", "dp_2", "rep"))
    placed = (P(DP_REP, None, None), P(DP, None), P(DP, None), P(DP, None))
    return jax.shard_map(
        body,
        mesh=split,
        in_specs=placed,
        out_specs=(P(), P(DP, None), P(DP, None), P(DP, None)),
        check_vma=False,
    )
```

profile of v0, /device:TPU:1, one launch (start us, length us, event | category | flops | bytes accessed | tf_op | source)
XLA Modules:
  0.0 272.5 jit_solution(14857958143674053917)
XLA Ops:
  7.2 0.0 reduce-scatter.4.cloned.1.call-start
  7.2 6.6 %bitcast_convert_fusion = f32[4096,512]{1,0:T(8,128)} fusion(bf16[1,4096,512]{2,1,0:T(8,128)(2,1)} %param.4), kind=kLoop, calls=%fused_computation | loop fusion | flops 2097152 | bytes 12582912 | tf_op jit(solution)/shard_map/convert_element_type | solution.py:70
  13.8 0.0 reduce-scatter.4.cloned.1.call-update
  13.8 0.0 reduce-scatter.6.cloned.1.call-start
  13.9 98.9 %reduce-scatter.4.cloned.1.call-done = f32[512,512]{1,0:T(8,128)} async-done(((f32[4096,512]{1,0:T(8,128)}), f32[512,512]{1,0:T(8,128)}) %reduce-scatter.4.cloned.1.call-update) | async-done | bytes 1048592 | tf_op jit(solution)/shard_map/reduce_scatter | solution.py:17
  112.8 0.0 reduce-scatter.6.cloned.1.call-update
  112.8 0.0 reduce-scatter.8.cloned.1.call-start
  112.8 25.8 %reduce-scatter.6.cloned.1.call-done = f32[128,512]{1,0:T(8,128)} async-done(((f32[512,512]{1,0:T(8,128)}), f32[128,512]{1,0:T(8,128)}) %reduce-scatter.6.cloned.1.call-update) | async-done | bytes 262160 | tf_op jit(solution)/shard_map/reduce_scatter | solution.py:17
  138.6 0.0 reduce-scatter.8.cloned.1.call-update
  138.6 0.0 all-gather.4.cloned.1.call-start
  138.7 17.4 %reduce-scatter.8.cloned.1.call-done = f32[64,512]{1,0:T(8,128)} async-done(((f32[128,512]{1,0:T(8,128)}), f32[64,512]{1,0:T(8,128)}) %reduce-scatter.8.cloned.1.call-update) | async-done | bytes 131088 | tf_op jit(solution)/shard_map/reduce_scatter | solution.py:17
  156.1 1.0 broadcast_in_dim.6
  157.1 12.7 %all_to_all.11 = f32[4,64,512]{2,1,0:T(8,128)S(1)} all-to-all(f32[4,64,512]{2,1,0:T(8,128)S(1)} %broadcast_in_dim.6), channel_id=1, replica_groups=mesh['dp_0'=8,'dp_1'=4,'dp_2'=2,'rep'=4] {'rep'}, dimensions={0} | all-to-all | bytes 1048576 | tf_op jit(solution)/shard_map/all_to_all | solution.py:23
  169.8 0.6 multiply_reduce_fusion
  170.4 0.7 broadcast_in_dim.7
  171.1 20.5 %all_to_all.12 = f32[64,1,1]{2,1,0:T(1,128)S(1)} all-to-all(f32[64,1,1]{2,1,0:T(1,128)S(1)} %broadcast_in_dim.7), channel_id=1, replica_groups=mesh['dp_0'=8,'dp_1'=4,'dp_2'=2,'rep'=4] {'dp_0','dp_1','dp_2'}, dimensions={0} | all-to-all | bytes 512 | tf_op jit(solution)/shard_map/all_to_all | solution.py:23
  191.6 0.7 reduce_sum.29
  193.0 0.8 fusion.1
  193.8 10.1 %all-gather = bf16[256,512]{1,0:T(8,128)(2,1)} all-gather(bf16[64,512]{1,0:T(8,128)(2,1)S(1)} %get-tuple-element.4), channel_id=2, replica_groups=mesh['dp_0'=8,'dp_1'=4,'dp_2'=2,'rep'=4] {'dp_1'}, dimensions={0}, use_global_device_ids=true | all-gather | bytes 327680 | tf_op jit(solution)/shard_map/all_gather | solution.py:42
  203.9 0.0 all-gather.4.cloned.1.call-update
  203.9 0.0 all-gather.6.cloned.1.call-start
  204.0 33.7 %all-gather.4.cloned.1.call-done = bf16[32,64,512]{2,1,0:T(8,128)(2,1)} async-done(((bf16[4,64,512]{2,1,0:T(8,128)(2,1)}), bf16[32,64,512]{2,1,0:T(8,128)(2,1)}) %all-gather.4.cloned.1.call-update) | async-done | bytes 2097168 | tf_op jit(solution)/shard_map/all_gather | solution.py:42
  237.7 23.6 %all-gather.6.cloned.1.call-done = bf16[64,64,512]{2,1,0:T(8,128)(2,1)} async-done(((bf16[32,64,512]{2,1,0:T(8,128)(2,1)}), bf16[64,64,512]{2,1,0:T(8,128)(2,1)}) %all-gather.6.cloned.1.call-update) | async-done | bytes 4194320 | tf_op jit(solution)/shard_map/all_gather | solution.py:42
  261.3 4.7 %copy.12 = bf16[8,4,2,64,512]{4,3,2,1,0:T(8,128)(2,1)} copy(bf16[8,4,2,64,512]{4,3,1,0,2:T(8,128)(2,1)} %bitcast.9) | data formatting | bytes 8388608 | tf_op jit(solution)/shard_map/transpose | solution.py:46
  (8 shorter events, 0.1 us)
Async XLA Ops:
  7.2 105.6 %reduce-scatter.4.cloned.1.call-start = ((), (), s32[]{:S(2)}) async-start(), calls=%async_computation.5 | async-start | bytes 9437184 | tf_op jit(solution)/shard_map/reduce_scatter | solution.py:17
  13.8 179.2 %copy-start = (f32[64,512]{1,0:T(8,128)S(1)}, f32[64,512]{1,0:T(8,128)}, u32[]{:S(2)}) copy-start(f32[64,512]{1,0:T(8,128)} %param.5) | copy-start | bytes 393220
  13.8 179.2 %copy-start.1 = (f32[64,512]{1,0:T(8,128)S(1)}, f32[64,512]{1,0:T(8,128)}, u32[]{:S(2)}) copy-start(f32[64,512]{1,0:T(8,128)} %param.6) | copy-start | bytes 393220
  13.8 179.2 %copy-start.2 = (f32[64,512]{1,0:T(8,128)S(1)}, f32[64,512]{1,0:T(8,128)}, u32[]{:S(2)}) copy-start(f32[64,512]{1,0:T(8,128)} %param.7) | copy-start | bytes 393220
  13.8 124.8 %reduce-scatter.6.cloned.1.call-start = ((), (), s32[]{:S(2)}) async-start(), calls=%async_computation.6 | async-start | bytes 1310720 | tf_op jit(solution)/shard_map/reduce_scatter | solution.py:17
  112.8 43.3 %reduce-scatter.8.cloned.1.call-start = ((), (), s32[]{:S(2)}) async-start(), calls=%async_computation.7 | async-start | bytes 393216 | tf_op jit(solution)/shard_map/reduce_scatter | solution.py:17
  138.6 99.0 %all-gather.4.cloned.1.call-start = ((), (), s32[]{:S(2)}) async-start(), calls=%async_computation.8 | async-start | bytes 2359296 | tf_op jit(solution)/shard_map/all_gather | solution.py:42
  203.9 57.4 %all-gather.6.cloned.1.call-start = ((), (), s32[]{:S(2)}) async-start(), calls=%async_computation.9 | async-start | bytes 6291456 | tf_op jit(solution)/shard_map/all_gather | solution.py:42
Sparse Core Ops, SparseCore 0:
  14.0 98.7 reduce-scatter.3
  115.3 23.2 reduce-scatter.5
  141.3 14.8 reduce-scatter.7
  204.0 33.5 all-gather.3
  239.3 21.9 all-gather.5
where the time goes:
time: 273 us
  waiting for transfers between devices  199 us (73%)
  blocking collectives  43.2 us (16%)
  between operations  14.6 us (5%)
  other arithmetic  8.75 us (3%)
  local copies, waits for them, and re-layouts  6.32 us (2%)
    reduce_scatter x3, waiting for transfers between devices, sum_by_axis(): shard = lax.psum_scatter(shard, axis, scatter_dimension=dim, tiled=True)  142 us
    all_gather x2, waiting for transfers between devices, gather_in_order(): pieces = lax.all_gather(pieces, axes[k], axis=0, tiled=True)  57.3 us
    all_to_all x2, blocking collectives, from_everyone(): lax.all_to_all(jnp.broadcast_to(shard[None], (length, *shard.shape)), axi...  33.1 us
    all_gather x1, blocking collectives, gather_in_order(): pieces = lax.all_gather(pieces, axes[k], axis=0, tiled=True)  10.1 us
    convert_element_type x1, other arithmetic, body(): local = grads[0].astype(jnp.float32)  6.6 us
  transfers between devices with their start and end apart: 5, of which 5 were waited for; matrix products, arithmetic and copies ran while one was open for 0% of the time, Pallas kernels for 0%

commit v1 on v0

v1 whole, which is shorter than its diff:
```python
import math

import jax
import jax.numpy as jnp
from jax import lax
from jax.sharding import Mesh
from jax.sharding import PartitionSpec as P

D_WIN = 4096
STEP = 20
AXES = ("zh", "zl", "y", "c", "x")
GROUP = ("zl", "y", "c", "x")


def to_all(block, axes):
    length = lax.axis_size(axes)
    return lax.all_to_all(
        jnp.broadcast_to(block[None], (length, *block.shape)), axes, 0, 0, tiled=True
    )


def adam_update(clipped, master, first_moment, second_moment):
    new_first = 0.9 * first_moment + 0.1 * clipped
    new_second = 0.95 * second_moment + 0.05 * clipped * clipped
    first_hat = new_first / (1.0 - 0.9**STEP)
    second_hat = new_second / (1.0 - 0.95**STEP)
    update = first_hat / (jnp.sqrt(second_hat) + 1e-08)
    new_master = master - 0.01 * (update + 0.1 * master)
    return (new_master, new_first, new_second)


def clip_factor(squares, width):
    threshold = 4.0 * math.sqrt(D_WIN * width)
    return jnp.minimum(1.0, threshold / (jnp.sqrt(squares) + 1e-06))


def ring(block, axis):
    n = lax.axis_size(axis)
    return [
        lax.ppermute(block, axis, [(i, (i + k) % n) for i in range(n)]) for k in range(1, n)
    ]


def gather_ring(block, axis):
    n = lax.axis_size(axis)
    me = lax.axis_index(axis)
    parts = [block] + ring(block, axis)
    out = jnp.zeros((n, *block.shape), block.dtype)
    for k, part in enumerate(parts):
        out = lax.dynamic_update_index_in_dim(out, part, lax.rem(me - k + n, n), 0)
    return out


def body(grads, master, first_moment, second_moment):
    width = grads.shape[2]
    zh, zl, y, c, x = (lax.axis_size(a) for a in AXES)
    rows = master.shape[0] // x
    me_x = lax.axis_index("x")
    me_zh = lax.axis_index("zh")

    own = jnp.concatenate([
        lax.dynamic_slice_in_dim(a, me_x * rows, rows, 0)
        for a in (master, first_moment, second_moment)
    ])
    states = gather_ring(own, "zh")
    states = states.reshape(zh, 3, rows, width).transpose(1, 0, 2, 3).reshape(3, zh * rows, width)

    local = grads[0].reshape(zh, zl, y, c, x, rows, width)
    local = local.transpose(1, 2, 3, 4, 0, 5, 6).reshape(-1, zh * rows, width)
    pieces = lax.all_to_all(local, GROUP, 0, 0, tiled=True)
    partial = jnp.sum(pieces.astype(jnp.float32), axis=0)
    total = jnp.sum(to_all(partial, "zh"), axis=0)

    mine = lax.dynamic_slice_in_dim(total, me_zh * rows, rows, 0)
    owned = gather_ring(mine, "x").reshape(-1, width)

    squares = jnp.sum(to_all(jnp.sum(total * total), GROUP))
    factor = clip_factor(squares, width)

    ahead = adam_update(factor * total, states[0], states[1], states[2])[0]
    gathered = to_all(ahead.astype(jnp.bfloat16), ("zl", "y", "x"))
    both = to_all(gathered, "c")
    weights = both.reshape(c, zl, y, x, zh, rows, width).transpose(4, 1, 2, 0, 3, 5, 6)
    weights = weights.reshape(-1, width)

    new_master, new_first, new_second = adam_update(
        factor * owned, master, first_moment, second_moment
    )
    return (weights, new_master, new_first, new_second)


def solution(mesh):
    split = Mesh(mesh.devices.reshape(4, 2, 4, 2, mesh.shape["rep"]), AXES)
    dp = AXES[:4]
    placed = (P(AXES, None, None), P(dp, None), P(dp, None), P(dp, None))
    return jax.shard_map(
        body,
        mesh=split,
        in_specs=placed,
        out_specs=(P(), P(dp, None), P(dp, None), P(dp, None)),
        check_vma=False,
    )
```

time: 273 us -> 160 us (0.59)
  waiting for transfers between devices: 199 us -> 87.7 us
  starting transfers between devices: 0.2 us -> 44.9 us
  blocking collectives: 43.2 us -> 8.6 us
  between operations: 14.6 us -> 1.59 us
  local copies, waits for them, and re-layouts: 6.32 us -> 11.7 us
  other arithmetic: 8.75 us -> 5.15 us
    reduce_scatter x3 -> x0, waiting for transfers between devices: 142 us -> none  [sum_by_axis(): shard = lax.psum_scatter(shard, axis, scatter_dimension=dim, tiled=True)]
    all_to_all x0 -> x4, waiting for transfers between devices: none -> 65.6 us  [the longest x1 43.6 us: body(): pieces = lax.all_to_all(local, GROUP, 0, 0, tiled=True)]
    all_gather x2 -> x0, waiting for transfers between devices: 57.3 us -> none  [gather_in_order(): pieces = lax.all_gather(pieces, axes[k], axis=0, tiled=True)]
    all_to_all x0 -> x4, starting transfers between devices: none -> 30.4 us  [the longest x3 19.8 us: to_all(): lax.all_to_all(jnp.broadcast_to(block[None], (length, *block.shape)), axe...]
    all_to_all x2 -> x1, blocking collectives: 33.1 us -> 8.6 us  [to_all(): lax.all_to_all(jnp.broadcast_to(block[None], (length, *block.shape)), axe...]
    ppermute x0 -> x6, waiting for transfers between devices: none -> 22.1 us  [ring(): lax.ppermute(block, axis, [(i, (i + k) % n) for i in range(n)])]
    ppermute x0 -> x6, starting transfers between devices: none -> 14.4 us  [ring(): lax.ppermute(block, axis, [(i, (i + k) % n) for i in range(n)])]
    all_gather x1 -> x0, blocking collectives: 10.1 us -> none  [gather_in_order(): pieces = lax.all_gather(pieces, axes[k], axis=0, tiled=True)]
  transfers between devices with their start and end apart: 5 -> 10, of which waited for: 5 -> 5; matrix products, arithmetic and copies ran while one was open for 0% -> 3% of each run, Pallas kernels for 0% -> 0%
where the time goes in v1:
time: 160 us
  waiting for transfers between devices  87.7 us (55%)
  starting transfers between devices  44.9 us (28%)
  local copies, waits for them, and re-layouts  11.7 us (7%)
  blocking collectives  8.6 us (5%)
  other arithmetic  5.15 us (3%)
    all_to_all x1, waiting for transfers between devices, body(): pieces = lax.all_to_all(local, GROUP, 0, 0, tiled=True)  43.6 us
    ppermute x6, waiting for transfers between devices, ring(): lax.ppermute(block, axis, [(i, (i + k) % n) for i in range(n)])  22.1 us
    all_to_all x3, waiting for transfers between devices, to_all(): lax.all_to_all(jnp.broadcast_to(block[None], (length, *block.shape)), axe...  22 us
    all_to_all x3, starting transfers between devices, to_all(): lax.all_to_all(jnp.broadcast_to(block[None], (length, *block.shape)), axe...  19.8 us
    ppermute x6, starting transfers between devices, ring(): lax.ppermute(block, axis, [(i, (i + k) % n) for i in range(n)])  14.4 us
    all_to_all x1, starting transfers between devices, body(): pieces = lax.all_to_all(local, GROUP, 0, 0, tiled=True)  10.7 us
    all_to_all x1, blocking collectives, to_all(): lax.all_to_all(jnp.broadcast_to(block[None], (length, *block.shape)), axe...  8.6 us
    transpose x1, local copies, waits for them, and re-layouts, body(): local = local.transpose(1, 2, 3, 4, 0, 5, 6).reshape(-1, zh * rows, width)  4.86 us
  transfers between devices with their start and end apart: 10, of which 5 were waited for; matrix products, arithmetic and copies ran while one was open for 3% of the time, Pallas kernels for 0%

profile of v1, /device:TPU:1, one launch (start us, length us, event | category | flops | bytes accessed | tf_op | source)
XLA Modules:
  0.0 159.6 jit_solution(8523110251453262956)
XLA Ops:
  0.6 4.9 %copy.12 = bf16[2,4,2,4,4,16,512]{6,5,4,3,2,1,0:T(8,128)(2,1)} copy(bf16[2,4,2,4,4,16,512]{6,5,3,2,1,0,4:T(8,128)(2,1)} %bitcast.57) | data formatting | bytes 8388608 | tf_op jit(solution)/shard_map/transpose | solution.py:69
  5.5 10.7 %all-to-all-start = ((bf16[64,64,512]{2,1,0:T(8,128)(2,1)}), bf16[64,64,512]{2,1,0:T(8,128)(2,1)}, u32[]{:S(2)}, u32[]{:S(2)}) async-start(bf16[64,64,512]{2,1,0:T(8,128)(2,1)} %bitcast.55), calls=%async_computation | async-start | bytes 8388608 | tf_op jit(solution)/shard_map/all_to_all | solution.py:70
  16.3 3.1 %collective-permute-start = (f32[48,512]{1,0:T(8,128)S(1)}, f32[48,512]{1,0:T(8,128)S(1)}, u32[]{:S(2)}, u32[]{:S(2)}) collective-permute-start(f32[48,512]{1,0:T(8,128)S(1)} %pad_maximum_fusion), channel_id=1, source_target_pairs={{0,64},{64,128},{128,192},{192,0},{1,65},{65,129},{129,193},{193,1... | collective-permute-start | bytes 294920 | tf_op jit(solution)/shard_map/ppermute | solution.py:40
  19.3 4.2 %collective-permute-start.1 = (f32[48,512]{1,0:T(8,128)S(1)}, f32[48,512]{1,0:T(8,128)S(1)}, u32[]{:S(2)}, u32[]{:S(2)}) collective-permute-start(f32[48,512]{1,0:T(8,128)S(1)} %pad_maximum_fusion), channel_id=1, source_target_pairs={{0,128},{64,192},{128,0},{192,64},{1,129},{65,193},{129,1},{193,65... | collective-permute-start | bytes 294920 | tf_op jit(solution)/shard_map/ppermute | solution.py:40
  23.5 2.4 %collective-permute-start.2 = (f32[48,512]{1,0:T(8,128)S(1)}, f32[48,512]{1,0:T(8,128)S(1)}, u32[]{:S(2)}, u32[]{:S(2)}) collective-permute-start(f32[48,512]{1,0:T(8,128)S(1)} %pad_maximum_fusion), channel_id=1, source_target_pairs={{0,192},{64,0},{128,64},{192,128},{1,193},{65,1},{129,65},{193,129... | collective-permute-start | bytes 294920 | tf_op jit(solution)/shard_map/ppermute | solution.py:40
  25.9 43.6 %all-to-all-done = bf16[64,64,512]{2,1,0:T(8,128)(2,1)} async-done(((bf16[64,64,512]{2,1,0:T(8,128)(2,1)}), bf16[64,64,512]{2,1,0:T(8,128)(2,1)}, u32[]{:S(2)}, u32[]{:S(2)}) %all-to-all-start) | async-done | bytes 4194336 | tf_op jit(solution)/shard_map/all_to_all | solution.py:70
  69.5 2.8 %convert_reduce_fusion = f32[64,512]{1,0:T(8,128)S(1)} fusion(bf16[64,64,512]{2,1,0:T(8,128)(2,1)} %all-to-all-done), kind=kLoop, calls=%fused_computation | loop fusion | flops 4161536 | bytes 4325376 | tf_op jit(solution)/shard_map/reduce_sum | solution.py:71
  72.3 0.9 broadcast_in_dim.61
  73.2 8.4 %all-to-all-start.1 = ((f32[4,64,512]{2,1,0:T(8,128)}), f32[4,64,512]{2,1,0:T(8,128)S(1)}, u32[]{:S(2)}, u32[]{:S(2)}) async-start(f32[4,64,512]{2,1,0:T(8,128)} %broadcast_in_dim.61), calls=%async_computation.1 | async-start | bytes 1048576 | tf_op jit(solution)/shard_map/all_to_all | solution.py:17
  81.8 14.1 %all-to-all-done.1 = f32[4,64,512]{2,1,0:T(8,128)S(1)} async-done(((f32[4,64,512]{2,1,0:T(8,128)}), f32[4,64,512]{2,1,0:T(8,128)S(1)}, u32[]{:S(2)}, u32[]{:S(2)}) %all-to-all-start.1) | async-done | bytes 524320 | tf_op jit(solution)/shard_map/all_to_all | solution.py:17
  96.6 1.3 broadcast_in_dim.62
  97.8 7.3 %all-to-all-start.2 = ((f32[64,1,1]{2,1,0:T(1,128)}), f32[64,1,1]{2,1,0:T(1,128)S(1)}, u32[]{:S(2)}, u32[]{:S(2)}) async-start(f32[64,1,1]{2,1,0:T(1,128)} %broadcast_in_dim.62), calls=%async_computation.2 | async-start | bytes 65536 | tf_op jit(solution)/shard_map/all_to_all | solution.py:17
  105.2 7.9 %all-to-all-done.2 = f32[64,1,1]{2,1,0:T(1,128)S(1)} async-done(((f32[64,1,1]{2,1,0:T(1,128)}), f32[64,1,1]{2,1,0:T(1,128)S(1)}, u32[]{:S(2)}, u32[]{:S(2)}) %all-to-all-start.2) | async-done | bytes 288 | tf_op jit(solution)/shard_map/all_to_all | solution.py:17
  113.1 0.7 reduce_sum.39
  114.6 1.6 broadcast_in_dim.63
  116.2 4.0 %all-to-all-start.3 = ((bf16[32,64,512]{2,1,0:T(8,128)(2,1)}), bf16[32,64,512]{2,1,0:T(8,128)(2,1)S(1)}, u32[]{:S(2)}, u32[]{:S(2)}) async-start(bf16[32,64,512]{2,1,0:T(8,128)(2,1)} %broadcast_in_dim.63), calls=%async_computation.3 | async-start | bytes 4194304 | tf_op jit(solution)/shard_map/all_to_all | solution.py:17
  120.3 1.2 collective-permute-start.3
  121.5 2.4 %collective-permute-start.4 = (f32[16,512]{1,0:T(8,128)S(1)}, f32[16,512]{1,0:T(8,128)S(1)}, u32[]{:S(2)}, u32[]{:S(2)}) collective-permute-start(f32[16,512]{1,0:T(8,128)S(1)} %get-tuple-element.8), channel_id=1, source_target_pairs={{0,2},{1,3},{2,0},{3,1},{4,6},{5,7},{6,4},{7,5},{8,10},{9,11},{10,... | collective-permute-start | bytes 98312 | tf_op jit(solution)/shard_map/ppermute | solution.py:40
  123.9 1.2 collective-permute-start.5
  125.0 16.2 %collective-permute-done.3 = f32[16,512]{1,0:T(8,128)S(1)} collective-permute-done((f32[16,512]{1,0:T(8,128)S(1)}, f32[16,512]{1,0:T(8,128)S(1)}, u32[]{:S(2)}, u32[]{:S(2)}) %collective-permute-start.3) | collective-permute-done | bytes 32800 | tf_op jit(solution)/shard_map/ppermute | solution.py:40
  141.2 5.9 %collective-permute-done.4 = f32[16,512]{1,0:T(8,128)S(1)} collective-permute-done((f32[16,512]{1,0:T(8,128)S(1)}, f32[16,512]{1,0:T(8,128)S(1)}, u32[]{:S(2)}, u32[]{:S(2)}) %collective-permute-start.4) | collective-permute-done | bytes 32800 | tf_op jit(solution)/shard_map/ppermute | solution.py:40
  147.2 0.8 multiply_subtract_fusion
  148.5 8.6 %all_to_all.26 = bf16[2,32,64,512]{3,2,1,0:T(8,128)(2,1)S(1)} all-to-all(bf16[2,32,64,512]{3,2,1,0:T(8,128)(2,1)S(1)} %broadcast_in_dim.64), channel_id=1, replica_groups=mesh['zh'=4,'zl'=2,'y'=4,'c'=2,'x'=4] {'c'}, dimensions={0} | all-to-all | bytes 8388608 | tf_op jit(solution)/shard_map/all_to_all | solution.py:17
  157.1 2.5 %copy.14 = bf16[4,2,4,2,4,16,512]{6,5,4,3,2,1,0:T(8,128)(2,1)} copy(bf16[4,2,4,2,4,16,512]{6,5,0,4,2,1,3:T(8,128)(2,1)S(1)} %bitcast.56) | data formatting | bytes 8388608 | tf_op jit(solution)/shard_map/transpose | solution.py:83
  (30 shorter events, 1.5 us)
Async XLA Ops:
  5.5 10.7 %copy-start = (f32[64,512]{1,0:T(8,128)S(1)}, f32[64,512]{1,0:T(8,128)}, u32[]{:S(2)}) copy-start(f32[64,512]{1,0:T(8,128)} %param.5) | copy-start | bytes 393220
  5.5 10.7 %copy-start.1 = (f32[64,512]{1,0:T(8,128)S(1)}, f32[64,512]{1,0:T(8,128)}, u32[]{:S(2)}) copy-start(f32[64,512]{1,0:T(8,128)} %param.7) | copy-start | bytes 393220
  5.5 10.7 %copy-start.2 = (f32[64,512]{1,0:T(8,128)S(1)}, f32[64,512]{1,0:T(8,128)}, u32[]{:S(2)}) copy-start(f32[64,512]{1,0:T(8,128)} %param.6) | copy-start | bytes 393220
  5.5 64.0 %all-to-all-start = ((bf16[64,64,512]{2,1,0:T(8,128)(2,1)}), bf16[64,64,512]{2,1,0:T(8,128)(2,1)}, u32[]{:S(2)}, u32[]{:S(2)}) async-start(bf16[64,64,512]{2,1,0:T(8,128)(2,1)} %bitcast.55), calls=%async_computation | async-start | bytes 8388608 | tf_op jit(solution)/shard_map/all_to_all | solution.py:70
  16.3 65.4 %collective-permute-start = (f32[48,512]{1,0:T(8,128)S(1)}, f32[48,512]{1,0:T(8,128)S(1)}, u32[]{:S(2)}, u32[]{:S(2)}) collective-permute-start(f32[48,512]{1,0:T(8,128)S(1)} %pad_maximum_fusion), channel_id=1, source_target_pairs={{0,64},{64,128},{128,192},{192,0},{1,65},{65,129},{129,193},{193,1... | collective-permute-start | bytes 294920 | tf_op jit(solution)/shard_map/ppermute | solution.py:40
  19.3 62.4 %collective-permute-start.1 = (f32[48,512]{1,0:T(8,128)S(1)}, f32[48,512]{1,0:T(8,128)S(1)}, u32[]{:S(2)}, u32[]{:S(2)}) collective-permute-start(f32[48,512]{1,0:T(8,128)S(1)} %pad_maximum_fusion), channel_id=1, source_target_pairs={{0,128},{64,192},{128,0},{192,64},{1,129},{65,193},{129,1},{193,65... | collective-permute-start | bytes 294920 | tf_op jit(solution)/shard_map/ppermute | solution.py:40
  23.5 58.2 %collective-permute-start.2 = (f32[48,512]{1,0:T(8,128)S(1)}, f32[48,512]{1,0:T(8,128)S(1)}, u32[]{:S(2)}, u32[]{:S(2)}) collective-permute-start(f32[48,512]{1,0:T(8,128)S(1)} %pad_maximum_fusion), channel_id=1, source_target_pairs={{0,192},{64,0},{128,64},{192,128},{1,193},{65,1},{129,65},{193,129... | collective-permute-start | bytes 294920 | tf_op jit(solution)/shard_map/ppermute | solution.py:40
  73.2 22.7 %all-to-all-start.1 = ((f32[4,64,512]{2,1,0:T(8,128)}), f32[4,64,512]{2,1,0:T(8,128)S(1)}, u32[]{:S(2)}, u32[]{:S(2)}) async-start(f32[4,64,512]{2,1,0:T(8,128)} %broadcast_in_dim.61), calls=%async_computation.1 | async-start | bytes 1048576 | tf_op jit(solution)/shard_map/all_to_all | solution.py:17
  97.8 15.3 %all-to-all-start.2 = ((f32[64,1,1]{2,1,0:T(1,128)}), f32[64,1,1]{2,1,0:T(1,128)S(1)}, u32[]{:S(2)}, u32[]{:S(2)}) async-start(f32[64,1,1]{2,1,0:T(1,128)} %broadcast_in_dim.62), calls=%async_computation.2 | async-start | bytes 65536 | tf_op jit(solution)/shard_map/all_to_all | solution.py:17
  116.2 31.8 %all-to-all-start.3 = ((bf16[32,64,512]{2,1,0:T(8,128)(2,1)}), bf16[32,64,512]{2,1,0:T(8,128)(2,1)S(1)}, u32[]{:S(2)}, u32[]{:S(2)}) async-start(bf16[32,64,512]{2,1,0:T(8,128)(2,1)} %broadcast_in_dim.63), calls=%async_computation.3 | async-start | bytes 4194304 | tf_op jit(solution)/shard_map/all_to_all | solution.py:17
  120.3 20.9 %collective-permute-start.3 = (f32[16,512]{1,0:T(8,128)S(1)}, f32[16,512]{1,0:T(8,128)S(1)}, u32[]{:S(2)}, u32[]{:S(2)}) collective-permute-start(f32[16,512]{1,0:T(8,128)S(1)} %get-tuple-element.8), channel_id=1, source_target_pairs={{0,1},{1,2},{2,3},{3,0},{4,5},{5,6},{6,7},{7,4},{8,9},{9,10},{10,1... | collective-permute-start | bytes 98312 | tf_op jit(solution)/shard_map/ppermute | solution.py:40
  121.5 25.7 %collective-permute-start.4 = (f32[16,512]{1,0:T(8,128)S(1)}, f32[16,512]{1,0:T(8,128)S(1)}, u32[]{:S(2)}, u32[]{:S(2)}) collective-permute-start(f32[16,512]{1,0:T(8,128)S(1)} %get-tuple-element.8), channel_id=1, source_target_pairs={{0,2},{1,3},{2,0},{3,1},{4,6},{5,7},{6,4},{7,5},{8,10},{9,11},{10,... | collective-permute-start | bytes 98312 | tf_op jit(solution)/shard_map/ppermute | solution.py:40
  123.9 23.3 %collective-permute-start.5 = (f32[16,512]{1,0:T(8,128)S(1)}, f32[16,512]{1,0:T(8,128)S(1)}, u32[]{:S(2)}, u32[]{:S(2)}) collective-permute-start(f32[16,512]{1,0:T(8,128)S(1)} %get-tuple-element.8), channel_id=1, source_target_pairs={{0,3},{1,0},{2,1},{3,2},{4,7},{5,4},{6,5},{7,6},{8,11},{9,8},{10,9... | collective-permute-start | bytes 98312 | tf_op jit(solution)/shard_map/ppermute | solution.py:40

commit v2 on v1

v2 whole, which is shorter than its diff:
```python
import math

import jax
import jax.numpy as jnp
from jax import lax
from jax.sharding import Mesh
from jax.sharding import PartitionSpec as P

D_WIN = 4096
STEP = 20
AXES = ("zh", "zl", "y", "c", "x")
PLANE = ("zl", "y", "x")
OWNERS = ("zl", "y", "c", "x")
SWAP = [(0, 1), (1, 0)]


def to_all(block, axes):
    length = lax.axis_size(axes)
    return lax.all_to_all(
        jnp.broadcast_to(block[None], (length, *block.shape)), axes, 0, 0, tiled=True
    )


def neighbour(block, axis, mask):
    return lax.ppermute(block, axis, [(i, i ^ mask) for i in range(4)])


def sum_of_four(block, axis):
    for mask in (1, 3):
        block = block + neighbour(block, axis, mask)
    return block


def gather_of_four(block, axis):
    me = lax.axis_index(axis)
    block = block[None]
    for mask, low in ((1, me % 2 == 0), (3, me < 2)):
        other = neighbour(block, axis, mask)
        block = jnp.concatenate([jnp.where(low, block, other), jnp.where(low, other, block)])
    return block


def gather_ring(block, axis):
    n = lax.axis_size(axis)
    me = lax.axis_index(axis)
    out = jnp.zeros((n, *block.shape), block.dtype)
    for k in range(n):
        part = lax.ppermute(block, axis, [(i, (i + k) % n) for i in range(n)]) if k else block
        out = lax.dynamic_update_index_in_dim(out, part, lax.rem(me - k + n, n), 0)
    return out


def encode(value):
    value = value * 2.0**20
    return (value * jnp.abs(value) * (value * value)).astype(jnp.bfloat16)


def decode(code):
    code = code.astype(jnp.float32)
    inverse = lax.rsqrt(jnp.maximum(jnp.abs(code), 1e-37))
    return (code * inverse) * (inverse * lax.rsqrt(inverse)) * 2.0**-20


def adam_update(clipped, master, first_moment, second_moment):
    new_first = 0.9 * first_moment + 0.1 * clipped
    new_second = 0.95 * second_moment + 0.05 * clipped * clipped
    first_hat = new_first / (1.0 - 0.9**STEP)
    second_hat = new_second / (1.0 - 0.95**STEP)
    update = first_hat / (jnp.sqrt(second_hat) + 1e-08)
    new_master = master - 0.01 * (update + 0.1 * master)
    return (new_master, new_first, new_second)


def clip_factor(squares, width):
    threshold = 4.0 * math.sqrt(D_WIN * width)
    return jnp.minimum(1.0, threshold / (jnp.sqrt(squares) + 1e-06))


def body(grads, master, first_moment, second_moment):
    width = grads.shape[2]
    zh, zl, y, c, x = (lax.axis_size(a) for a in AXES)
    rows = master.shape[0] // x
    me_c, me_x, me_zh = (lax.axis_index(a) for a in ("c", "x", "zh"))

    local = grads[0].reshape(zh, zl, y, c, x, rows, width)
    sent = lax.dynamic_index_in_dim(local, 1 - me_c, 3, keepdims=False)
    kept = lax.dynamic_index_in_dim(local, me_c, 3, keepdims=False)
    pair = kept.astype(jnp.float32) + lax.ppermute(sent, "c", SWAP).astype(jnp.float32)
    coded = encode(pair).transpose(1, 2, 3, 0, 4, 5).reshape(-1, zh * rows, width)
    pieces = lax.all_to_all(coded, PLANE, 0, 0, tiled=True)
    total = sum_of_four(jnp.sum(decode(pieces), axis=0), "zh")

    squares = jnp.sum(to_all(jnp.sum(total * total), OWNERS))
    factor = clip_factor(squares, width)

    mine = factor * lax.dynamic_slice_in_dim(total, me_zh * rows, rows, 0)
    quarter = (lax.dynamic_slice_in_dim(a, me_x * rows, rows, 0) for a in (master, first_moment, second_moment))
    ahead = adam_update(mine, *quarter)[0].astype(jnp.bfloat16)
    gathered = to_all(gather_of_four(ahead, "zh").reshape(-1, width), PLANE)
    owned = gather_ring(mine, "x").reshape(-1, width)
    gathered, owned = lax.optimization_barrier((gathered, owned))
    new_master, new_first, new_second = adam_update(owned, master, first_moment, second_moment)

    other = lax.ppermute(gathered, "c", SWAP)
    weights = jnp.zeros((zh, zl, y, c, x, rows, width), jnp.bfloat16)
    for half, place in ((gathered, me_c), (other, 1 - me_c)):
        half = half.reshape(zl, y, x, zh, rows, width).transpose(3, 0, 1, 2, 4, 5)
        weights = lax.dynamic_update_index_in_dim(weights, half, place, 3)
    return (weights.reshape(-1, width), new_master, new_first, new_second)


def solution(mesh):
    split = Mesh(mesh.devices.reshape(4, 2, 4, 2, mesh.shape["rep"]), AXES)
    dp = AXES[:4]
    placed = (P(AXES, None, None), P(dp, None), P(dp, None), P(dp, None))
    return jax.shard_map(
        body,
        mesh=split,
        in_specs=placed,
        out_specs=(P(), P(dp, None), P(dp, None), P(dp, None)),
        check_vma=False,
    )
```

time: 160 us -> 136 us (0.85)
  waiting for transfers between devices: 87.7 us -> 47.6 us
  blocking collectives: 8.6 us -> 33 us
  starting transfers between devices: 44.9 us -> 37.7 us
  local copies, waits for them, and re-layouts: 11.7 us -> 9.36 us
    all_to_all x1 -> x0, waiting for transfers between devices: 43.6 us -> none  [body(): pieces = lax.all_to_all(local, GROUP, 0, 0, tiled=True)]
    all_to_all x1, blocking collectives: 8.6 us -> 33 us  [body(): pieces = lax.all_to_all(coded, PLANE, 0, 0, tiled=True)]
    ppermute x6 -> x9, waiting for transfers between devices: 22.1 us -> 38.4 us  [the longest x3 18.4 us: gather_ring(): lax.ppermute(block, axis, [(i, (i + k) % n) for i in range(n)])]
    all_to_all x3 -> x2, waiting for transfers between devices: 22 us -> 9.16 us  [to_all(): lax.all_to_all(jnp.broadcast_to(block[None], (length, *block.shape)), axe...]
    all_to_all x1 -> x0, starting transfers between devices: 10.7 us -> none  [body(): pieces = lax.all_to_all(local, GROUP, 0, 0, tiled=True)]
    ppermute x6 -> x9, starting transfers between devices: 14.4 us -> 22.6 us  [the longest x4 9.42 us: neighbour(): return lax.ppermute(block, axis, [(i, i ^ mask) for i in range(4)])]
    transpose x2 -> x1, local copies, waits for them, and re-layouts: 7.34 us -> 0.2 us  [body(): encode(pair).transpose(1, 2, 3, 0, 4, 5).reshape(-1, zh * rows, width)]
    all_to_all x3 -> x2, starting transfers between devices: 19.8 us -> 15.1 us  [to_all(): lax.all_to_all(jnp.broadcast_to(block[None], (length, *block.shape)), axe...]
  transfers between devices with their start and end apart: 10 -> 11, of which waited for: 5 -> 10; matrix products, arithmetic and copies ran while one was open for 3% -> 1% of each run, Pallas kernels for 0% -> 0%
where the time goes in v2:
time: 136 us
  waiting for transfers between devices  47.6 us (35%)
  starting transfers between devices  37.7 us (28%)
  blocking collectives  33 us (24%)
  local copies, waits for them, and re-layouts  9.36 us (7%)
  other arithmetic  6.34 us (5%)
  between operations  1.55 us (1%)
    all_to_all x1, blocking collectives, body(): pieces = lax.all_to_all(coded, PLANE, 0, 0, tiled=True)  33 us
    ppermute x3, waiting for transfers between devices, gather_ring(): lax.ppermute(block, axis, [(i, (i + k) % n) for i in range(n)])  18.4 us
    all_to_all x2, starting transfers between devices, to_all(): lax.all_to_all(jnp.broadcast_to(block[None], (length, *block.shape)), axe...  15.1 us
    ppermute x4, waiting for transfers between devices, neighbour(): return lax.ppermute(block, axis, [(i, i ^ mask) for i in range(4)])  13.8 us
    ppermute x4, starting transfers between devices, neighbour(): return lax.ppermute(block, axis, [(i, i ^ mask) for i in range(4)])  9.42 us
    all_to_all x2, waiting for transfers between devices, to_all(): lax.all_to_all(jnp.broadcast_to(block[None], (length, *block.shape)), axe...  9.16 us
    ppermute x1, starting transfers between devices, body(): other = lax.ppermute(gathered, 'c', SWAP)  5.16 us
    ppermute x3, starting transfers between devices, gather_ring(): lax.ppermute(block, axis, [(i, (i + k) % n) for i in range(n)])  4.78 us
  transfers between devices with their start and end apart: 11, of which 10 were waited for; matrix products, arithmetic and copies ran while one was open for 1% of the time, Pallas kernels for 0%

profile of v2, /device:TPU:1, one launch (start us, length us, event | category | flops | bytes accessed | tf_op | source)
XLA Modules:
  0.0 135.5 jit_solution(3259621706903309984)
XLA Ops:
  0.6 3.2 %dynamic-slice_bitcast_fusion = bf16[4,2,4,4,16,512]{5,4,3,2,1,0:T(8,128)(2,1)} fusion(bf16[4,2,4,2,4,16,512]{6,5,4,3,2,1,0:T(8,128)(2,1)} %bitcast.34, s32[]{:T(128)S(6)} %select_n.67), kind=kLoop, calls=%fused_computation.16 | loop fusion | bytes 4194308 | tf_op jit(solution)/shard_map/jit(dynamic_index_in_dim)/squeeze | solution.py:86
  3.8 3.2 %collective-permute-start = (bf16[4,2,4,4,16,512]{5,4,3,2,1,0:T(8,128)(2,1)}, bf16[4,2,4,4,16,512]{5,4,3,2,1,0:T(8,128)(2,1)S(1)}, u32[]{:S(2)}, u32[]{:S(2)}) collective-permute-start(bf16[4,2,4,4,16,512]{5,4,3,2,1,0:T(8,128)(2,1)} %dynamic-slice_bitcast_fusion), channel_id=1, source_target_pairs={{0,4},{4,0},{1,5},{5,1},{2,6},{6,2},{3,7},{7,3},{8,12},{12,8},{9,1... | collective-permute-start | bytes 6291464 | tf_op jit(solution)/shard_map/ppermute | solution.py:88
  7.1 4.0 %collective-permute-done = bf16[4,2,4,4,16,512]{5,4,3,2,1,0:T(8,128)(2,1)S(1)} collective-permute-done((bf16[4,2,4,4,16,512]{5,4,3,2,1,0:T(8,128)(2,1)}, bf16[4,2,4,4,16,512]{5,4,3,2,1,0:T(8,128)(2,1)S(1)}, u32[]{:S(2)}, u32[]{:S(2)}) %collective-permute-start) | collective-permute-done | bytes 2097184 | tf_op jit(solution)/shard_map/ppermute | solution.py:88
  11.1 2.8 %fusion.8 = bf16[2,4,4,4,16,512]{5,4,2,1,0,3:T(8,128)(2,1)S(1)} fusion(bf16[4,2,4,4,16,512]{5,4,3,2,1,0:T(8,128)(2,1)S(1)} %collective-permute-done, bf16[4,2,4,2,4,16,512]{6,5,4,3,2,1,0:T(8,128)(2,1)} %bitcast.35, s32[]{:T(128)S(6)} %select_n.66), kind=kLoop, calls=%fused_computation.13 | loop fusion | flops 9437184 | bytes 6291460 | tf_op jit(solution)/shard_map/transpose | solution.py:89
  14.1 33.0 %all_to_all.16 = bf16[32,64,512]{2,1,0:T(8,128)(2,1)S(1)} all-to-all(bf16[32,64,512]{2,1,0:T(8,128)(2,1)S(1)} %bitcast.33), channel_id=1, replica_groups=mesh['zh'=4,'zl'=2,'y'=4,'c'=2,'x'=4] {'zl','y','x'}, dimensions={0} | all-to-all | bytes 4194304 | tf_op jit(solution)/shard_map/all_to_all | solution.py:90
  47.0 1.4 %fusion.4 = f32[64,512]{1,0:T(8,128)S(1)} fusion(bf16[32,64,512]{2,1,0:T(8,128)(2,1)S(1)} %all_to_all.16), kind=kLoop, calls=%fused_computation.8 | loop fusion | flops 8355840 | bytes 2228224 | tf_op jit(solution)/shard_map/reduce_sum | solution.py:91
  48.4 3.1 %collective-permute-start.1 = (f32[64,512]{1,0:T(8,128)S(1)}, f32[64,512]{1,0:T(8,128)S(1)}, u32[]{:S(2)}, u32[]{:S(2)}) collective-permute-start(f32[64,512]{1,0:T(8,128)S(1)} %fusion.4), channel_id=1, source_target_pairs={{0,64},{64,0},{128,192},{192,128},{1,65},{65,1},{129,193},{193,129... | collective-permute-start | bytes 393224 | tf_op jit(solution)/shard_map/ppermute | solution.py:25
  51.5 4.2 %collective-permute-done.1 = f32[64,512]{1,0:T(8,128)S(1)} collective-permute-done((f32[64,512]{1,0:T(8,128)S(1)}, f32[64,512]{1,0:T(8,128)S(1)}, u32[]{:S(2)}, u32[]{:S(2)}) %collective-permute-start.1) | collective-permute-done | bytes 131104 | tf_op jit(solution)/shard_map/ppermute | solution.py:25
  55.8 2.8 %collective-permute-start.2 = (f32[64,512]{1,0:T(8,128)S(1)}, f32[64,512]{1,0:T(8,128)S(1)}, u32[]{:S(2)}, u32[]{:S(2)}) collective-permute-start(f32[64,512]{1,0:T(8,128)S(1)} %add.104), channel_id=1, source_target_pairs={{0,192},{64,128},{128,64},{192,0},{1,193},{65,129},{129,65},{193,1... | collective-permute-start | bytes 393224 | tf_op jit(solution)/shard_map/ppermute | solution.py:25
  58.6 4.6 %collective-permute-done.2 = f32[64,512]{1,0:T(8,128)S(1)} collective-permute-done((f32[64,512]{1,0:T(8,128)S(1)}, f32[64,512]{1,0:T(8,128)S(1)}, u32[]{:S(2)}, u32[]{:S(2)}) %collective-permute-start.2) | collective-permute-done | bytes 131104 | tf_op jit(solution)/shard_map/ppermute | solution.py:25
  63.8 1.3 broadcast_in_dim.43
  65.1 11.1 %all-to-all-start.1 = ((f32[64,1,1]{2,1,0:T(1,128)}), f32[64,1,1]{2,1,0:T(1,128)S(1)}, u32[]{:S(2)}, u32[]{:S(2)}) async-start(f32[64,1,1]{2,1,0:T(1,128)} %broadcast_in_dim.43), calls=%async_computation.1 | async-start | bytes 65536 | tf_op jit(solution)/shard_map/all_to_all | solution.py:19
  76.2 7.9 %all-to-all-done.1 = f32[64,1,1]{2,1,0:T(1,128)S(1)} async-done(((f32[64,1,1]{2,1,0:T(1,128)}), f32[64,1,1]{2,1,0:T(1,128)S(1)}, u32[]{:S(2)}, u32[]{:S(2)}) %all-to-all-start.1) | async-done | bytes 288 | tf_op jit(solution)/shard_map/all_to_all | solution.py:19
  86.8 2.4 %collective-permute-done.3 = bf16[1,16,512]{2,1,0:T(8,128)(2,1)S(1)} collective-permute-done((bf16[1,16,512]{2,1,0:T(8,128)(2,1)S(1)}, bf16[1,16,512]{2,1,0:T(8,128)(2,1)S(1)}, u32[]{:S(2)}, u32[]{:S(2)}) %collective-permute-start.3) | collective-permute-done | bytes 16416 | tf_op jit(solution)/shard_map/ppermute | solution.py:25
  89.3 2.4 %collective-permute-start.4 = (bf16[2,16,512]{2,1,0:T(8,128)(2,1)S(1)}, bf16[2,16,512]{2,1,0:T(8,128)(2,1)S(1)}, u32[]{:S(2)}, u32[]{:S(2)}) collective-permute-start(bf16[2,16,512]{2,1,0:T(8,128)(2,1)S(1)} %pad_maximum_fusion.1), channel_id=1, source_target_pairs={{0,192},{64,128},{128,64},{192,0},{1,193},{65,129},{129,65},{193,1... | collective-permute-start | bytes 98312 | tf_op jit(solution)/shard_map/ppermute | solution.py:25
  91.6 2.6 %collective-permute-done.4 = bf16[2,16,512]{2,1,0:T(8,128)(2,1)S(1)} collective-permute-done((bf16[2,16,512]{2,1,0:T(8,128)(2,1)S(1)}, bf16[2,16,512]{2,1,0:T(8,128)(2,1)S(1)}, u32[]{:S(2)}, u32[]{:S(2)}) %collective-permute-start.4) | collective-permute-done | bytes 32800 | tf_op jit(solution)/shard_map/ppermute | solution.py:25
  94.3 1.6 %broadcast_in_dim.46 = bf16[32,64,512]{2,1,0:T(8,128)(2,1)} broadcast(bf16[64,512]{1,0:T(8,128)(2,1)S(1)} %bitcast.39), dimensions={1,2} | broadcast | bytes 2162688 | tf_op jit(solution)/shard_map/broadcast_in_dim | solution.py:20
  95.8 4.0 %all-to-all-start.2 = ((bf16[32,64,512]{2,1,0:T(8,128)(2,1)}), bf16[32,64,512]{2,1,0:T(8,128)(2,1)S(1)}, u32[]{:S(2)}, u32[]{:S(2)}) async-start(bf16[32,64,512]{2,1,0:T(8,128)(2,1)} %broadcast_in_dim.46), calls=%async_computation.2 | async-start | bytes 4194304 | tf_op jit(solution)/shard_map/all_to_all | solution.py:19
  101.0 2.4 %collective-permute-start.6 = (f32[16,512]{1,0:T(8,128)S(1)}, f32[16,512]{1,0:T(8,128)S(1)}, u32[]{:S(2)}, u32[]{:S(2)}) collective-permute-start(f32[16,512]{1,0:T(8,128)S(1)} %get-tuple-element.12), channel_id=1, source_target_pairs={{0,2},{1,3},{2,0},{3,1},{4,6},{5,7},{6,4},{7,5},{8,10},{9,11},{10,... | collective-permute-start | bytes 98312 | tf_op jit(solution)/shard_map/ppermute | solution.py:48
  104.6 12.9 %collective-permute-done.5 = f32[16,512]{1,0:T(8,128)S(1)} collective-permute-done((f32[16,512]{1,0:T(8,128)S(1)}, f32[16,512]{1,0:T(8,128)S(1)}, u32[]{:S(2)}, u32[]{:S(2)}) %collective-permute-start.5) | collective-permute-done | bytes 32800 | tf_op jit(solution)/shard_map/ppermute | solution.py:48
  117.5 5.6 %collective-permute-done.6 = f32[16,512]{1,0:T(8,128)S(1)} collective-permute-done((f32[16,512]{1,0:T(8,128)S(1)}, f32[16,512]{1,0:T(8,128)S(1)}, u32[]{:S(2)}, u32[]{:S(2)}) %collective-permute-start.6) | collective-permute-done | bytes 32800 | tf_op jit(solution)/shard_map/ppermute | solution.py:48
  124.3 5.2 %collective-permute-start.8 = (bf16[32,64,512]{2,1,0:T(8,128)(2,1)S(1)}, bf16[32,64,512]{2,1,0:T(8,128)(2,1)S(1)}, u32[]{:S(2)}, u32[]{:S(2)}) collective-permute-start(bf16[32,64,512]{2,1,0:T(8,128)(2,1)S(1)} %all-to-all-done.2), channel_id=1, source_target_pairs={{0,4},{4,0},{1,5},{5,1},{2,6},{6,2},{3,7},{7,3},{8,12},{12,8},{9,1... | collective-permute-start | bytes 6291464 | tf_op jit(solution)/shard_map/ppermute | solution.py:104
  131.1 2.2 %collective-permute-done.8 = bf16[32,64,512]{2,1,0:T(8,128)(2,1)S(1)} collective-permute-done((bf16[32,64,512]{2,1,0:T(8,128)(2,1)S(1)}, bf16[32,64,512]{2,1,0:T(8,128)(2,1)S(1)}, u32[]{:S(2)}, u32[]{:S(2)}) %collective-permute-start.8) | collective-permute-done | bytes 2097184 | tf_op jit(solution)/shard_map/ppermute | solution.py:104
  133.5 2.0 %copy-done = bf16[4,2,4,2,4,16,512]{6,5,4,3,2,1,0:T(8,128)(2,1)} copy-done((bf16[4,2,4,2,4,16,512]{6,5,4,3,2,1,0:T(8,128)(2,1)}, bf16[4,2,4,2,4,16,512]{6,5,4,3,2,1,0:T(8,128)(2,1)S(1)}, u32[]{:S(2)}) %copy-start) | copy-done | bytes 4194328
  (30 shorter events, 8.3 us)
Async XLA Ops:
  3.8 7.2 %collective-permute-start = (bf16[4,2,4,4,16,512]{5,4,3,2,1,0:T(8,128)(2,1)}, bf16[4,2,4,4,16,512]{5,4,3,2,1,0:T(8,128)(2,1)S(1)}, u32[]{:S(2)}, u32[]{:S(2)}) collective-permute-start(bf16[4,2,4,4,16,512]{5,4,3,2,1,0:T(8,128)(2,1)} %dynamic-slice_bitcast_fusion), channel_id=1, source_target_pairs={{0,4},{4,0},{1,5},{5,1},{2,6},{6,2},{3,7},{7,3},{8,12},{12,8},{9,1... | collective-permute-start | bytes 6291464 | tf_op jit(solution)/shard_map/ppermute | solution.py:88
  14.0 71.6 %copy-start.1 = (f32[64,512]{1,0:T(8,128)S(1)}, f32[64,512]{1,0:T(8,128)}, u32[]{:S(2)}) copy-start(f32[64,512]{1,0:T(8,128)} %param.7) | copy-start | bytes 393220
  14.0 71.6 %copy-start.2 = (f32[64,512]{1,0:T(8,128)S(1)}, f32[64,512]{1,0:T(8,128)}, u32[]{:S(2)}) copy-start(f32[64,512]{1,0:T(8,128)} %param.6) | copy-start | bytes 393220
  14.1 71.6 %copy-start.3 = (f32[64,512]{1,0:T(8,128)S(1)}, f32[64,512]{1,0:T(8,128)}, u32[]{:S(2)}) copy-start(f32[64,512]{1,0:T(8,128)} %param.5) | copy-start | bytes 393220
  48.4 7.3 %collective-permute-start.1 = (f32[64,512]{1,0:T(8,128)S(1)}, f32[64,512]{1,0:T(8,128)S(1)}, u32[]{:S(2)}, u32[]{:S(2)}) collective-permute-start(f32[64,512]{1,0:T(8,128)S(1)} %fusion.4), channel_id=1, source_target_pairs={{0,64},{64,0},{128,192},{192,128},{1,65},{65,1},{129,193},{193,129... | collective-permute-start | bytes 393224 | tf_op jit(solution)/shard_map/ppermute | solution.py:25
  55.8 7.4 %collective-permute-start.2 = (f32[64,512]{1,0:T(8,128)S(1)}, f32[64,512]{1,0:T(8,128)S(1)}, u32[]{:S(2)}, u32[]{:S(2)}) collective-permute-start(f32[64,512]{1,0:T(8,128)S(1)} %add.104), channel_id=1, source_target_pairs={{0,192},{64,128},{128,64},{192,0},{1,193},{65,129},{129,65},{193,1... | collective-permute-start | bytes 393224 | tf_op jit(solution)/shard_map/ppermute | solution.py:25
  65.1 19.1 %all-to-all-start.1 = ((f32[64,1,1]{2,1,0:T(1,128)}), f32[64,1,1]{2,1,0:T(1,128)S(1)}, u32[]{:S(2)}, u32[]{:S(2)}) async-start(f32[64,1,1]{2,1,0:T(1,128)} %broadcast_in_dim.43), calls=%async_computation.1 | async-start | bytes 65536 | tf_op jit(solution)/shard_map/all_to_all | solution.py:19
  85.7 3.6 %collective-permute-start.3 = (bf16[1,16,512]{2,1,0:T(8,128)(2,1)S(1)}, bf16[1,16,512]{2,1,0:T(8,128)(2,1)S(1)}, u32[]{:S(2)}, u32[]{:S(2)}) collective-permute-start(bf16[1,16,512]{2,1,0:T(8,128)(2,1)S(1)} %fusion.16), channel_id=1, source_target_pairs={{0,64},{64,0},{128,192},{192,128},{1,65},{65,1},{129,193},{193,129... | collective-permute-start | bytes 49160 | tf_op jit(solution)/shard_map/ppermute | solution.py:25
  89.3 5.0 %collective-permute-start.4 = (bf16[2,16,512]{2,1,0:T(8,128)(2,1)S(1)}, bf16[2,16,512]{2,1,0:T(8,128)(2,1)S(1)}, u32[]{:S(2)}, u32[]{:S(2)}) collective-permute-start(bf16[2,16,512]{2,1,0:T(8,128)(2,1)S(1)} %pad_maximum_fusion.1), channel_id=1, source_target_pairs={{0,192},{64,128},{128,64},{192,0},{1,193},{65,129},{129,65},{193,1... | collective-permute-start | bytes 98312 | tf_op jit(solution)/shard_map/ppermute | solution.py:25
  95.8 28.5 %all-to-all-start.2 = ((bf16[32,64,512]{2,1,0:T(8,128)(2,1)}), bf16[32,64,512]{2,1,0:T(8,128)(2,1)S(1)}, u32[]{:S(2)}, u32[]{:S(2)}) async-start(bf16[32,64,512]{2,1,0:T(8,128)(2,1)} %broadcast_in_dim.46), calls=%async_computation.2 | async-start | bytes 4194304 | tf_op jit(solution)/shard_map/all_to_all | solution.py:19
  99.8 17.6 %collective-permute-start.5 = (f32[16,512]{1,0:T(8,128)S(1)}, f32[16,512]{1,0:T(8,128)S(1)}, u32[]{:S(2)}, u32[]{:S(2)}) collective-permute-start(f32[16,512]{1,0:T(8,128)S(1)} %get-tuple-element.12), channel_id=1, source_target_pairs={{0,1},{1,2},{2,3},{3,0},{4,5},{5,6},{6,7},{7,4},{8,9},{9,10},{10,1... | collective-permute-start | bytes 98312 | tf_op jit(solution)/shard_map/ppermute | solution.py:48
  101.0 22.0 %collective-permute-start.6 = (f32[16,512]{1,0:T(8,128)S(1)}, f32[16,512]{1,0:T(8,128)S(1)}, u32[]{:S(2)}, u32[]{:S(2)}) collective-permute-start(f32[16,512]{1,0:T(8,128)S(1)} %get-tuple-element.12), channel_id=1, source_target_pairs={{0,2},{1,3},{2,0},{3,1},{4,6},{5,7},{6,4},{7,5},{8,10},{9,11},{10,... | collective-permute-start | bytes 98312 | tf_op jit(solution)/shard_map/ppermute | solution.py:48
  103.4 19.6 %collective-permute-start.7 = (f32[16,512]{1,0:T(8,128)S(1)}, f32[16,512]{1,0:T(8,128)S(1)}, u32[]{:S(2)}, u32[]{:S(2)}) collective-permute-start(f32[16,512]{1,0:T(8,128)S(1)} %get-tuple-element.12), channel_id=1, source_target_pairs={{0,3},{1,0},{2,1},{3,2},{4,7},{5,4},{6,5},{7,6},{8,11},{9,8},{10,9... | collective-permute-start | bytes 98312 | tf_op jit(solution)/shard_map/ppermute | solution.py:48
  124.3 9.0 %collective-permute-start.8 = (bf16[32,64,512]{2,1,0:T(8,128)(2,1)S(1)}, bf16[32,64,512]{2,1,0:T(8,128)(2,1)S(1)}, u32[]{:S(2)}, u32[]{:S(2)}) collective-permute-start(bf16[32,64,512]{2,1,0:T(8,128)(2,1)S(1)} %all-to-all-done.2), channel_id=1, source_target_pairs={{0,4},{4,0},{1,5},{5,1},{2,6},{6,2},{3,7},{7,3},{8,12},{12,8},{9,1... | collective-permute-start | bytes 6291464 | tf_op jit(solution)/shard_map/ppermute | solution.py:104
  133.5 2.0 %copy-start = (bf16[4,2,4,2,4,16,512]{6,5,4,3,2,1,0:T(8,128)(2,1)}, bf16[4,2,4,2,4,16,512]{6,5,4,3,2,1,0:T(8,128)(2,1)S(1)}, u32[]{:S(2)}) copy-start(bf16[4,2,4,2,4,16,512]{6,5,4,3,2,1,0:T(8,128)(2,1)S(1)} %copy_dynamic-update-slice_fusion) | copy-start | bytes 12582916

commit v3 on v2

--- a/solution.py
+++ b/solution.py
@@ -3,6 +3,8 @@
 import jax
 import jax.numpy as jnp
 from jax import lax
+from jax.experimental import pallas as pl
+from jax.experimental.pallas import tpu as pltpu
 from jax.sharding import Mesh
 from jax.sharding import PartitionSpec as P
 
@@ -31,23 +33,77 @@
     return block
 
 
-def gather_of_four(block, axis):
+def doubled(block, axis, mask):
     me = lax.axis_index(axis)
-    block = block[None]
-    for mask, low in ((1, me % 2 == 0), (3, me < 2)):
-        other = neighbour(block, axis, mask)
-        block = jnp.concatenate([jnp.where(low, block, other), jnp.where(low, other, block)])
-    return block
+    low = me % 2 == 0 if mask == 1 else me < 2
+    other = neighbour(block, axis, mask)
+    return jnp.concatenate([jnp.where(low, block, other), jnp.where(low, other, block)])
 
 
-def gather_ring(block, axis):
+def around(block, axis):
+    n = lax.axis_size(axis)
+    ring = {k: lax.ppermute(block, axis, [(i, (i + k) % n) for i in range(n)]) for k in (1, 3, 2)}
+    return [block, ring[1], ring[2], ring[3]]
+
+
+def by_place(parts, axis):
     n = lax.axis_size(axis)
     me = lax.axis_index(axis)
-    out = jnp.zeros((n, *block.shape), block.dtype)
-    for k in range(n):
-        part = lax.ppermute(block, axis, [(i, (i + k) % n) for i in range(n)]) if k else block
+    out = jnp.zeros((n, *parts[0].shape), parts[0].dtype)
+    for k, part in enumerate(parts):
         out = lax.dynamic_update_index_in_dim(out, part, lax.rem(me - k + n, n), 0)
     return out
+
+
+def place(own, xs_ref, ys_ref, own_there, xs_there, ys_there, out, whole, sems):
+    zl, y, c, x = (lax.axis_index(a) for a in ("zl", "y", "c", "x"))
+    ys = [lax.rem(y - k + 4, 4) for k in range(4)]
+    xs = [lax.rem(x - k + 4, 4) for k in range(4)]
+    zls = (zl, 1 - zl)
+    copies = []
+    for zh in range(4):
+        half, h = divmod(zh, 2)
+        for core, mine, rest in (
+            (c, own, (xs_ref, ys_ref)[half]), (1 - c, own_there, (xs_there, ys_there)[half])
+        ):
+            for j in range(4):
+                for k in range(4):
+                    at_y, at_x = (ys[k], xs[j]) if half == 0 else (ys[j], xs[k])
+                    for l in range(2):
+                        piece = rest[j - 1, k, l, h] if j else mine[half, k, l, h]
+                        whole[zh, zls[l], at_y, core, at_x] = piece
+        copy = pltpu.make_async_copy(whole.at[zh], out.at[zh], sems.at[zh])
+        copy.start()
+        copies.append(copy)
+    for copy in copies:
+        copy.wait()
+
+
+def gather_weights(ahead, mine):
+    zh, rows, width = ahead.shape
+    high = lax.reduce_precision(mine, 8, 7)
+    halves = jnp.stack([high, mine - high]).astype(jnp.bfloat16)
+    pair = jnp.stack([ahead, lax.ppermute(ahead, "zl", SWAP)])
+    second = pair[:, zh // 2 :].reshape(-1, rows, width)
+    second = around(jnp.concatenate([second, halves]), "x")
+    owned = by_place([part[4].astype(jnp.float32) + part[5].astype(jnp.float32) for part in second], "x")
+    second = jnp.stack([part[:4].reshape(2, 2, rows, width) for part in second])
+    first = jnp.stack(around(pair[:, : zh // 2], "y"))
+    own = lax.optimization_barrier(jnp.stack([first, second]))
+    along_x = jnp.stack(around(own[0], "x")[1:])
+    along_y = jnp.stack(around(own[1], "y")[1:])
+    here = (own, along_x, along_y)
+    there = [lax.ppermute(piece, "c", SWAP) for piece in here]
+    shape = (zh, 2, 4, 2, 4, rows, width)
+    out = pl.pallas_call(
+        place,
+        out_shape=jax.ShapeDtypeStruct(shape, ahead.dtype),
+        in_specs=[pl.BlockSpec(memory_space=pltpu.VMEM)] * 6,
+        out_specs=pl.BlockSpec(memory_space=pl.ANY),
+        scratch_shapes=[pltpu.VMEM(shape, ahead.dtype), pltpu.SemaphoreType.DMA((zh,))],
+        compiler_params=pltpu.CompilerParams(vmem_limit_bytes=24 * 2**20),
+    )(*here, *there)
+    return out.reshape(-1, width), owned.reshape(-1, width)
 
 
 def encode(value):
@@ -82,31 +138,34 @@
     rows = master.shape[0] // x
     me_c, me_x, me_zh = (lax.axis_index(a) for a in ("c", "x", "zh"))
 
+    states = jnp.stack([
+        lax.dynamic_slice_in_dim(a, me_x * rows, rows, 0)
+        for a in (master, first_moment, second_moment)
+    ])[None]
+    states = doubled(states, "zh", 1)
+
     local = grads[0].reshape(zh, zl, y, c, x, rows, width)
     sent = lax.dynamic_index_in_dim(local, 1 - me_c, 3, keepdims=False)
     kept = lax.dynamic_index_in_dim(local, me_c, 3, keepdims=False)
     pair = kept.astype(jnp.float32) + lax.ppermute(sent, "c", SWAP).astype(jnp.float32)
     coded = encode(pair).transpose(1, 2, 3, 0, 4, 5).reshape(-1, zh * rows, width)
+    coded, states = lax.optimization_barrier((coded, states))
     pieces = lax.all_to_all(coded, PLANE, 0, 0, tiled=True)
     total = sum_of_four(jnp.sum(decode(pieces), axis=0), "zh")
 
+    total, states = lax.optimization_barrier((total, states))
+    states = doubled(states, "zh", 3)
     squares = jnp.sum(to_all(jnp.sum(total * total), OWNERS))
     factor = clip_factor(squares, width)
 
-    mine = factor * lax.dynamic_slice_in_dim(total, me_zh * rows, rows, 0)
-    quarter = (lax.dynamic_slice_in_dim(a, me_x * rows, rows, 0) for a in (master, first_moment, second_moment))
-    ahead = adam_update(mine, *quarter)[0].astype(jnp.bfloat16)
-    gathered = to_all(gather_of_four(ahead, "zh").reshape(-1, width), PLANE)
-    owned = gather_ring(mine, "x").reshape(-1, width)
-    gathered, owned = lax.optimization_barrier((gathered, owned))
+    clipped = factor * total
+    states = states.transpose(1, 0, 2, 3).reshape(3, -1, width)
+    ahead = adam_update(clipped, states[0], states[1], states[2])[0]
+    mine = lax.dynamic_slice_in_dim(clipped, me_zh * rows, rows, 0)
+    weights, owned = gather_weights(ahead.astype(jnp.bfloat16).reshape(zh, rows, width), mine)
     new_master, new_first, new_second = adam_update(owned, master, first_moment, second_moment)
 
-    other = lax.ppermute(gathered, "c", SWAP)
-    weights = jnp.zeros((zh, zl, y, c, x, rows, width), jnp.bfloat16)
-    for half, place in ((gathered, me_c), (other, 1 - me_c)):
-        half = half.reshape(zl, y, x, zh, rows, width).transpose(3, 0, 1, 2, 4, 5)
-        weights = lax.dynamic_update_index_in_dim(weights, half, place, 3)
-    return (weights.reshape(-1, width), new_master, new_first, new_second)
+    return (weights, new_master, new_first, new_second)
 
 
 def solution(mesh):

time: 136 us -> 131 us (0.963)
  waiting for transfers between devices: 47.6 us -> 33.7 us
  starting transfers between devices: 37.7 us -> 48.6 us
  local copies, waits for them, and re-layouts: 9.36 us -> 4.84 us
  Pallas kernels: 0 us -> 2.11 us
    ppermute x4 -> x16, starting transfers between devices: 9.94 us -> 23.9 us  [the longest x3 13.1 us: gather_weights(): there = [lax.ppermute(piece, 'c', SWAP) for piece in here]]
    ppermute x4 -> x16, waiting for transfers between devices: 20.6 us -> 10.4 us  [the longest x12 6.31 us: around(): lax.ppermute(block, axis, [(i, (i + k) % n) for i in range(n)])]
    ppermute x1, waiting for transfers between devices: 4 us -> 0.01 us  [body(): lax.ppermute(sent, 'c', SWAP).astype(jnp.float32)]
    pallas_call x0 -> x1, Pallas kernels: none -> 2.11 us  [gather_weights(): pl.pallas_call(place, out_shape=jax.ShapeDtypeStruct(shape, ahead.dtype),...]
    unnamed x8 -> x6, local copies, waits for them, and re-layouts: 2.03 us -> 0.01 us
    all_to_all x2 -> x1, starting transfers between devices: 15.1 us -> 13.1 us  [to_all(): lax.all_to_all(jnp.broadcast_to(block[None], (length, *block.shape)), axe...]
    broadcast_in_dim x2 -> x1, local copies, waits for them, and re-layouts: 2.83 us -> 1.28 us  [to_all(): jnp.broadcast_to(block[None], (length, *block.shape))]
    ppermute x4, waiting for transfers between devices: 13.8 us -> 15.3 us  [neighbour(): return lax.ppermute(block, axis, [(i, i ^ mask) for i in range(4)])]
  transfers between devices with their start and end apart: 11 -> 22, of which waited for: 10 -> 13; matrix products, arithmetic and copies ran while one was open for 1% -> 3% of each run, Pallas kernels for 0% -> 0%
where the time goes in v3:
time: 131 us; the launch traced here: 130 us
  starting transfers between devices  48.6 us (37%)
  waiting for transfers between devices  33.7 us (26%)
  blocking collectives  32.4 us (25%)
  other arithmetic  6.89 us (5%)
  local copies, waits for them, and re-layouts  4.84 us (4%)
  Pallas kernels  2.11 us (2%)
  between operations  1.79 us (1%)
    all_to_all x1, blocking collectives, body(): pieces = lax.all_to_all(coded, PLANE, 0, 0, tiled=True)  32.4 us
    ppermute x4, waiting for transfers between devices, neighbour(): return lax.ppermute(block, axis, [(i, i ^ mask) for i in range(4)])  15.3 us
    all_to_all x1, starting transfers between devices, to_all(): lax.all_to_all(jnp.broadcast_to(block[None], (length, *block.shape)), axe...  13.1 us
    ppermute x3, starting transfers between devices, gather_weights(): there = [lax.ppermute(piece, 'c', SWAP) for piece in here]  13.1 us
    ppermute x12, starting transfers between devices, around(): lax.ppermute(block, axis, [(i, (i + k) % n) for i in range(n)])  10.7 us
    ppermute x4, starting transfers between devices, neighbour(): return lax.ppermute(block, axis, [(i, i ^ mask) for i in range(4)])  8.31 us
    all_to_all x1, waiting for transfers between devices, to_all(): lax.all_to_all(jnp.broadcast_to(block[None], (length, *block.shape)), axe...  7.94 us
    ppermute x12, waiting for transfers between devices, around(): lax.ppermute(block, axis, [(i, (i + k) % n) for i in range(n)])  6.31 us
  transfers between devices with their start and end apart: 22, of which 13 were waited for; matrix products, arithmetic and copies ran while one was open for 3% of the time, Pallas kernels for 0%

profile of v3, /device:TPU:1, one launch (start us, length us, event | category | flops | bytes accessed | tf_op | source)
XLA Modules:
  0.0 130.3 jit_solution(17887560533335654916)
XLA Ops:
  0.7 3.3 %dynamic-slice_bitcast_fusion = bf16[4,2,4,4,16,512]{5,4,3,2,1,0:T(8,128)(2,1)} fusion(bf16[4,2,4,2,4,16,512]{6,5,4,3,2,1,0:T(8,128)(2,1)} %bitcast.85, s32[]{:T(128)S(6)} %select_n.61), kind=kLoop, calls=%fused_computation.14 | loop fusion | bytes 4194308 | tf_op jit(solution)/shard_map/jit(dynamic_index_in_dim)/squeeze | solution.py:148
  3.9 3.2 %collective-permute-start = (bf16[4,2,4,4,16,512]{5,4,3,2,1,0:T(8,128)(2,1)}, bf16[4,2,4,4,16,512]{5,4,3,2,1,0:T(8,128)(2,1)S(1)}, u32[]{:S(2)}, u32[]{:S(2)}) collective-permute-start(bf16[4,2,4,4,16,512]{5,4,3,2,1,0:T(8,128)(2,1)} %dynamic-slice_bitcast_fusion), channel_id=1, source_target_pairs={{0,4},{4,0},{1,5},{5,1},{2,6},{6,2},{3,7},{7,3},{8,12},{12,8},{9,1... | collective-permute-start | bytes 6291464 | tf_op jit(solution)/shard_map/ppermute | solution.py:150
  7.2 1.3 %collective-permute-start.1 = (f32[1,3,16,512]{3,2,0,1:T(8,128)S(1)}, f32[1,3,16,512]{3,2,0,1:T(8,128)S(1)}, u32[]{:S(2)}, u32[]{:S(2)}) collective-permute-start(f32[1,3,16,512]{3,2,0,1:T(8,128)S(1)} %maximum_bitcast_fusion.3), channel_id=1, source_target_pairs={{0,64},{64,0},{128,192},{192,128},{1,65},{65,1},{129,193},{193,129... | collective-permute-start | bytes 294920 | tf_op jit(solution)/shard_map/ppermute | solution.py:27
  8.6 6.3 %collective-permute-done.1 = f32[1,3,16,512]{3,2,0,1:T(8,128)S(1)} collective-permute-done((f32[1,3,16,512]{3,2,0,1:T(8,128)S(1)}, f32[1,3,16,512]{3,2,0,1:T(8,128)S(1)}, u32[]{:S(2)}, u32[]{:S(2)}) %collective-permute-start.1) | collective-permute-done | bytes 98336 | tf_op jit(solution)/shard_map/ppermute | solution.py:27
  14.9 2.8 %fusion.8 = bf16[2,4,4,4,16,512]{5,4,2,1,0,3:T(8,128)(2,1)S(1)} fusion(bf16[4,2,4,4,16,512]{5,4,3,2,1,0:T(8,128)(2,1)S(1)} %collective-permute-done, bf16[4,2,4,2,4,16,512]{6,5,4,3,2,1,0:T(8,128)(2,1)} %bitcast.86, s32[]{:T(128)S(6)} %select_n.60), kind=kLoop, calls=%fused_computation.13 | loop fusion | flops 9437184 | bytes 6291460 | tf_op jit(solution)/shard_map/transpose | solution.py:151
  17.9 32.4 %all_to_all.11 = bf16[32,64,512]{2,1,0:T(8,128)(2,1)S(1)} all-to-all(bf16[32,64,512]{2,1,0:T(8,128)(2,1)S(1)} %bitcast.84), channel_id=1, replica_groups=mesh['zh'=4,'zl'=2,'y'=4,'c'=2,'x'=4] {'zl','y','x'}, dimensions={0} | all-to-all | bytes 4194304 | tf_op jit(solution)/shard_map/all_to_all | solution.py:153
  50.3 1.4 %fusion.4 = f32[64,512]{1,0:T(8,128)S(1)} fusion(bf16[32,64,512]{2,1,0:T(8,128)(2,1)S(1)} %all_to_all.11), kind=kLoop, calls=%fused_computation.8 | loop fusion | flops 8355840 | bytes 2228224 | tf_op jit(solution)/shard_map/reduce_sum | solution.py:154
  51.7 3.2 %collective-permute-start.2 = (f32[64,512]{1,0:T(8,128)S(1)}, f32[64,512]{1,0:T(8,128)S(1)}, u32[]{:S(2)}, u32[]{:S(2)}) collective-permute-start(f32[64,512]{1,0:T(8,128)S(1)} %fusion.4), channel_id=1, source_target_pairs={{0,64},{64,0},{128,192},{192,128},{1,65},{65,1},{129,193},{193,129... | collective-permute-start | bytes 393224 | tf_op jit(solution)/shard_map/ppermute | solution.py:27
  54.9 4.2 %collective-permute-done.2 = f32[64,512]{1,0:T(8,128)S(1)} collective-permute-done((f32[64,512]{1,0:T(8,128)S(1)}, f32[64,512]{1,0:T(8,128)S(1)}, u32[]{:S(2)}, u32[]{:S(2)}) %collective-permute-start.2) | collective-permute-done | bytes 131104 | tf_op jit(solution)/shard_map/ppermute | solution.py:27
  59.1 2.6 %collective-permute-start.3 = (f32[64,512]{1,0:T(8,128)S(1)}, f32[64,512]{1,0:T(8,128)S(1)}, u32[]{:S(2)}, u32[]{:S(2)}) collective-permute-start(f32[64,512]{1,0:T(8,128)S(1)} %add.111), channel_id=1, source_target_pairs={{0,192},{64,128},{128,64},{192,0},{1,193},{65,129},{129,65},{193,1... | collective-permute-start | bytes 393224 | tf_op jit(solution)/shard_map/ppermute | solution.py:27
  61.7 4.8 %collective-permute-done.3 = f32[64,512]{1,0:T(8,128)S(1)} collective-permute-done((f32[64,512]{1,0:T(8,128)S(1)}, f32[64,512]{1,0:T(8,128)S(1)}, u32[]{:S(2)}, u32[]{:S(2)}) %collective-permute-start.3) | collective-permute-done | bytes 131104 | tf_op jit(solution)/shard_map/ppermute | solution.py:27
  68.4 1.3 broadcast_in_dim.18
  69.6 13.1 %all-to-all-start.1 = ((f32[64,1,1]{2,1,0:T(1,128)}), f32[64,1,1]{2,1,0:T(1,128)S(1)}, u32[]{:S(2)}, u32[]{:S(2)}) async-start(f32[64,1,1]{2,1,0:T(1,128)} %broadcast_in_dim.18), calls=%async_computation.1 | async-start | bytes 65536 | tf_op jit(solution)/shard_map/all_to_all | solution.py:21
  82.8 7.9 %all-to-all-done.1 = f32[64,1,1]{2,1,0:T(1,128)S(1)} async-done(((f32[64,1,1]{2,1,0:T(1,128)}), f32[64,1,1]{2,1,0:T(1,128)S(1)}, u32[]{:S(2)}, u32[]{:S(2)}) %all-to-all-start.1) | async-done | bytes 288 | tf_op jit(solution)/shard_map/all_to_all | solution.py:21
  92.6 3.0 %collective-permute-done.5 = bf16[4,16,512]{2,1,0:T(8,128)(2,1)S(1)} collective-permute-done((bf16[4,16,512]{2,1,0:T(8,128)(2,1)S(1)}, bf16[4,16,512]{2,1,0:T(8,128)(2,1)S(1)}, u32[]{:S(2)}, u32[]{:S(2)}) %collective-permute-start.5) | collective-permute-done | bytes 65568 | tf_op jit(solution)/shard_map/ppermute | solution.py:86
  96.3 1.5 %collective-permute-start.7 = (bf16[2,2,16,512]{3,2,1,0:T(8,128)(2,1)S(1)}, bf16[2,2,16,512]{3,2,1,0:T(8,128)(2,1)S(1)}, u32[]{:S(2)}, u32[]{:S(2)}) collective-permute-start(bf16[2,2,16,512]{3,2,1,0:T(8,128)(2,1)S(1)} %get-tuple-element.29), channel_id=1, source_target_pairs={{0,16},{8,24},{16,0},{24,8},{1,17},{9,25},{17,1},{25,9},{2,18},{10... | collective-permute-start | bytes 196616 | tf_op jit(solution)/shard_map/ppermute | solution.py:45
  98.5 1.5 %collective-permute-start.10 = (bf16[6,16,512]{2,1,0:T(8,128)(2,1)S(1)}, bf16[6,16,512]{2,1,0:T(8,128)(2,1)S(1)}, u32[]{:S(2)}, u32[]{:S(2)}) collective-permute-start(bf16[6,16,512]{2,1,0:T(8,128)(2,1)S(1)} %pad_maximum_fusion.4), channel_id=1, source_target_pairs={{0,2},{1,3},{2,0},{3,1},{4,6},{5,7},{6,4},{7,5},{8,10},{9,11},{10,... | collective-permute-start | bytes 294920 | tf_op jit(solution)/shard_map/ppermute | solution.py:45
  102.2 1.5 %collective-permute-done.10 = bf16[6,16,512]{2,1,0:T(8,128)(2,1)S(1)} collective-permute-done((bf16[6,16,512]{2,1,0:T(8,128)(2,1)S(1)}, bf16[6,16,512]{2,1,0:T(8,128)(2,1)S(1)}, u32[]{:S(2)}, u32[]{:S(2)}) %collective-permute-start.10) | collective-permute-done | bytes 98336 | tf_op jit(solution)/shard_map/ppermute | solution.py:45
  105.7 1.7 %collective-permute-start.13 = (bf16[4,2,2,16,512]{4,3,2,1,0:T(8,128)(2,1)S(1)}, bf16[4,2,2,16,512]{4,3,2,1,0:T(8,128)(2,1)S(1)}, u32[]{:S(2)}, u32[]{:S(2)}) collective-permute-start(bf16[4,2,2,16,512]{4,3,2,1,0:T(8,128)(2,1)S(1)} %get-tuple-element.21), channel_id=1, source_target_pairs={{0,2},{1,3},{2,0},{3,1},{4,6},{5,7},{6,4},{7,5},{8,10},{9,11},{10,... | collective-permute-start | bytes 786440 | tf_op jit(solution)/shard_map/ppermute | solution.py:45
  107.5 2.6 %collective-permute-start.17 = (bf16[4,2,2,16,512]{4,3,2,1,0:T(8,128)(2,1)S(1)}, bf16[4,2,2,16,512]{4,3,2,1,0:T(8,128)(2,1)S(1)}, u32[]{:S(2)}, u32[]{:S(2)}) collective-permute-start(bf16[4,2,2,16,512]{4,3,2,1,0:T(8,128)(2,1)S(1)} %get-tuple-element.20), channel_id=1, source_target_pairs={{0,24},{8,0},{16,8},{24,16},{1,25},{9,1},{17,9},{25,17},{2,26},{10... | collective-permute-start | bytes 786440 | tf_op jit(solution)/shard_map/ppermute | solution.py:45
  112.6 6.3 %collective-permute-start.18 = (bf16[2,4,2,2,16,512]{5,4,3,2,1,0:T(8,128)(2,1)S(1)}, bf16[2,4,2,2,16,512]{5,4,3,2,1,0:T(8,128)(2,1)S(1)}, u32[]{:S(2)}, u32[]{:S(2)}) collective-permute-start(bf16[2,4,2,2,16,512]{5,4,3,2,1,0:T(8,128)(2,1)S(1)} %pad_maximum_fusion.2.own), channel_id=1, source_target_pairs={{0,4},{4,0},{1,5},{5,1},{2,6},{6,2},{3,7},{7,3},{8,12},{12,8},{9,1... | collective-permute-start | bytes 1572872 | tf_op jit(solution)/shard_map/ppermute | solution.py:96
  119.2 2.5 %collective-permute-start.19 = (bf16[3,4,2,2,16,512]{5,4,3,2,1,0:T(8,128)(2,1)S(1)}, bf16[3,4,2,2,16,512]{5,4,3,2,1,0:T(8,128)(2,1)S(1)}, u32[]{:S(2)}, u32[]{:S(2)}) collective-permute-start(bf16[3,4,2,2,16,512]{5,4,3,2,1,0:T(8,128)(2,1)S(1)} %pad_maximum_fusion.xs_ref), channel_id=1, source_target_pairs={{0,4},{4,0},{1,5},{5,1},{2,6},{6,2},{3,7},{7,3},{8,12},{12,8},{9,1... | collective-permute-start | bytes 2359304 | tf_op jit(solution)/shard_map/ppermute | solution.py:96
  121.9 4.2 %collective-permute-start.20 = (bf16[3,4,2,2,16,512]{5,4,3,2,1,0:T(8,128)(2,1)S(1)}, bf16[3,4,2,2,16,512]{5,4,3,2,1,0:T(8,128)(2,1)S(1)}, u32[]{:S(2)}, u32[]{:S(2)}) collective-permute-start(bf16[3,4,2,2,16,512]{5,4,3,2,1,0:T(8,128)(2,1)S(1)} %pad_maximum_fusion.1.ys_ref), channel_id=1, source_target_pairs={{0,4},{4,0},{1,5},{5,1},{2,6},{6,2},{3,7},{7,3},{8,12},{12,8},{9,1... | collective-permute-start | bytes 2359304 | tf_op jit(solution)/shard_map/ppermute | solution.py:96
  128.0 2.1 %shard_map.75 = bf16[4,2,4,2,4,16,512]{6,5,4,3,2,1,0:T(8,128)(2,1)} custom-call(bf16[2,4,2,2,16,512]{5,4,3,2,1,0:T(8,128)(2,1)S(1)} %pad_maximum_fusion.2.own, bf16[3,4,2,2,16,512]{5,4,3,2,1,0:T(8,128)(2,1)S(1)} %pad_maximum_fusion.xs_ref, bf16[3,4,2,2,16,512]{5,4,3,2,1,0:T(8,128)(2,1)S(1)} %pad_maximum_fusion.1.ys_ref, ...), custom_call_target="tpu_custom_call" | custom-call | tf_op jit(solution)/shard_map/pallas_call | solution.py:98
  (63 shorter events, 13.7 us)
Async XLA Ops:
  0.6 6.5 %copy-start = (f32[64,512]{1,0:T(8,128)S(1)}, f32[64,512]{1,0:T(8,128)}, u32[]{:S(2)}) copy-start(f32[64,512]{1,0:T(8,128)} %param.5) | copy-start | bytes 393220
  0.6 6.5 %copy-start.1 = (f32[64,512]{1,0:T(8,128)S(1)}, f32[64,512]{1,0:T(8,128)}, u32[]{:S(2)}) copy-start(f32[64,512]{1,0:T(8,128)} %param.7) | copy-start | bytes 393220
  3.9 11.0 %collective-permute-start = (bf16[4,2,4,4,16,512]{5,4,3,2,1,0:T(8,128)(2,1)}, bf16[4,2,4,4,16,512]{5,4,3,2,1,0:T(8,128)(2,1)S(1)}, u32[]{:S(2)}, u32[]{:S(2)}) collective-permute-start(bf16[4,2,4,4,16,512]{5,4,3,2,1,0:T(8,128)(2,1)} %dynamic-slice_bitcast_fusion), channel_id=1, source_target_pairs={{0,4},{4,0},{1,5},{5,1},{2,6},{6,2},{3,7},{7,3},{8,12},{12,8},{9,1... | collective-permute-start | bytes 6291464 | tf_op jit(solution)/shard_map/ppermute | solution.py:150
  7.2 7.6 %collective-permute-start.1 = (f32[1,3,16,512]{3,2,0,1:T(8,128)S(1)}, f32[1,3,16,512]{3,2,0,1:T(8,128)S(1)}, u32[]{:S(2)}, u32[]{:S(2)}) collective-permute-start(f32[1,3,16,512]{3,2,0,1:T(8,128)S(1)} %maximum_bitcast_fusion.3), channel_id=1, source_target_pairs={{0,64},{64,0},{128,192},{192,128},{1,65},{65,1},{129,193},{193,129... | collective-permute-start | bytes 294920 | tf_op jit(solution)/shard_map/ppermute | solution.py:27
  51.7 7.4 %collective-permute-start.2 = (f32[64,512]{1,0:T(8,128)S(1)}, f32[64,512]{1,0:T(8,128)S(1)}, u32[]{:S(2)}, u32[]{:S(2)}) collective-permute-start(f32[64,512]{1,0:T(8,128)S(1)} %fusion.4), channel_id=1, source_target_pairs={{0,64},{64,0},{128,192},{192,128},{1,65},{65,1},{129,193},{193,129... | collective-permute-start | bytes 393224 | tf_op jit(solution)/shard_map/ppermute | solution.py:27
  59.1 7.4 %collective-permute-start.3 = (f32[64,512]{1,0:T(8,128)S(1)}, f32[64,512]{1,0:T(8,128)S(1)}, u32[]{:S(2)}, u32[]{:S(2)}) collective-permute-start(f32[64,512]{1,0:T(8,128)S(1)} %add.111), channel_id=1, source_target_pairs={{0,192},{64,128},{128,64},{192,0},{1,193},{65,129},{129,65},{193,1... | collective-permute-start | bytes 393224 | tf_op jit(solution)/shard_map/ppermute | solution.py:27
  66.5 25.6 %collective-permute-start.4 = (f32[2,3,16,512]{3,2,0,1:T(8,128)S(1)}, f32[2,3,16,512]{3,2,0,1:T(8,128)S(1)}, u32[]{:S(2)}, u32[]{:S(2)}) collective-permute-start(f32[2,3,16,512]{3,2,0,1:T(8,128)S(1)} %pad_maximum_fusion.3), channel_id=1, source_target_pairs={{0,192},{64,128},{128,64},{192,0},{1,193},{65,129},{129,65},{193,1... | collective-permute-start | bytes 589832 | tf_op jit(solution)/shard_map/ppermute | solution.py:27
  69.6 21.1 %all-to-all-start.1 = ((f32[64,1,1]{2,1,0:T(1,128)}), f32[64,1,1]{2,1,0:T(1,128)S(1)}, u32[]{:S(2)}, u32[]{:S(2)}) async-start(f32[64,1,1]{2,1,0:T(1,128)} %broadcast_in_dim.18), calls=%async_computation.1 | async-start | bytes 65536 | tf_op jit(solution)/shard_map/all_to_all | solution.py:21
  92.4 3.2 %collective-permute-start.5 = (bf16[4,16,512]{2,1,0:T(8,128)(2,1)S(1)}, bf16[4,16,512]{2,1,0:T(8,128)(2,1)S(1)}, u32[]{:S(2)}, u32[]{:S(2)}) collective-permute-start(bf16[4,16,512]{2,1,0:T(8,128)(2,1)S(1)} %bitcast.90), channel_id=1, source_target_pairs={{0,32},{32,0},{1,33},{33,1},{2,34},{34,2},{3,35},{35,3},{4,36},{36... | collective-permute-start | bytes 196616 | tf_op jit(solution)/shard_map/ppermute | solution.py:86
  95.6 4.4 %collective-permute-start.8 = (bf16[2,2,16,512]{3,2,1,0:T(8,128)(2,1)S(1)}, bf16[2,2,16,512]{3,2,1,0:T(8,128)(2,1)S(1)}, u32[]{:S(2)}, u32[]{:S(2)}) collective-permute-start(bf16[2,2,16,512]{3,2,1,0:T(8,128)(2,1)S(1)} %get-tuple-element.29), channel_id=1, source_target_pairs={{0,24},{8,0},{16,8},{24,16},{1,25},{9,1},{17,9},{25,17},{2,26},{10... | collective-permute-start | bytes 196616 | tf_op jit(solution)/shard_map/ppermute | solution.py:45
  96.3 4.6 %collective-permute-start.7 = (bf16[2,2,16,512]{3,2,1,0:T(8,128)(2,1)S(1)}, bf16[2,2,16,512]{3,2,1,0:T(8,128)(2,1)S(1)}, u32[]{:S(2)}, u32[]{:S(2)}) collective-permute-start(bf16[2,2,16,512]{3,2,1,0:T(8,128)(2,1)S(1)} %get-tuple-element.29), channel_id=1, source_target_pairs={{0,16},{8,24},{16,0},{24,8},{1,17},{9,25},{17,1},{25,9},{2,18},{10... | collective-permute-start | bytes 196616 | tf_op jit(solution)/shard_map/ppermute | solution.py:45
  97.8 4.3 %collective-permute-start.6 = (bf16[2,2,16,512]{3,2,1,0:T(8,128)(2,1)S(1)}, bf16[2,2,16,512]{3,2,1,0:T(8,128)(2,1)S(1)}, u32[]{:S(2)}, u32[]{:S(2)}) collective-permute-start(bf16[2,2,16,512]{3,2,1,0:T(8,128)(2,1)S(1)} %get-tuple-element.29), channel_id=1, source_target_pairs={{0,8},{8,16},{16,24},{24,0},{1,9},{9,17},{17,25},{25,1},{2,10},{10... | collective-permute-start | bytes 196616 | tf_op jit(solution)/shard_map/ppermute | solution.py:45
  97.8 4.3 %collective-permute-start.11 = (bf16[6,16,512]{2,1,0:T(8,128)(2,1)S(1)}, bf16[6,16,512]{2,1,0:T(8,128)(2,1)S(1)}, u32[]{:S(2)}, u32[]{:S(2)}) collective-permute-start(bf16[6,16,512]{2,1,0:T(8,128)(2,1)S(1)} %pad_maximum_fusion.4), channel_id=1, source_target_pairs={{0,3},{1,0},{2,1},{3,2},{4,7},{5,4},{6,5},{7,6},{8,11},{9,8},{10,9... | collective-permute-start | bytes 294920 | tf_op jit(solution)/shard_map/ppermute | solution.py:45
  98.5 5.2 %collective-permute-start.10 = (bf16[6,16,512]{2,1,0:T(8,128)(2,1)S(1)}, bf16[6,16,512]{2,1,0:T(8,128)(2,1)S(1)}, u32[]{:S(2)}, u32[]{:S(2)}) collective-permute-start(bf16[6,16,512]{2,1,0:T(8,128)(2,1)S(1)} %pad_maximum_fusion.4), channel_id=1, source_target_pairs={{0,2},{1,3},{2,0},{3,1},{4,6},{5,7},{6,4},{7,5},{8,10},{9,11},{10,... | collective-permute-start | bytes 294920 | tf_op jit(solution)/shard_map/ppermute | solution.py:45
  100.0 5.0 %collective-permute-start.9 = (bf16[6,16,512]{2,1,0:T(8,128)(2,1)S(1)}, bf16[6,16,512]{2,1,0:T(8,128)(2,1)S(1)}, u32[]{:S(2)}, u32[]{:S(2)}) collective-permute-start(bf16[6,16,512]{2,1,0:T(8,128)(2,1)S(1)} %pad_maximum_fusion.4), channel_id=1, source_target_pairs={{0,1},{1,2},{2,3},{3,0},{4,5},{5,6},{6,7},{7,4},{8,9},{9,10},{10,1... | collective-permute-start | bytes 294920 | tf_op jit(solution)/shard_map/ppermute | solution.py:45
  105.1 5.3 %collective-permute-start.14 = (bf16[4,2,2,16,512]{4,3,2,1,0:T(8,128)(2,1)S(1)}, bf16[4,2,2,16,512]{4,3,2,1,0:T(8,128)(2,1)S(1)}, u32[]{:S(2)}, u32[]{:S(2)}) collective-permute-start(bf16[4,2,2,16,512]{4,3,2,1,0:T(8,128)(2,1)S(1)} %get-tuple-element.21), channel_id=1, source_target_pairs={{0,3},{1,0},{2,1},{3,2},{4,7},{5,4},{6,5},{7,6},{8,11},{9,8},{10,9... | collective-permute-start | bytes 786440 | tf_op jit(solution)/shard_map/ppermute | solution.py:45
  105.7 6.8 %collective-permute-start.13 = (bf16[4,2,2,16,512]{4,3,2,1,0:T(8,128)(2,1)S(1)}, bf16[4,2,2,16,512]{4,3,2,1,0:T(8,128)(2,1)S(1)}, u32[]{:S(2)}, u32[]{:S(2)}) collective-permute-start(bf16[4,2,2,16,512]{4,3,2,1,0:T(8,128)(2,1)S(1)} %get-tuple-element.21), channel_id=1, source_target_pairs={{0,2},{1,3},{2,0},{3,1},{4,6},{5,7},{6,4},{7,5},{8,10},{9,11},{10,... | collective-permute-start | bytes 786440 | tf_op jit(solution)/shard_map/ppermute | solution.py:45
  107.4 11.7 %collective-permute-start.12 = (bf16[4,2,2,16,512]{4,3,2,1,0:T(8,128)(2,1)S(1)}, bf16[4,2,2,16,512]{4,3,2,1,0:T(8,128)(2,1)S(1)}, u32[]{:S(2)}, u32[]{:S(2)}) collective-permute-start(bf16[4,2,2,16,512]{4,3,2,1,0:T(8,128)(2,1)S(1)} %get-tuple-element.21), channel_id=1, source_target_pairs={{0,1},{1,2},{2,3},{3,0},{4,5},{5,6},{6,7},{7,4},{8,9},{9,10},{10,1... | collective-permute-start | bytes 786440 | tf_op jit(solution)/shard_map/ppermute | solution.py:45
  107.5 14.3 %collective-permute-start.17 = (bf16[4,2,2,16,512]{4,3,2,1,0:T(8,128)(2,1)S(1)}, bf16[4,2,2,16,512]{4,3,2,1,0:T(8,128)(2,1)S(1)}, u32[]{:S(2)}, u32[]{:S(2)}) collective-permute-start(bf16[4,2,2,16,512]{4,3,2,1,0:T(8,128)(2,1)S(1)} %get-tuple-element.20), channel_id=1, source_target_pairs={{0,24},{8,0},{16,8},{24,16},{1,25},{9,1},{17,9},{25,17},{2,26},{10... | collective-permute-start | bytes 786440 | tf_op jit(solution)/shard_map/ppermute | solution.py:45
  110.0 11.7 %collective-permute-start.16 = (bf16[4,2,2,16,512]{4,3,2,1,0:T(8,128)(2,1)S(1)}, bf16[4,2,2,16,512]{4,3,2,1,0:T(8,128)(2,1)S(1)}, u32[]{:S(2)}, u32[]{:S(2)}) collective-permute-start(bf16[4,2,2,16,512]{4,3,2,1,0:T(8,128)(2,1)S(1)} %get-tuple-element.20), channel_id=1, source_target_pairs={{0,16},{8,24},{16,0},{24,8},{1,17},{9,25},{17,1},{25,9},{2,18},{10... | collective-permute-start | bytes 786440 | tf_op jit(solution)/shard_map/ppermute | solution.py:45
  110.4 11.4 %collective-permute-start.15 = (bf16[4,2,2,16,512]{4,3,2,1,0:T(8,128)(2,1)S(1)}, bf16[4,2,2,16,512]{4,3,2,1,0:T(8,128)(2,1)S(1)}, u32[]{:S(2)}, u32[]{:S(2)}) collective-permute-start(bf16[4,2,2,16,512]{4,3,2,1,0:T(8,128)(2,1)S(1)} %get-tuple-element.20), channel_id=1, source_target_pairs={{0,8},{8,16},{16,24},{24,0},{1,9},{9,17},{17,25},{25,1},{2,10},{10... | collective-permute-start | bytes 786440 | tf_op jit(solution)/shard_map/ppermute | solution.py:45
  112.6 14.4 %collective-permute-start.18 = (bf16[2,4,2,2,16,512]{5,4,3,2,1,0:T(8,128)(2,1)S(1)}, bf16[2,4,2,2,16,512]{5,4,3,2,1,0:T(8,128)(2,1)S(1)}, u32[]{:S(2)}, u32[]{:S(2)}) collective-permute-start(bf16[2,4,2,2,16,512]{5,4,3,2,1,0:T(8,128)(2,1)S(1)} %pad_maximum_fusion.2.own), channel_id=1, source_target_pairs={{0,4},{4,0},{1,5},{5,1},{2,6},{6,2},{3,7},{7,3},{8,12},{12,8},{9,1... | collective-permute-start | bytes 1572872 | tf_op jit(solution)/shard_map/ppermute | solution.py:96
  119.2 7.7 %collective-permute-start.19 = (bf16[3,4,2,2,16,512]{5,4,3,2,1,0:T(8,128)(2,1)S(1)}, bf16[3,4,2,2,16,512]{5,4,3,2,1,0:T(8,128)(2,1)S(1)}, u32[]{:S(2)}, u32[]{:S(2)}) collective-permute-start(bf16[3,4,2,2,16,512]{5,4,3,2,1,0:T(8,128)(2,1)S(1)} %pad_maximum_fusion.xs_ref), channel_id=1, source_target_pairs={{0,4},{4,0},{1,5},{5,1},{2,6},{6,2},{3,7},{7,3},{8,12},{12,8},{9,1... | collective-permute-start | bytes 2359304 | tf_op jit(solution)/shard_map/ppermute | solution.py:96
  121.9 6.1 %collective-permute-start.20 = (bf16[3,4,2,2,16,512]{5,4,3,2,1,0:T(8,128)(2,1)S(1)}, bf16[3,4,2,2,16,512]{5,4,3,2,1,0:T(8,128)(2,1)S(1)}, u32[]{:S(2)}, u32[]{:S(2)}) collective-permute-start(bf16[3,4,2,2,16,512]{5,4,3,2,1,0:T(8,128)(2,1)S(1)} %pad_maximum_fusion.1.ys_ref), channel_id=1, source_target_pairs={{0,4},{4,0},{1,5},{5,1},{2,6},{6,2},{3,7},{7,3},{8,12},{12,8},{9,1... | collective-permute-start | bytes 2359304 | tf_op jit(solution)/shard_map/ppermute | solution.py:96
  (1 other events, 6.5 us)

commit v4 on v3

--- a/solution.py
+++ b/solution.py
@@ -33,11 +33,56 @@
     return block
 
 
-def doubled(block, axis, mask):
+def interleaved(block, other, axis, mask):
     me = lax.axis_index(axis)
     low = me % 2 == 0 if mask == 1 else me < 2
-    other = neighbour(block, axis, mask)
     return jnp.concatenate([jnp.where(low, block, other), jnp.where(low, other, block)])
+
+
+def doubled(block, axis, mask):
+    return interleaved(block, neighbour(block, axis, mask), axis, mask)
+
+
+def rows_of_core(local, swapped):
+    def kernel(source, out, sem):
+        core = lax.axis_index("c")
+        copy = pltpu.make_async_copy(source.at[:, 1 - core if swapped else core], out, sem)
+        copy.start()
+        copy.wait()
+
+    blocks, _, rows, width = local.shape
+    return pl.pallas_call(
+        kernel,
+        out_shape=jax.ShapeDtypeStruct((blocks, rows, width), local.dtype),
+        in_specs=[pl.BlockSpec(memory_space=pl.ANY)],
+        out_specs=pl.BlockSpec(memory_space=pltpu.VMEM),
+        scratch_shapes=[pltpu.SemaphoreType.DMA],
+        compiler_params=pltpu.CompilerParams(vmem_limit_bytes=8 * 2**20),
+    )(local)
+
+
+def add_and_encode(ours, theirs, dims):
+    zh, zl, y, x, rows, width = dims
+
+    def kernel(ours, theirs, out):
+        def step(i, carry):
+            for h in range(zh):
+                block = h * zl * y + i
+                pair = ours[block].astype(jnp.float32) + theirs[block].astype(jnp.float32)
+                code = encode(pair)
+                for q in range(x):
+                    out[i * x + q, h * rows : (h + 1) * rows] = code[q * rows : (q + 1) * rows]
+            return carry
+
+        lax.fori_loop(0, zl * y, step, 0)
+
+    return pl.pallas_call(
+        kernel,
+        out_shape=jax.ShapeDtypeStruct((zl * y * x, zh * rows, width), ours.dtype),
+        in_specs=[pl.BlockSpec(memory_space=pltpu.VMEM)] * 2,
+        out_specs=pl.BlockSpec(memory_space=pltpu.VMEM),
+        compiler_params=pltpu.CompilerParams(vmem_limit_bytes=16 * 2**20),
+    )(ours, theirs)
 
 
 def around(block, axis):
@@ -142,14 +187,14 @@
         lax.dynamic_slice_in_dim(a, me_x * rows, rows, 0)
         for a in (master, first_moment, second_moment)
     ])[None]
-    states = doubled(states, "zh", 1)
-
-    local = grads[0].reshape(zh, zl, y, c, x, rows, width)
-    sent = lax.dynamic_index_in_dim(local, 1 - me_c, 3, keepdims=False)
-    kept = lax.dynamic_index_in_dim(local, me_c, 3, keepdims=False)
-    pair = kept.astype(jnp.float32) + lax.ppermute(sent, "c", SWAP).astype(jnp.float32)
-    coded = encode(pair).transpose(1, 2, 3, 0, 4, 5).reshape(-1, zh * rows, width)
-    coded, states = lax.optimization_barrier((coded, states))
+    other_states = neighbour(states, "zh", 1)
+
+    local = grads[0].reshape(-1, c, x * rows, width)
+    theirs = rows_of_core(local, True)
+    ours = rows_of_core(local, False)
+    coded = add_and_encode(ours, lax.ppermute(theirs, "c", SWAP), (zh, zl, y, x, rows, width))
+    coded, states, other_states = lax.optimization_barrier((coded, states, other_states))
+    states = interleaved(states, other_states, "zh", 1)
     pieces = lax.all_to_all(coded, PLANE, 0, 0, tiled=True)
     total = sum_of_four(jnp.sum(decode(pieces), axis=0), "zh")
 

time: 131 us -> 128 us (0.977)
  waiting for transfers between devices: 33.7 us -> 30 us
  Pallas kernels: 2.11 us -> 5.09 us
  other arithmetic: 6.89 us -> 4.13 us
    unnamed x6 -> x10, local copies, waits for them, and re-layouts: 0.01 us -> 4.38 us
    ppermute x4, waiting for transfers between devices: 15.3 us -> 11.6 us  [neighbour(): return lax.ppermute(block, axis, [(i, i ^ mask) for i in range(4)])]
    squeeze x1 -> x0, local copies, waits for them, and re-layouts: 3.26 us -> none  [body(): sent = lax.dynamic_index_in_dim(local, 1 - me_c, 3, keepdims=False)]
    pallas_call x0 -> x3, Pallas kernels: none -> 2.97 us  [the longest x2 1.79 us: rows_of_core(): pl.pallas_call(kernel, out_shape=jax.ShapeDtypeStruct((blocks, rows, widt...]
    transpose x1 -> x0, other arithmetic: 2.76 us -> none  [body(): encode(pair).transpose(1, 2, 3, 0, 4, 5).reshape(-1, zh * rows, width)]
  transfers between devices with their start and end apart: 22 -> 22, of which waited for: 13 -> 14; matrix products, arithmetic and copies ran while one was open for 3% -> 3% of each run, Pallas kernels for 0% -> 1%
where the time goes in v4:
time: 128 us
  starting transfers between devices  48.8 us (38%)
  blocking collectives  32.4 us (25%)
  waiting for transfers between devices  30 us (23%)
  local copies, waits for them, and re-layouts  5.74 us (4%)
  Pallas kernels  5.09 us (4%)
  other arithmetic  4.13 us (3%)
  between operations  1.77 us (1%)
    all_to_all x1, blocking collectives, body(): pieces = lax.all_to_all(coded, PLANE, 0, 0, tiled=True)  32.4 us
    all_to_all x1, starting transfers between devices, to_all(): lax.all_to_all(jnp.broadcast_to(block[None], (length, *block.shape)), axe...  13.2 us
    ppermute x3, starting transfers between devices, gather_weights(): there = [lax.ppermute(piece, 'c', SWAP) for piece in here]  13.1 us
    ppermute x4, waiting for transfers between devices, neighbour(): return lax.ppermute(block, axis, [(i, i ^ mask) for i in range(4)])  11.6 us
    ppermute x12, starting transfers between devices, around(): lax.ppermute(block, axis, [(i, (i + k) % n) for i in range(n)])  10.9 us
    ppermute x4, starting transfers between devices, neighbour(): return lax.ppermute(block, axis, [(i, i ^ mask) for i in range(4)])  8.17 us
    all_to_all x1, waiting for transfers between devices, to_all(): lax.all_to_all(jnp.broadcast_to(block[None], (length, *block.shape)), axe...  7.94 us
    ppermute x12, waiting for transfers between devices, around(): lax.ppermute(block, axis, [(i, (i + k) % n) for i in range(n)])  6.31 us
  transfers between devices with their start and end apart: 22, of which 14 were waited for; matrix products, arithmetic and copies ran while one was open for 3% of the time, Pallas kernels for 1%

profile of v4, /device:TPU:1, one launch (start us, length us, event | category | flops | bytes accessed | tf_op | source)
XLA Modules:
  0.0 128.0 jit_solution(13831198750783156709)
XLA Ops:
  0.6 2.2 %copy-done = bf16[1,4096,512]{2,1,0:T(8,128)(2,1)S(1)} copy-done((bf16[1,4096,512]{2,1,0:T(8,128)(2,1)S(1)}, bf16[1,4096,512]{2,1,0:T(8,128)(2,1)}, u32[]{:S(2)}) %copy-start) | copy-done | bytes 4194328
  2.8 1.6 %shard_map.76 = bf16[32,64,512]{2,1,0:T(8,128)(2,1)} custom-call(bf16[32,2,64,512]{3,2,1,0:T(8,128)(2,1)S(1)} %bitcast.72), custom_call_target="tpu_custom_call" | custom-call | tf_op jit(solution)/shard_map/pallas_call | solution.py:54
  4.4 3.3 %collective-permute-start = (bf16[32,64,512]{2,1,0:T(8,128)(2,1)}, bf16[32,64,512]{2,1,0:T(8,128)(2,1)S(1)}, u32[]{:S(2)}, u32[]{:S(2)}) collective-permute-start(bf16[32,64,512]{2,1,0:T(8,128)(2,1)} %shard_map.76), channel_id=1, source_target_pairs={{0,4},{4,0},{1,5},{5,1},{2,6},{6,2},{3,7},{7,3},{8,12},{12,8},{9,1... | collective-permute-start | bytes 6291464 | tf_op jit(solution)/shard_map/ppermute | solution.py:195
  7.8 1.3 %collective-permute-start.1 = (f32[1,3,16,512]{3,2,0,1:T(8,128)S(1)}, f32[1,3,16,512]{3,2,0,1:T(8,128)S(1)}, u32[]{:S(2)}, u32[]{:S(2)}) collective-permute-start(f32[1,3,16,512]{3,2,0,1:T(8,128)S(1)} %maximum_bitcast_fusion.3), channel_id=1, source_target_pairs={{0,64},{64,0},{128,192},{192,128},{1,65},{65,1},{129,193},{193,129... | collective-permute-start | bytes 294920 | tf_op jit(solution)/shard_map/ppermute | solution.py:27
  9.1 2.2 %copy-done.1 = bf16[1,4096,512]{2,1,0:T(8,128)(2,1)S(1)} copy-done((bf16[1,4096,512]{2,1,0:T(8,128)(2,1)S(1)}, bf16[1,4096,512]{2,1,0:T(8,128)(2,1)}, u32[]{:S(2)}) %copy-start.1) | copy-done | bytes 4194328
  12.9 2.5 %collective-permute-done.1 = f32[1,3,16,512]{3,2,0,1:T(8,128)S(1)} collective-permute-done((f32[1,3,16,512]{3,2,0,1:T(8,128)S(1)}, f32[1,3,16,512]{3,2,0,1:T(8,128)S(1)}, u32[]{:S(2)}, u32[]{:S(2)}) %collective-permute-start.1) | collective-permute-done | bytes 98336 | tf_op jit(solution)/shard_map/ppermute | solution.py:27
  15.4 32.4 %all_to_all.11 = bf16[32,64,512]{2,1,0:T(8,128)(2,1)S(1)} all-to-all(bf16[32,64,512]{2,1,0:T(8,128)(2,1)S(1)} %shard_map.77), channel_id=1, replica_groups=mesh['zh'=4,'zl'=2,'y'=4,'c'=2,'x'=4] {'zl','y','x'}, dimensions={0} | all-to-all | bytes 4194304 | tf_op jit(solution)/shard_map/all_to_all | solution.py:198
  47.8 1.4 %fusion.4 = f32[64,512]{1,0:T(8,128)S(1)} fusion(bf16[32,64,512]{2,1,0:T(8,128)(2,1)S(1)} %all_to_all.11), kind=kLoop, calls=%fused_computation.7 | loop fusion | flops 8355840 | bytes 2228224 | tf_op jit(solution)/shard_map/reduce_sum | solution.py:199
  49.2 3.2 %collective-permute-start.2 = (f32[64,512]{1,0:T(8,128)S(1)}, f32[64,512]{1,0:T(8,128)S(1)}, u32[]{:S(2)}, u32[]{:S(2)}) collective-permute-start(f32[64,512]{1,0:T(8,128)S(1)} %fusion.4), channel_id=1, source_target_pairs={{0,64},{64,0},{128,192},{192,128},{1,65},{65,1},{129,193},{193,129... | collective-permute-start | bytes 393224 | tf_op jit(solution)/shard_map/ppermute | solution.py:27
  52.4 4.2 %collective-permute-done.2 = f32[64,512]{1,0:T(8,128)S(1)} collective-permute-done((f32[64,512]{1,0:T(8,128)S(1)}, f32[64,512]{1,0:T(8,128)S(1)}, u32[]{:S(2)}, u32[]{:S(2)}) %collective-permute-start.2) | collective-permute-done | bytes 131104 | tf_op jit(solution)/shard_map/ppermute | solution.py:27
  56.6 2.5 %collective-permute-start.3 = (f32[64,512]{1,0:T(8,128)S(1)}, f32[64,512]{1,0:T(8,128)S(1)}, u32[]{:S(2)}, u32[]{:S(2)}) collective-permute-start(f32[64,512]{1,0:T(8,128)S(1)} %add.96), channel_id=1, source_target_pairs={{0,192},{64,128},{128,64},{192,0},{1,193},{65,129},{129,65},{193,1... | collective-permute-start | bytes 393224 | tf_op jit(solution)/shard_map/ppermute | solution.py:27
  59.2 4.9 %collective-permute-done.3 = f32[64,512]{1,0:T(8,128)S(1)} collective-permute-done((f32[64,512]{1,0:T(8,128)S(1)}, f32[64,512]{1,0:T(8,128)S(1)}, u32[]{:S(2)}, u32[]{:S(2)}) %collective-permute-start.3) | collective-permute-done | bytes 131104 | tf_op jit(solution)/shard_map/ppermute | solution.py:27
  67.1 13.2 %all-to-all-start.1 = ((f32[64,1,1]{2,1,0:T(1,128)}), f32[64,1,1]{2,1,0:T(1,128)S(1)}, u32[]{:S(2)}, u32[]{:S(2)}) async-start(f32[64,1,1]{2,1,0:T(1,128)} %broadcast_in_dim.18), calls=%async_computation.1 | async-start | bytes 65536 | tf_op jit(solution)/shard_map/all_to_all | solution.py:21
  80.3 7.9 %all-to-all-done.1 = f32[64,1,1]{2,1,0:T(1,128)S(1)} async-done(((f32[64,1,1]{2,1,0:T(1,128)}), f32[64,1,1]{2,1,0:T(1,128)S(1)}, u32[]{:S(2)}, u32[]{:S(2)}) %all-to-all-start.1) | async-done | bytes 288 | tf_op jit(solution)/shard_map/all_to_all | solution.py:21
  90.0 3.0 %collective-permute-done.5 = bf16[4,16,512]{2,1,0:T(8,128)(2,1)S(1)} collective-permute-done((bf16[4,16,512]{2,1,0:T(8,128)(2,1)S(1)}, bf16[4,16,512]{2,1,0:T(8,128)(2,1)S(1)}, u32[]{:S(2)}, u32[]{:S(2)}) %collective-permute-start.5) | collective-permute-done | bytes 65568 | tf_op jit(solution)/shard_map/ppermute | solution.py:131
  93.7 1.5 %collective-permute-start.7 = (bf16[2,2,16,512]{3,2,1,0:T(8,128)(2,1)S(1)}, bf16[2,2,16,512]{3,2,1,0:T(8,128)(2,1)S(1)}, u32[]{:S(2)}, u32[]{:S(2)}) collective-permute-start(bf16[2,2,16,512]{3,2,1,0:T(8,128)(2,1)S(1)} %get-tuple-element.31), channel_id=1, source_target_pairs={{0,16},{8,24},{16,0},{24,8},{1,17},{9,25},{17,1},{25,9},{2,18},{10... | collective-permute-start | bytes 196616 | tf_op jit(solution)/shard_map/ppermute | solution.py:90
  96.0 1.5 %collective-permute-start.10 = (bf16[6,16,512]{2,1,0:T(8,128)(2,1)S(1)}, bf16[6,16,512]{2,1,0:T(8,128)(2,1)S(1)}, u32[]{:S(2)}, u32[]{:S(2)}) collective-permute-start(bf16[6,16,512]{2,1,0:T(8,128)(2,1)S(1)} %pad_maximum_fusion.4), channel_id=1, source_target_pairs={{0,2},{1,3},{2,0},{3,1},{4,6},{5,7},{6,4},{7,5},{8,10},{9,11},{10,... | collective-permute-start | bytes 294920 | tf_op jit(solution)/shard_map/ppermute | solution.py:90
  99.7 1.5 %collective-permute-done.10 = bf16[6,16,512]{2,1,0:T(8,128)(2,1)S(1)} collective-permute-done((bf16[6,16,512]{2,1,0:T(8,128)(2,1)S(1)}, bf16[6,16,512]{2,1,0:T(8,128)(2,1)S(1)}, u32[]{:S(2)}, u32[]{:S(2)}) %collective-permute-start.10) | collective-permute-done | bytes 98336 | tf_op jit(solution)/shard_map/ppermute | solution.py:90
  103.4 1.7 %collective-permute-start.13 = (bf16[4,2,2,16,512]{4,3,2,1,0:T(8,128)(2,1)S(1)}, bf16[4,2,2,16,512]{4,3,2,1,0:T(8,128)(2,1)S(1)}, u32[]{:S(2)}, u32[]{:S(2)}) collective-permute-start(bf16[4,2,2,16,512]{4,3,2,1,0:T(8,128)(2,1)S(1)} %get-tuple-element.23), channel_id=1, source_target_pairs={{0,2},{1,3},{2,0},{3,1},{4,6},{5,7},{6,4},{7,5},{8,10},{9,11},{10,... | collective-permute-start | bytes 786440 | tf_op jit(solution)/shard_map/ppermute | solution.py:90
  105.1 2.6 %collective-permute-start.17 = (bf16[4,2,2,16,512]{4,3,2,1,0:T(8,128)(2,1)S(1)}, bf16[4,2,2,16,512]{4,3,2,1,0:T(8,128)(2,1)S(1)}, u32[]{:S(2)}, u32[]{:S(2)}) collective-permute-start(bf16[4,2,2,16,512]{4,3,2,1,0:T(8,128)(2,1)S(1)} %get-tuple-element.22), channel_id=1, source_target_pairs={{0,24},{8,0},{16,8},{24,16},{1,25},{9,1},{17,9},{25,17},{2,26},{10... | collective-permute-start | bytes 786440 | tf_op jit(solution)/shard_map/ppermute | solution.py:90
  110.2 6.3 %collective-permute-start.18 = (bf16[2,4,2,2,16,512]{5,4,3,2,1,0:T(8,128)(2,1)S(1)}, bf16[2,4,2,2,16,512]{5,4,3,2,1,0:T(8,128)(2,1)S(1)}, u32[]{:S(2)}, u32[]{:S(2)}) collective-permute-start(bf16[2,4,2,2,16,512]{5,4,3,2,1,0:T(8,128)(2,1)S(1)} %pad_maximum_fusion.2.own), channel_id=1, source_target_pairs={{0,4},{4,0},{1,5},{5,1},{2,6},{6,2},{3,7},{7,3},{8,12},{12,8},{9,1... | collective-permute-start | bytes 1572872 | tf_op jit(solution)/shard_map/ppermute | solution.py:141
  116.9 2.5 %collective-permute-start.19 = (bf16[3,4,2,2,16,512]{5,4,3,2,1,0:T(8,128)(2,1)S(1)}, bf16[3,4,2,2,16,512]{5,4,3,2,1,0:T(8,128)(2,1)S(1)}, u32[]{:S(2)}, u32[]{:S(2)}) collective-permute-start(bf16[3,4,2,2,16,512]{5,4,3,2,1,0:T(8,128)(2,1)S(1)} %pad_maximum_fusion.xs_ref), channel_id=1, source_target_pairs={{0,4},{4,0},{1,5},{5,1},{2,6},{6,2},{3,7},{7,3},{8,12},{12,8},{9,1... | collective-permute-start | bytes 2359304 | tf_op jit(solution)/shard_map/ppermute | solution.py:141
  119.5 4.2 %collective-permute-start.20 = (bf16[3,4,2,2,16,512]{5,4,3,2,1,0:T(8,128)(2,1)S(1)}, bf16[3,4,2,2,16,512]{5,4,3,2,1,0:T(8,128)(2,1)S(1)}, u32[]{:S(2)}, u32[]{:S(2)}) collective-permute-start(bf16[3,4,2,2,16,512]{5,4,3,2,1,0:T(8,128)(2,1)S(1)} %pad_maximum_fusion.1.ys_ref), channel_id=1, source_target_pairs={{0,4},{4,0},{1,5},{5,1},{2,6},{6,2},{3,7},{7,3},{8,12},{12,8},{9,1... | collective-permute-start | bytes 2359304 | tf_op jit(solution)/shard_map/ppermute | solution.py:141
  125.7 2.1 %shard_map.78 = bf16[4,2,4,2,4,16,512]{6,5,4,3,2,1,0:T(8,128)(2,1)} custom-call(bf16[2,4,2,2,16,512]{5,4,3,2,1,0:T(8,128)(2,1)S(1)} %pad_maximum_fusion.2.own, bf16[3,4,2,2,16,512]{5,4,3,2,1,0:T(8,128)(2,1)S(1)} %pad_maximum_fusion.xs_ref, bf16[3,4,2,2,16,512]{5,4,3,2,1,0:T(8,128)(2,1)S(1)} %pad_maximum_fusion.1.ys_ref, ...), custom_call_target="tpu_custom_call" | custom-call | tf_op jit(solution)/shard_map/pallas_call | solution.py:143
  (67 shorter events, 16.4 us)
Async XLA Ops:
  2.8 4.9 %copy-start.3 = (f32[64,512]{1,0:T(8,128)S(1)}, f32[64,512]{1,0:T(8,128)}, u32[]{:S(2)}) copy-start(f32[64,512]{1,0:T(8,128)} %param.7) | copy-start | bytes 393220
  2.8 4.9 %copy-start.4 = (f32[64,512]{1,0:T(8,128)S(1)}, f32[64,512]{1,0:T(8,128)}, u32[]{:S(2)}) copy-start(f32[64,512]{1,0:T(8,128)} %param.6) | copy-start | bytes 393220
  4.4 7.3 %collective-permute-start = (bf16[32,64,512]{2,1,0:T(8,128)(2,1)}, bf16[32,64,512]{2,1,0:T(8,128)(2,1)S(1)}, u32[]{:S(2)}, u32[]{:S(2)}) collective-permute-start(bf16[32,64,512]{2,1,0:T(8,128)(2,1)} %shard_map.76), channel_id=1, source_target_pairs={{0,4},{4,0},{1,5},{5,1},{2,6},{6,2},{3,7},{7,3},{8,12},{12,8},{9,1... | collective-permute-start | bytes 6291464 | tf_op jit(solution)/shard_map/ppermute | solution.py:195
  7.8 7.6 %collective-permute-start.1 = (f32[1,3,16,512]{3,2,0,1:T(8,128)S(1)}, f32[1,3,16,512]{3,2,0,1:T(8,128)S(1)}, u32[]{:S(2)}, u32[]{:S(2)}) collective-permute-start(f32[1,3,16,512]{3,2,0,1:T(8,128)S(1)} %maximum_bitcast_fusion.3), channel_id=1, source_target_pairs={{0,64},{64,0},{128,192},{192,128},{1,65},{65,1},{129,193},{193,129... | collective-permute-start | bytes 294920 | tf_op jit(solution)/shard_map/ppermute | solution.py:27
  49.2 7.4 %collective-permute-start.2 = (f32[64,512]{1,0:T(8,128)S(1)}, f32[64,512]{1,0:T(8,128)S(1)}, u32[]{:S(2)}, u32[]{:S(2)}) collective-permute-start(f32[64,512]{1,0:T(8,128)S(1)} %fusion.4), channel_id=1, source_target_pairs={{0,64},{64,0},{128,192},{192,128},{1,65},{65,1},{129,193},{193,129... | collective-permute-start | bytes 393224 | tf_op jit(solution)/shard_map/ppermute | solution.py:27
  56.6 7.4 %collective-permute-start.3 = (f32[64,512]{1,0:T(8,128)S(1)}, f32[64,512]{1,0:T(8,128)S(1)}, u32[]{:S(2)}, u32[]{:S(2)}) collective-permute-start(f32[64,512]{1,0:T(8,128)S(1)} %add.96), channel_id=1, source_target_pairs={{0,192},{64,128},{128,64},{192,0},{1,193},{65,129},{129,65},{193,1... | collective-permute-start | bytes 393224 | tf_op jit(solution)/shard_map/ppermute | solution.py:27
  64.0 25.6 %collective-permute-start.4 = (f32[2,3,16,512]{3,2,0,1:T(8,128)S(1)}, f32[2,3,16,512]{3,2,0,1:T(8,128)S(1)}, u32[]{:S(2)}, u32[]{:S(2)}) collective-permute-start(f32[2,3,16,512]{3,2,0,1:T(8,128)S(1)} %pad_maximum_fusion.3), channel_id=1, source_target_pairs={{0,192},{64,128},{128,64},{192,0},{1,193},{65,129},{129,65},{193,1... | collective-permute-start | bytes 589832 | tf_op jit(solution)/shard_map/ppermute | solution.py:27
  67.1 21.1 %all-to-all-start.1 = ((f32[64,1,1]{2,1,0:T(1,128)}), f32[64,1,1]{2,1,0:T(1,128)S(1)}, u32[]{:S(2)}, u32[]{:S(2)}) async-start(f32[64,1,1]{2,1,0:T(1,128)} %broadcast_in_dim.18), calls=%async_computation.1 | async-start | bytes 65536 | tf_op jit(solution)/shard_map/all_to_all | solution.py:21
  89.8 3.2 %collective-permute-start.5 = (bf16[4,16,512]{2,1,0:T(8,128)(2,1)S(1)}, bf16[4,16,512]{2,1,0:T(8,128)(2,1)S(1)}, u32[]{:S(2)}, u32[]{:S(2)}) collective-permute-start(bf16[4,16,512]{2,1,0:T(8,128)(2,1)S(1)} %bitcast.77), channel_id=1, source_target_pairs={{0,32},{32,0},{1,33},{33,1},{2,34},{34,2},{3,35},{35,3},{4,36},{36... | collective-permute-start | bytes 196616 | tf_op jit(solution)/shard_map/ppermute | solution.py:131
  93.1 4.4 %collective-permute-start.8 = (bf16[2,2,16,512]{3,2,1,0:T(8,128)(2,1)S(1)}, bf16[2,2,16,512]{3,2,1,0:T(8,128)(2,1)S(1)}, u32[]{:S(2)}, u32[]{:S(2)}) collective-permute-start(bf16[2,2,16,512]{3,2,1,0:T(8,128)(2,1)S(1)} %get-tuple-element.31), channel_id=1, source_target_pairs={{0,24},{8,0},{16,8},{24,16},{1,25},{9,1},{17,9},{25,17},{2,26},{10... | collective-permute-start | bytes 196616 | tf_op jit(solution)/shard_map/ppermute | solution.py:90
  93.7 4.6 %collective-permute-start.7 = (bf16[2,2,16,512]{3,2,1,0:T(8,128)(2,1)S(1)}, bf16[2,2,16,512]{3,2,1,0:T(8,128)(2,1)S(1)}, u32[]{:S(2)}, u32[]{:S(2)}) collective-permute-start(bf16[2,2,16,512]{3,2,1,0:T(8,128)(2,1)S(1)} %get-tuple-element.31), channel_id=1, source_target_pairs={{0,16},{8,24},{16,0},{24,8},{1,17},{9,25},{17,1},{25,9},{2,18},{10... | collective-permute-start | bytes 196616 | tf_op jit(solution)/shard_map/ppermute | solution.py:90
  95.3 4.3 %collective-permute-start.6 = (bf16[2,2,16,512]{3,2,1,0:T(8,128)(2,1)S(1)}, bf16[2,2,16,512]{3,2,1,0:T(8,128)(2,1)S(1)}, u32[]{:S(2)}, u32[]{:S(2)}) collective-permute-start(bf16[2,2,16,512]{3,2,1,0:T(8,128)(2,1)S(1)} %get-tuple-element.31), channel_id=1, source_target_pairs={{0,8},{8,16},{16,24},{24,0},{1,9},{9,17},{17,25},{25,1},{2,10},{10... | collective-permute-start | bytes 196616 | tf_op jit(solution)/shard_map/ppermute | solution.py:90
  95.3 4.3 %collective-permute-start.11 = (bf16[6,16,512]{2,1,0:T(8,128)(2,1)S(1)}, bf16[6,16,512]{2,1,0:T(8,128)(2,1)S(1)}, u32[]{:S(2)}, u32[]{:S(2)}) collective-permute-start(bf16[6,16,512]{2,1,0:T(8,128)(2,1)S(1)} %pad_maximum_fusion.4), channel_id=1, source_target_pairs={{0,3},{1,0},{2,1},{3,2},{4,7},{5,4},{6,5},{7,6},{8,11},{9,8},{10,9... | collective-permute-start | bytes 294920 | tf_op jit(solution)/shard_map/ppermute | solution.py:90
  96.0 5.2 %collective-permute-start.10 = (bf16[6,16,512]{2,1,0:T(8,128)(2,1)S(1)}, bf16[6,16,512]{2,1,0:T(8,128)(2,1)S(1)}, u32[]{:S(2)}, u32[]{:S(2)}) collective-permute-start(bf16[6,16,512]{2,1,0:T(8,128)(2,1)S(1)} %pad_maximum_fusion.4), channel_id=1, source_target_pairs={{0,2},{1,3},{2,0},{3,1},{4,6},{5,7},{6,4},{7,5},{8,10},{9,11},{10,... | collective-permute-start | bytes 294920 | tf_op jit(solution)/shard_map/ppermute | solution.py:90
  97.4 5.0 %collective-permute-start.9 = (bf16[6,16,512]{2,1,0:T(8,128)(2,1)S(1)}, bf16[6,16,512]{2,1,0:T(8,128)(2,1)S(1)}, u32[]{:S(2)}, u32[]{:S(2)}) collective-permute-start(bf16[6,16,512]{2,1,0:T(8,128)(2,1)S(1)} %pad_maximum_fusion.4), channel_id=1, source_target_pairs={{0,1},{1,2},{2,3},{3,0},{4,5},{5,6},{6,7},{7,4},{8,9},{9,10},{10,1... | collective-permute-start | bytes 294920 | tf_op jit(solution)/shard_map/ppermute | solution.py:90
  102.6 5.5 %collective-permute-start.14 = (bf16[4,2,2,16,512]{4,3,2,1,0:T(8,128)(2,1)S(1)}, bf16[4,2,2,16,512]{4,3,2,1,0:T(8,128)(2,1)S(1)}, u32[]{:S(2)}, u32[]{:S(2)}) collective-permute-start(bf16[4,2,2,16,512]{4,3,2,1,0:T(8,128)(2,1)S(1)} %get-tuple-element.23), channel_id=1, source_target_pairs={{0,3},{1,0},{2,1},{3,2},{4,7},{5,4},{6,5},{7,6},{8,11},{9,8},{10,9... | collective-permute-start | bytes 786440 | tf_op jit(solution)/shard_map/ppermute | solution.py:90
  103.4 6.8 %collective-permute-start.13 = (bf16[4,2,2,16,512]{4,3,2,1,0:T(8,128)(2,1)S(1)}, bf16[4,2,2,16,512]{4,3,2,1,0:T(8,128)(2,1)S(1)}, u32[]{:S(2)}, u32[]{:S(2)}) collective-permute-start(bf16[4,2,2,16,512]{4,3,2,1,0:T(8,128)(2,1)S(1)} %get-tuple-element.23), channel_id=1, source_target_pairs={{0,2},{1,3},{2,0},{3,1},{4,6},{5,7},{6,4},{7,5},{8,10},{9,11},{10,... | collective-permute-start | bytes 786440 | tf_op jit(solution)/shard_map/ppermute | solution.py:90
  105.1 11.7 %collective-permute-start.12 = (bf16[4,2,2,16,512]{4,3,2,1,0:T(8,128)(2,1)S(1)}, bf16[4,2,2,16,512]{4,3,2,1,0:T(8,128)(2,1)S(1)}, u32[]{:S(2)}, u32[]{:S(2)}) collective-permute-start(bf16[4,2,2,16,512]{4,3,2,1,0:T(8,128)(2,1)S(1)} %get-tuple-element.23), channel_id=1, source_target_pairs={{0,1},{1,2},{2,3},{3,0},{4,5},{5,6},{6,7},{7,4},{8,9},{9,10},{10,1... | collective-permute-start | bytes 786440 | tf_op jit(solution)/shard_map/ppermute | solution.py:90
  105.1 14.3 %collective-permute-start.17 = (bf16[4,2,2,16,512]{4,3,2,1,0:T(8,128)(2,1)S(1)}, bf16[4,2,2,16,512]{4,3,2,1,0:T(8,128)(2,1)S(1)}, u32[]{:S(2)}, u32[]{:S(2)}) collective-permute-start(bf16[4,2,2,16,512]{4,3,2,1,0:T(8,128)(2,1)S(1)} %get-tuple-element.22), channel_id=1, source_target_pairs={{0,24},{8,0},{16,8},{24,16},{1,25},{9,1},{17,9},{25,17},{2,26},{10... | collective-permute-start | bytes 786440 | tf_op jit(solution)/shard_map/ppermute | solution.py:90
  107.7 11.7 %collective-permute-start.16 = (bf16[4,2,2,16,512]{4,3,2,1,0:T(8,128)(2,1)S(1)}, bf16[4,2,2,16,512]{4,3,2,1,0:T(8,128)(2,1)S(1)}, u32[]{:S(2)}, u32[]{:S(2)}) collective-permute-start(bf16[4,2,2,16,512]{4,3,2,1,0:T(8,128)(2,1)S(1)} %get-tuple-element.22), channel_id=1, source_target_pairs={{0,16},{8,24},{16,0},{24,8},{1,17},{9,25},{17,1},{25,9},{2,18},{10... | collective-permute-start | bytes 786440 | tf_op jit(solution)/shard_map/ppermute | solution.py:90
  108.1 11.4 %collective-permute-start.15 = (bf16[4,2,2,16,512]{4,3,2,1,0:T(8,128)(2,1)S(1)}, bf16[4,2,2,16,512]{4,3,2,1,0:T(8,128)(2,1)S(1)}, u32[]{:S(2)}, u32[]{:S(2)}) collective-permute-start(bf16[4,2,2,16,512]{4,3,2,1,0:T(8,128)(2,1)S(1)} %get-tuple-element.22), channel_id=1, source_target_pairs={{0,8},{8,16},{16,24},{24,0},{1,9},{9,17},{17,25},{25,1},{2,10},{10... | collective-permute-start | bytes 786440 | tf_op jit(solution)/shard_map/ppermute | solution.py:90
  110.2 14.4 %collective-permute-start.18 = (bf16[2,4,2,2,16,512]{5,4,3,2,1,0:T(8,128)(2,1)S(1)}, bf16[2,4,2,2,16,512]{5,4,3,2,1,0:T(8,128)(2,1)S(1)}, u32[]{:S(2)}, u32[]{:S(2)}) collective-permute-start(bf16[2,4,2,2,16,512]{5,4,3,2,1,0:T(8,128)(2,1)S(1)} %pad_maximum_fusion.2.own), channel_id=1, source_target_pairs={{0,4},{4,0},{1,5},{5,1},{2,6},{6,2},{3,7},{7,3},{8,12},{12,8},{9,1... | collective-permute-start | bytes 1572872 | tf_op jit(solution)/shard_map/ppermute | solution.py:141
  116.9 7.7 %collective-permute-start.19 = (bf16[3,4,2,2,16,512]{5,4,3,2,1,0:T(8,128)(2,1)S(1)}, bf16[3,4,2,2,16,512]{5,4,3,2,1,0:T(8,128)(2,1)S(1)}, u32[]{:S(2)}, u32[]{:S(2)}) collective-permute-start(bf16[3,4,2,2,16,512]{5,4,3,2,1,0:T(8,128)(2,1)S(1)} %pad_maximum_fusion.xs_ref), channel_id=1, source_target_pairs={{0,4},{4,0},{1,5},{5,1},{2,6},{6,2},{3,7},{7,3},{8,12},{12,8},{9,1... | collective-permute-start | bytes 2359304 | tf_op jit(solution)/shard_map/ppermute | solution.py:141
  119.5 6.1 %collective-permute-start.20 = (bf16[3,4,2,2,16,512]{5,4,3,2,1,0:T(8,128)(2,1)S(1)}, bf16[3,4,2,2,16,512]{5,4,3,2,1,0:T(8,128)(2,1)S(1)}, u32[]{:S(2)}, u32[]{:S(2)}) collective-permute-start(bf16[3,4,2,2,16,512]{5,4,3,2,1,0:T(8,128)(2,1)S(1)} %pad_maximum_fusion.1.ys_ref), channel_id=1, source_target_pairs={{0,4},{4,0},{1,5},{5,1},{2,6},{6,2},{3,7},{7,3},{8,12},{12,8},{9,1... | collective-permute-start | bytes 2359304 | tf_op jit(solution)/shard_map/ppermute | solution.py:141
  (3 other events, 9.3 us)

commit v5 on v4

--- a/solution.py
+++ b/solution.py
@@ -37,10 +37,6 @@
     me = lax.axis_index(axis)
     low = me % 2 == 0 if mask == 1 else me < 2
     return jnp.concatenate([jnp.where(low, block, other), jnp.where(low, other, block)])
-
-
-def doubled(block, axis, mask):
-    return interleaved(block, neighbour(block, axis, mask), axis, mask)
 
 
 def rows_of_core(local, swapped):
@@ -194,12 +190,14 @@
     ours = rows_of_core(local, False)
     coded = add_and_encode(ours, lax.ppermute(theirs, "c", SWAP), (zh, zl, y, x, rows, width))
     coded, states, other_states = lax.optimization_barrier((coded, states, other_states))
-    states = interleaved(states, other_states, "zh", 1)
+    coded, states = lax.optimization_barrier((coded, interleaved(states, other_states, "zh", 1)))
     pieces = lax.all_to_all(coded, PLANE, 0, 0, tiled=True)
-    total = sum_of_four(jnp.sum(decode(pieces), axis=0), "zh")
-
-    total, states = lax.optimization_barrier((total, states))
-    states = doubled(states, "zh", 3)
+    partial, states = lax.optimization_barrier((jnp.sum(decode(pieces), axis=0), states))
+    other_states = neighbour(states, "zh", 3)
+    total = sum_of_four(partial, "zh")
+
+    total, states, other_states = lax.optimization_barrier((total, states, other_states))
+    states = interleaved(states, other_states, "zh", 3)
     squares = jnp.sum(to_all(jnp.sum(total * total), OWNERS))
     factor = clip_factor(squares, width)
 

time: 128 us -> 127 us (level)
  starting transfers between devices: 48.8 us -> 46.8 us
  waiting for transfers between devices: 30 us -> 28.3 us
  Pallas kernels: 5.09 us -> 6.59 us
    all_to_all x1, starting transfers between devices: 13.2 us -> 11.2 us  [to_all(): lax.all_to_all(jnp.broadcast_to(block[None], (length, *block.shape)), axe...]
    ppermute x4, waiting for transfers between devices: 11.6 us -> 9.75 us  [neighbour(): return lax.ppermute(block, axis, [(i, i ^ mask) for i in range(4)])]
    pallas_call x1, Pallas kernels: 1.19 us -> 2.78 us  [add_and_encode(): pl.pallas_call(kernel, out_shape=jax.ShapeDtypeStruct((zl * y * x, zh * r...]
  transfers between devices with their start and end apart: 22 -> 22, of which waited for: 14 -> 14; matrix products, arithmetic and copies ran while one was open for 3% -> 1% of each run, Pallas kernels for 1% -> 2%
where the time goes in v5:
time: 127 us
  starting transfers between devices  46.8 us (37%)
  blocking collectives  33.5 us (26%)
  waiting for transfers between devices  28.3 us (22%)
  Pallas kernels  6.59 us (5%)
  local copies, waits for them, and re-layouts  5.74 us (5%)
  other arithmetic  4.13 us (3%)
  between operations  1.77 us (1%)
    all_to_all x1, blocking collectives, body(): pieces = lax.all_to_all(coded, PLANE, 0, 0, tiled=True)  33.5 us
    ppermute x3, starting transfers between devices, gather_weights(): there = [lax.ppermute(piece, 'c', SWAP) for piece in here]  13.1 us
    all_to_all x1, starting transfers between devices, to_all(): lax.all_to_all(jnp.broadcast_to(block[None], (length, *block.shape)), axe...  11.2 us
    ppermute x12, starting transfers between devices, around(): lax.ppermute(block, axis, [(i, (i + k) % n) for i in range(n)])  10.9 us
    ppermute x4, waiting for transfers between devices, neighbour(): return lax.ppermute(block, axis, [(i, i ^ mask) for i in range(4)])  9.75 us
    ppermute x4, starting transfers between devices, neighbour(): return lax.ppermute(block, axis, [(i, i ^ mask) for i in range(4)])  8.15 us
    all_to_all x1, waiting for transfers between devices, to_all(): lax.all_to_all(jnp.broadcast_to(block[None], (length, *block.shape)), axe...  7.84 us
    ppermute x12, waiting for transfers between devices, around(): lax.ppermute(block, axis, [(i, (i + k) % n) for i in range(n)])  6.3 us
  transfers between devices with their start and end apart: 22, of which 14 were waited for; matrix products, arithmetic and copies ran while one was open for 1% of the time, Pallas kernels for 2%

profile of v5, /device:TPU:1, one launch (start us, length us, event | category | flops | bytes accessed | tf_op | source)
XLA Modules:
  0.0 126.9 jit_solution(3825197324451131614)
XLA Ops:
  0.6 2.2 %copy-done = bf16[1,4096,512]{2,1,0:T(8,128)(2,1)S(1)} copy-done((bf16[1,4096,512]{2,1,0:T(8,128)(2,1)S(1)}, bf16[1,4096,512]{2,1,0:T(8,128)(2,1)}, u32[]{:S(2)}) %copy-start) | copy-done | bytes 4194328
  2.8 1.6 %shard_map.76 = bf16[32,64,512]{2,1,0:T(8,128)(2,1)} custom-call(bf16[32,2,64,512]{3,2,1,0:T(8,128)(2,1)S(1)} %bitcast.72), custom_call_target="tpu_custom_call" | custom-call | tf_op jit(solution)/shard_map/pallas_call | solution.py:50
  4.4 3.3 %collective-permute-start = (bf16[32,64,512]{2,1,0:T(8,128)(2,1)}, bf16[32,64,512]{2,1,0:T(8,128)(2,1)}, u32[]{:S(2)}, u32[]{:S(2)}) collective-permute-start(bf16[32,64,512]{2,1,0:T(8,128)(2,1)} %shard_map.76), channel_id=1, source_target_pairs={{0,4},{4,0},{1,5},{5,1},{2,6},{6,2},{3,7},{7,3},{8,12},{12,8},{9,1... | collective-permute-start | bytes 6291464 | tf_op jit(solution)/shard_map/ppermute | solution.py:191
  9.1 2.2 %copy-done.1 = bf16[1,4096,512]{2,1,0:T(8,128)(2,1)S(1)} copy-done((bf16[1,4096,512]{2,1,0:T(8,128)(2,1)S(1)}, bf16[1,4096,512]{2,1,0:T(8,128)(2,1)}, u32[]{:S(2)}) %copy-start.1) | copy-done | bytes 4194328
  11.8 2.8 %shard_map.77 = bf16[32,64,512]{2,1,0:T(8,128)(2,1)S(1)} custom-call(bf16[32,64,512]{2,1,0:T(8,128)(2,1)S(1)} %shard_map.75.ours, bf16[32,64,512]{2,1,0:T(8,128)(2,1)} %collective-permute-done.theirs), custom_call_target="tpu_custom_call" | custom-call | tf_op jit(solution)/shard_map/pallas_call | solution.py:75
  15.5 33.5 %all_to_all.11 = bf16[32,64,512]{2,1,0:T(8,128)(2,1)S(1)} all-to-all(bf16[32,64,512]{2,1,0:T(8,128)(2,1)S(1)} %shard_map.77), channel_id=1, replica_groups=mesh['zh'=4,'zl'=2,'y'=4,'c'=2,'x'=4] {'zl','y','x'}, dimensions={0} | all-to-all | bytes 4194304 | tf_op jit(solution)/shard_map/all_to_all | solution.py:194
  49.0 1.4 %fusion.4 = f32[64,512]{1,0:T(8,128)S(1)} fusion(bf16[32,64,512]{2,1,0:T(8,128)(2,1)S(1)} %all_to_all.11), kind=kLoop, calls=%fused_computation.7 | loop fusion | flops 8355840 | bytes 2228224 | tf_op jit(solution)/shard_map/reduce_sum | solution.py:195
  50.3 2.1 %collective-permute-start.2 = (f32[64,512]{1,0:T(8,128)S(1)}, f32[64,512]{1,0:T(8,128)S(1)}, u32[]{:S(2)}, u32[]{:S(2)}) collective-permute-start(f32[64,512]{1,0:T(8,128)S(1)} %fusion.4), channel_id=1, source_target_pairs={{0,64},{64,0},{128,192},{192,128},{1,65},{65,1},{129,193},{193,129... | collective-permute-start | bytes 393224 | tf_op jit(solution)/shard_map/ppermute | solution.py:27
  52.4 2.5 %collective-permute-start.4 = (f32[2,3,16,512]{3,2,0,1:T(8,128)S(1)}, f32[2,3,16,512]{3,2,0,1:T(8,128)S(1)}, u32[]{:S(2)}, u32[]{:S(2)}) collective-permute-start(f32[2,3,16,512]{3,2,0,1:T(8,128)S(1)} %pad_maximum_fusion.3), channel_id=1, source_target_pairs={{0,192},{64,128},{128,64},{192,0},{1,193},{65,129},{129,65},{193,1... | collective-permute-start | bytes 589832 | tf_op jit(solution)/shard_map/ppermute | solution.py:27
  55.0 2.0 %collective-permute-done.2 = f32[64,512]{1,0:T(8,128)S(1)} collective-permute-done((f32[64,512]{1,0:T(8,128)S(1)}, f32[64,512]{1,0:T(8,128)S(1)}, u32[]{:S(2)}, u32[]{:S(2)}) %collective-permute-start.2) | collective-permute-done | bytes 131104 | tf_op jit(solution)/shard_map/ppermute | solution.py:27
  57.0 2.2 %collective-permute-start.3 = (f32[64,512]{1,0:T(8,128)S(1)}, f32[64,512]{1,0:T(8,128)S(1)}, u32[]{:S(2)}, u32[]{:S(2)}) collective-permute-start(f32[64,512]{1,0:T(8,128)S(1)} %add.97), channel_id=1, source_target_pairs={{0,192},{64,128},{128,64},{192,0},{1,193},{65,129},{129,65},{193,1... | collective-permute-start | bytes 393224 | tf_op jit(solution)/shard_map/ppermute | solution.py:27
  59.2 7.0 %collective-permute-done.3 = f32[64,512]{1,0:T(8,128)S(1)} collective-permute-done((f32[64,512]{1,0:T(8,128)S(1)}, f32[64,512]{1,0:T(8,128)S(1)}, u32[]{:S(2)}, u32[]{:S(2)}) %collective-permute-start.3) | collective-permute-done | bytes 131104 | tf_op jit(solution)/shard_map/ppermute | solution.py:27
  68.1 11.2 %all-to-all-start.1 = ((f32[64,1,1]{2,1,0:T(1,128)}), f32[64,1,1]{2,1,0:T(1,128)S(1)}, u32[]{:S(2)}, u32[]{:S(2)}) async-start(f32[64,1,1]{2,1,0:T(1,128)} %broadcast_in_dim.18), calls=%async_computation.1 | async-start | bytes 65536 | tf_op jit(solution)/shard_map/all_to_all | solution.py:21
  79.5 7.8 %all-to-all-done.1 = f32[64,1,1]{2,1,0:T(1,128)S(1)} async-done(((f32[64,1,1]{2,1,0:T(1,128)}), f32[64,1,1]{2,1,0:T(1,128)S(1)}, u32[]{:S(2)}, u32[]{:S(2)}) %all-to-all-start.1) | async-done | bytes 288 | tf_op jit(solution)/shard_map/all_to_all | solution.py:21
  89.0 3.0 %collective-permute-done.5 = bf16[4,16,512]{2,1,0:T(8,128)(2,1)S(1)} collective-permute-done((bf16[4,16,512]{2,1,0:T(8,128)(2,1)S(1)}, bf16[4,16,512]{2,1,0:T(8,128)(2,1)S(1)}, u32[]{:S(2)}, u32[]{:S(2)}) %collective-permute-start.5) | collective-permute-done | bytes 65568 | tf_op jit(solution)/shard_map/ppermute | solution.py:127
  92.7 1.5 %collective-permute-start.7 = (bf16[2,2,16,512]{3,2,1,0:T(8,128)(2,1)S(1)}, bf16[2,2,16,512]{3,2,1,0:T(8,128)(2,1)S(1)}, u32[]{:S(2)}, u32[]{:S(2)}) collective-permute-start(bf16[2,2,16,512]{3,2,1,0:T(8,128)(2,1)S(1)} %get-tuple-element.41), channel_id=1, source_target_pairs={{0,16},{8,24},{16,0},{24,8},{1,17},{9,25},{17,1},{25,9},{2,18},{10... | collective-permute-start | bytes 196616 | tf_op jit(solution)/shard_map/ppermute | solution.py:86
  95.0 1.5 %collective-permute-start.10 = (bf16[6,16,512]{2,1,0:T(8,128)(2,1)S(1)}, bf16[6,16,512]{2,1,0:T(8,128)(2,1)S(1)}, u32[]{:S(2)}, u32[]{:S(2)}) collective-permute-start(bf16[6,16,512]{2,1,0:T(8,128)(2,1)S(1)} %pad_maximum_fusion.4), channel_id=1, source_target_pairs={{0,2},{1,3},{2,0},{3,1},{4,6},{5,7},{6,4},{7,5},{8,10},{9,11},{10,... | collective-permute-start | bytes 294920 | tf_op jit(solution)/shard_map/ppermute | solution.py:86
  98.6 1.5 %collective-permute-done.10 = bf16[6,16,512]{2,1,0:T(8,128)(2,1)S(1)} collective-permute-done((bf16[6,16,512]{2,1,0:T(8,128)(2,1)S(1)}, bf16[6,16,512]{2,1,0:T(8,128)(2,1)S(1)}, u32[]{:S(2)}, u32[]{:S(2)}) %collective-permute-start.10) | collective-permute-done | bytes 98336 | tf_op jit(solution)/shard_map/ppermute | solution.py:86
  102.4 1.7 %collective-permute-start.13 = (bf16[4,2,2,16,512]{4,3,2,1,0:T(8,128)(2,1)S(1)}, bf16[4,2,2,16,512]{4,3,2,1,0:T(8,128)(2,1)S(1)}, u32[]{:S(2)}, u32[]{:S(2)}) collective-permute-start(bf16[4,2,2,16,512]{4,3,2,1,0:T(8,128)(2,1)S(1)} %get-tuple-element.33), channel_id=1, source_target_pairs={{0,2},{1,3},{2,0},{3,1},{4,6},{5,7},{6,4},{7,5},{8,10},{9,11},{10,... | collective-permute-start | bytes 786440 | tf_op jit(solution)/shard_map/ppermute | solution.py:86
  104.1 2.6 %collective-permute-start.17 = (bf16[4,2,2,16,512]{4,3,2,1,0:T(8,128)(2,1)S(1)}, bf16[4,2,2,16,512]{4,3,2,1,0:T(8,128)(2,1)S(1)}, u32[]{:S(2)}, u32[]{:S(2)}) collective-permute-start(bf16[4,2,2,16,512]{4,3,2,1,0:T(8,128)(2,1)S(1)} %get-tuple-element.32), channel_id=1, source_target_pairs={{0,24},{8,0},{16,8},{24,16},{1,25},{9,1},{17,9},{25,17},{2,26},{10... | collective-permute-start | bytes 786440 | tf_op jit(solution)/shard_map/ppermute | solution.py:86
  109.2 6.3 %collective-permute-start.18 = (bf16[2,4,2,2,16,512]{5,4,3,2,1,0:T(8,128)(2,1)S(1)}, bf16[2,4,2,2,16,512]{5,4,3,2,1,0:T(8,128)(2,1)S(1)}, u32[]{:S(2)}, u32[]{:S(2)}) collective-permute-start(bf16[2,4,2,2,16,512]{5,4,3,2,1,0:T(8,128)(2,1)S(1)} %pad_maximum_fusion.2.own), channel_id=1, source_target_pairs={{0,4},{4,0},{1,5},{5,1},{2,6},{6,2},{3,7},{7,3},{8,12},{12,8},{9,1... | collective-permute-start | bytes 1572872 | tf_op jit(solution)/shard_map/ppermute | solution.py:137
  115.8 2.5 %collective-permute-start.19 = (bf16[3,4,2,2,16,512]{5,4,3,2,1,0:T(8,128)(2,1)S(1)}, bf16[3,4,2,2,16,512]{5,4,3,2,1,0:T(8,128)(2,1)S(1)}, u32[]{:S(2)}, u32[]{:S(2)}) collective-permute-start(bf16[3,4,2,2,16,512]{5,4,3,2,1,0:T(8,128)(2,1)S(1)} %pad_maximum_fusion.xs_ref), channel_id=1, source_target_pairs={{0,4},{4,0},{1,5},{5,1},{2,6},{6,2},{3,7},{7,3},{8,12},{12,8},{9,1... | collective-permute-start | bytes 2359304 | tf_op jit(solution)/shard_map/ppermute | solution.py:137
  118.5 4.2 %collective-permute-start.20 = (bf16[3,4,2,2,16,512]{5,4,3,2,1,0:T(8,128)(2,1)S(1)}, bf16[3,4,2,2,16,512]{5,4,3,2,1,0:T(8,128)(2,1)S(1)}, u32[]{:S(2)}, u32[]{:S(2)}) collective-permute-start(bf16[3,4,2,2,16,512]{5,4,3,2,1,0:T(8,128)(2,1)S(1)} %pad_maximum_fusion.1.ys_ref), channel_id=1, source_target_pairs={{0,4},{4,0},{1,5},{5,1},{2,6},{6,2},{3,7},{7,3},{8,12},{12,8},{9,1... | collective-permute-start | bytes 2359304 | tf_op jit(solution)/shard_map/ppermute | solution.py:137
  124.7 2.1 %shard_map.78 = bf16[4,2,4,2,4,16,512]{6,5,4,3,2,1,0:T(8,128)(2,1)} custom-call(bf16[2,4,2,2,16,512]{5,4,3,2,1,0:T(8,128)(2,1)S(1)} %pad_maximum_fusion.2.own, bf16[3,4,2,2,16,512]{5,4,3,2,1,0:T(8,128)(2,1)S(1)} %pad_maximum_fusion.xs_ref, bf16[3,4,2,2,16,512]{5,4,3,2,1,0:T(8,128)(2,1)S(1)} %pad_maximum_fusion.1.ys_ref, ...), custom_call_target="tpu_custom_call" | custom-call | tf_op jit(solution)/shard_map/pallas_call | solution.py:139
  (67 shorter events, 16.4 us)
Async XLA Ops:
  2.8 4.9 %copy-start.3 = (f32[64,512]{1,0:T(8,128)S(1)}, f32[64,512]{1,0:T(8,128)}, u32[]{:S(2)}) copy-start(f32[64,512]{1,0:T(8,128)} %param.7) | copy-start | bytes 393220
  2.8 4.9 %copy-start.4 = (f32[64,512]{1,0:T(8,128)S(1)}, f32[64,512]{1,0:T(8,128)}, u32[]{:S(2)}) copy-start(f32[64,512]{1,0:T(8,128)} %param.6) | copy-start | bytes 393220
  4.4 7.5 %collective-permute-start = (bf16[32,64,512]{2,1,0:T(8,128)(2,1)}, bf16[32,64,512]{2,1,0:T(8,128)(2,1)}, u32[]{:S(2)}, u32[]{:S(2)}) collective-permute-start(bf16[32,64,512]{2,1,0:T(8,128)(2,1)} %shard_map.76), channel_id=1, source_target_pairs={{0,4},{4,0},{1,5},{5,1},{2,6},{6,2},{3,7},{7,3},{8,12},{12,8},{9,1... | collective-permute-start | bytes 6291464 | tf_op jit(solution)/shard_map/ppermute | solution.py:191
  7.8 7.6 %collective-permute-start.1 = (f32[1,3,16,512]{3,2,0,1:T(8,128)S(1)}, f32[1,3,16,512]{3,2,0,1:T(8,128)S(1)}, u32[]{:S(2)}, u32[]{:S(2)}) collective-permute-start(f32[1,3,16,512]{3,2,0,1:T(8,128)S(1)} %maximum_bitcast_fusion.3), channel_id=1, source_target_pairs={{0,64},{64,0},{128,192},{192,128},{1,65},{65,1},{129,193},{193,129... | collective-permute-start | bytes 294920 | tf_op jit(solution)/shard_map/ppermute | solution.py:27
  50.3 6.6 %collective-permute-start.2 = (f32[64,512]{1,0:T(8,128)S(1)}, f32[64,512]{1,0:T(8,128)S(1)}, u32[]{:S(2)}, u32[]{:S(2)}) collective-permute-start(f32[64,512]{1,0:T(8,128)S(1)} %fusion.4), channel_id=1, source_target_pairs={{0,64},{64,0},{128,192},{192,128},{1,65},{65,1},{129,193},{193,129... | collective-permute-start | bytes 393224 | tf_op jit(solution)/shard_map/ppermute | solution.py:27
  52.4 13.7 %collective-permute-start.4 = (f32[2,3,16,512]{3,2,0,1:T(8,128)S(1)}, f32[2,3,16,512]{3,2,0,1:T(8,128)S(1)}, u32[]{:S(2)}, u32[]{:S(2)}) collective-permute-start(f32[2,3,16,512]{3,2,0,1:T(8,128)S(1)} %pad_maximum_fusion.3), channel_id=1, source_target_pairs={{0,192},{64,128},{128,64},{192,0},{1,193},{65,129},{129,65},{193,1... | collective-permute-start | bytes 589832 | tf_op jit(solution)/shard_map/ppermute | solution.py:27
  57.0 9.2 %collective-permute-start.3 = (f32[64,512]{1,0:T(8,128)S(1)}, f32[64,512]{1,0:T(8,128)S(1)}, u32[]{:S(2)}, u32[]{:S(2)}) collective-permute-start(f32[64,512]{1,0:T(8,128)S(1)} %add.97), channel_id=1, source_target_pairs={{0,192},{64,128},{128,64},{192,0},{1,193},{65,129},{129,65},{193,1... | collective-permute-start | bytes 393224 | tf_op jit(solution)/shard_map/ppermute | solution.py:27
  68.1 19.2 %all-to-all-start.1 = ((f32[64,1,1]{2,1,0:T(1,128)}), f32[64,1,1]{2,1,0:T(1,128)S(1)}, u32[]{:S(2)}, u32[]{:S(2)}) async-start(f32[64,1,1]{2,1,0:T(1,128)} %broadcast_in_dim.18), calls=%async_computation.1 | async-start | bytes 65536 | tf_op jit(solution)/shard_map/all_to_all | solution.py:21
  88.8 3.2 %collective-permute-start.5 = (bf16[4,16,512]{2,1,0:T(8,128)(2,1)S(1)}, bf16[4,16,512]{2,1,0:T(8,128)(2,1)S(1)}, u32[]{:S(2)}, u32[]{:S(2)}) collective-permute-start(bf16[4,16,512]{2,1,0:T(8,128)(2,1)S(1)} %bitcast.77), channel_id=1, source_target_pairs={{0,32},{32,0},{1,33},{33,1},{2,34},{34,2},{3,35},{35,3},{4,36},{36... | collective-permute-start | bytes 196616 | tf_op jit(solution)/shard_map/ppermute | solution.py:127
  92.0 4.4 %collective-permute-start.8 = (bf16[2,2,16,512]{3,2,1,0:T(8,128)(2,1)S(1)}, bf16[2,2,16,512]{3,2,1,0:T(8,128)(2,1)S(1)}, u32[]{:S(2)}, u32[]{:S(2)}) collective-permute-start(bf16[2,2,16,512]{3,2,1,0:T(8,128)(2,1)S(1)} %get-tuple-element.41), channel_id=1, source_target_pairs={{0,24},{8,0},{16,8},{24,16},{1,25},{9,1},{17,9},{25,17},{2,26},{10... | collective-permute-start | bytes 196616 | tf_op jit(solution)/shard_map/ppermute | solution.py:86
  92.7 4.6 %collective-permute-start.7 = (bf16[2,2,16,512]{3,2,1,0:T(8,128)(2,1)S(1)}, bf16[2,2,16,512]{3,2,1,0:T(8,128)(2,1)S(1)}, u32[]{:S(2)}, u32[]{:S(2)}) collective-permute-start(bf16[2,2,16,512]{3,2,1,0:T(8,128)(2,1)S(1)} %get-tuple-element.41), channel_id=1, source_target_pairs={{0,16},{8,24},{16,0},{24,8},{1,17},{9,25},{17,1},{25,9},{2,18},{10... | collective-permute-start | bytes 196616 | tf_op jit(solution)/shard_map/ppermute | solution.py:86
  94.2 4.3 %collective-permute-start.6 = (bf16[2,2,16,512]{3,2,1,0:T(8,128)(2,1)S(1)}, bf16[2,2,16,512]{3,2,1,0:T(8,128)(2,1)S(1)}, u32[]{:S(2)}, u32[]{:S(2)}) collective-permute-start(bf16[2,2,16,512]{3,2,1,0:T(8,128)(2,1)S(1)} %get-tuple-element.41), channel_id=1, source_target_pairs={{0,8},{8,16},{16,24},{24,0},{1,9},{9,17},{17,25},{25,1},{2,10},{10... | collective-permute-start | bytes 196616 | tf_op jit(solution)/shard_map/ppermute | solution.py:86
  94.3 4.3 %collective-permute-start.11 = (bf16[6,16,512]{2,1,0:T(8,128)(2,1)S(1)}, bf16[6,16,512]{2,1,0:T(8,128)(2,1)S(1)}, u32[]{:S(2)}, u32[]{:S(2)}) collective-permute-start(bf16[6,16,512]{2,1,0:T(8,128)(2,1)S(1)} %pad_maximum_fusion.4), channel_id=1, source_target_pairs={{0,3},{1,0},{2,1},{3,2},{4,7},{5,4},{6,5},{7,6},{8,11},{9,8},{10,9... | collective-permute-start | bytes 294920 | tf_op jit(solution)/shard_map/ppermute | solution.py:86
  95.0 5.2 %collective-permute-start.10 = (bf16[6,16,512]{2,1,0:T(8,128)(2,1)S(1)}, bf16[6,16,512]{2,1,0:T(8,128)(2,1)S(1)}, u32[]{:S(2)}, u32[]{:S(2)}) collective-permute-start(bf16[6,16,512]{2,1,0:T(8,128)(2,1)S(1)} %pad_maximum_fusion.4), channel_id=1, source_target_pairs={{0,2},{1,3},{2,0},{3,1},{4,6},{5,7},{6,4},{7,5},{8,10},{9,11},{10,... | collective-permute-start | bytes 294920 | tf_op jit(solution)/shard_map/ppermute | solution.py:86
  96.4 5.0 %collective-permute-start.9 = (bf16[6,16,512]{2,1,0:T(8,128)(2,1)S(1)}, bf16[6,16,512]{2,1,0:T(8,128)(2,1)S(1)}, u32[]{:S(2)}, u32[]{:S(2)}) collective-permute-start(bf16[6,16,512]{2,1,0:T(8,128)(2,1)S(1)} %pad_maximum_fusion.4), channel_id=1, source_target_pairs={{0,1},{1,2},{2,3},{3,0},{4,5},{5,6},{6,7},{7,4},{8,9},{9,10},{10,1... | collective-permute-start | bytes 294920 | tf_op jit(solution)/shard_map/ppermute | solution.py:86
  101.5 5.5 %collective-permute-start.14 = (bf16[4,2,2,16,512]{4,3,2,1,0:T(8,128)(2,1)S(1)}, bf16[4,2,2,16,512]{4,3,2,1,0:T(8,128)(2,1)S(1)}, u32[]{:S(2)}, u32[]{:S(2)}) collective-permute-start(bf16[4,2,2,16,512]{4,3,2,1,0:T(8,128)(2,1)S(1)} %get-tuple-element.33), channel_id=1, source_target_pairs={{0,3},{1,0},{2,1},{3,2},{4,7},{5,4},{6,5},{7,6},{8,11},{9,8},{10,9... | collective-permute-start | bytes 786440 | tf_op jit(solution)/shard_map/ppermute | solution.py:86
  102.4 6.8 %collective-permute-start.13 = (bf16[4,2,2,16,512]{4,3,2,1,0:T(8,128)(2,1)S(1)}, bf16[4,2,2,16,512]{4,3,2,1,0:T(8,128)(2,1)S(1)}, u32[]{:S(2)}, u32[]{:S(2)}) collective-permute-start(bf16[4,2,2,16,512]{4,3,2,1,0:T(8,128)(2,1)S(1)} %get-tuple-element.33), channel_id=1, source_target_pairs={{0,2},{1,3},{2,0},{3,1},{4,6},{5,7},{6,4},{7,5},{8,10},{9,11},{10,... | collective-permute-start | bytes 786440 | tf_op jit(solution)/shard_map/ppermute | solution.py:86
  104.1 11.7 %collective-permute-start.12 = (bf16[4,2,2,16,512]{4,3,2,1,0:T(8,128)(2,1)S(1)}, bf16[4,2,2,16,512]{4,3,2,1,0:T(8,128)(2,1)S(1)}, u32[]{:S(2)}, u32[]{:S(2)}) collective-permute-start(bf16[4,2,2,16,512]{4,3,2,1,0:T(8,128)(2,1)S(1)} %get-tuple-element.33), channel_id=1, source_target_pairs={{0,1},{1,2},{2,3},{3,0},{4,5},{5,6},{6,7},{7,4},{8,9},{9,10},{10,1... | collective-permute-start | bytes 786440 | tf_op jit(solution)/shard_map/ppermute | solution.py:86
  104.1 14.3 %collective-permute-start.17 = (bf16[4,2,2,16,512]{4,3,2,1,0:T(8,128)(2,1)S(1)}, bf16[4,2,2,16,512]{4,3,2,1,0:T(8,128)(2,1)S(1)}, u32[]{:S(2)}, u32[]{:S(2)}) collective-permute-start(bf16[4,2,2,16,512]{4,3,2,1,0:T(8,128)(2,1)S(1)} %get-tuple-element.32), channel_id=1, source_target_pairs={{0,24},{8,0},{16,8},{24,16},{1,25},{9,1},{17,9},{25,17},{2,26},{10... | collective-permute-start | bytes 786440 | tf_op jit(solution)/shard_map/ppermute | solution.py:86
  106.7 11.7 %collective-permute-start.16 = (bf16[4,2,2,16,512]{4,3,2,1,0:T(8,128)(2,1)S(1)}, bf16[4,2,2,16,512]{4,3,2,1,0:T(8,128)(2,1)S(1)}, u32[]{:S(2)}, u32[]{:S(2)}) collective-permute-start(bf16[4,2,2,16,512]{4,3,2,1,0:T(8,128)(2,1)S(1)} %get-tuple-element.32), channel_id=1, source_target_pairs={{0,16},{8,24},{16,0},{24,8},{1,17},{9,25},{17,1},{25,9},{2,18},{10... | collective-permute-start | bytes 786440 | tf_op jit(solution)/shard_map/ppermute | solution.py:86
  107.0 11.4 %collective-permute-start.15 = (bf16[4,2,2,16,512]{4,3,2,1,0:T(8,128)(2,1)S(1)}, bf16[4,2,2,16,512]{4,3,2,1,0:T(8,128)(2,1)S(1)}, u32[]{:S(2)}, u32[]{:S(2)}) collective-permute-start(bf16[4,2,2,16,512]{4,3,2,1,0:T(8,128)(2,1)S(1)} %get-tuple-element.32), channel_id=1, source_target_pairs={{0,8},{8,16},{16,24},{24,0},{1,9},{9,17},{17,25},{25,1},{2,10},{10... | collective-permute-start | bytes 786440 | tf_op jit(solution)/shard_map/ppermute | solution.py:86
  109.2 14.4 %collective-permute-start.18 = (bf16[2,4,2,2,16,512]{5,4,3,2,1,0:T(8,128)(2,1)S(1)}, bf16[2,4,2,2,16,512]{5,4,3,2,1,0:T(8,128)(2,1)S(1)}, u32[]{:S(2)}, u32[]{:S(2)}) collective-permute-start(bf16[2,4,2,2,16,512]{5,4,3,2,1,0:T(8,128)(2,1)S(1)} %pad_maximum_fusion.2.own), channel_id=1, source_target_pairs={{0,4},{4,0},{1,5},{5,1},{2,6},{6,2},{3,7},{7,3},{8,12},{12,8},{9,1... | collective-permute-start | bytes 1572872 | tf_op jit(solution)/shard_map/ppermute | solution.py:137
  115.8 7.7 %collective-permute-start.19 = (bf16[3,4,2,2,16,512]{5,4,3,2,1,0:T(8,128)(2,1)S(1)}, bf16[3,4,2,2,16,512]{5,4,3,2,1,0:T(8,128)(2,1)S(1)}, u32[]{:S(2)}, u32[]{:S(2)}) collective-permute-start(bf16[3,4,2,2,16,512]{5,4,3,2,1,0:T(8,128)(2,1)S(1)} %pad_maximum_fusion.xs_ref), channel_id=1, source_target_pairs={{0,4},{4,0},{1,5},{5,1},{2,6},{6,2},{3,7},{7,3},{8,12},{12,8},{9,1... | collective-permute-start | bytes 2359304 | tf_op jit(solution)/shard_map/ppermute | solution.py:137
  118.5 6.1 %collective-permute-start.20 = (bf16[3,4,2,2,16,512]{5,4,3,2,1,0:T(8,128)(2,1)S(1)}, bf16[3,4,2,2,16,512]{5,4,3,2,1,0:T(8,128)(2,1)S(1)}, u32[]{:S(2)}, u32[]{:S(2)}) collective-permute-start(bf16[3,4,2,2,16,512]{5,4,3,2,1,0:T(8,128)(2,1)S(1)} %pad_maximum_fusion.1.ys_ref), channel_id=1, source_target_pairs={{0,4},{4,0},{1,5},{5,1},{2,6},{6,2},{3,7},{7,3},{8,12},{12,8},{9,1... | collective-permute-start | bytes 2359304 | tf_op jit(solution)/shard_map/ppermute | solution.py:137
  (3 other events, 9.3 us)

commit v6 on v5

--- a/solution.py
+++ b/solution.py
@@ -39,10 +39,10 @@
     return jnp.concatenate([jnp.where(low, block, other), jnp.where(low, other, block)])
 
 
-def rows_of_core(local, swapped):
+def rows_of_core(local):
     def kernel(source, out, sem):
         core = lax.axis_index("c")
-        copy = pltpu.make_async_copy(source.at[:, 1 - core if swapped else core], out, sem)
+        copy = pltpu.make_async_copy(source.at[:, core], out, sem)
         copy.start()
         copy.wait()
 
@@ -186,8 +186,8 @@
     other_states = neighbour(states, "zh", 1)
 
     local = grads[0].reshape(-1, c, x * rows, width)
-    theirs = rows_of_core(local, True)
-    ours = rows_of_core(local, False)
+    theirs = lax.dynamic_index_in_dim(local, 1 - lax.axis_index("c"), 1, keepdims=False)
+    ours = rows_of_core(local)
     coded = add_and_encode(ours, lax.ppermute(theirs, "c", SWAP), (zh, zl, y, x, rows, width))
     coded, states, other_states = lax.optimization_barrier((coded, states, other_states))
     coded, states = lax.optimization_barrier((coded, interleaved(states, other_states, "zh", 1)))

time: 127 us -> 127 us (level)
  Pallas kernels: 6.59 us -> 5.04 us
    squeeze x0 -> x1, local copies, waits for them, and re-layouts: none -> 3.2 us  [body(): lax.dynamic_index_in_dim(local, 1 - lax.axis_index('c'), 1, keepdims=False)]
    unnamed x10 -> x8, local copies, waits for them, and re-layouts: 4.38 us -> 2.2 us
    pallas_call x2 -> x1, Pallas kernels: 1.7 us -> 0.15 us  [rows_of_core(): pl.pallas_call(kernel, out_shape=jax.ShapeDtypeStruct((blocks, rows, widt...]
where the time goes in v6:
time: 127 us; the launch traced here: 126 us
  starting transfers between devices  46.7 us (37%)
  blocking collectives  33.6 us (26%)
  waiting for transfers between devices  28.4 us (22%)
  local copies, waits for them, and re-layouts  6.76 us (5%)
  Pallas kernels  5.04 us (4%)
  other arithmetic  4.13 us (3%)
  between operations  1.78 us (1%)
    all_to_all x1, blocking collectives, body(): pieces = lax.all_to_all(coded, PLANE, 0, 0, tiled=True)  33.6 us
    ppermute x3, starting transfers between devices, gather_weights(): there = [lax.ppermute(piece, 'c', SWAP) for piece in here]  13.1 us
    all_to_all x1, starting transfers between devices, to_all(): lax.all_to_all(jnp.broadcast_to(block[None], (length, *block.shape)), axe...  11.1 us
    ppermute x12, starting transfers between devices, around(): lax.ppermute(block, axis, [(i, (i + k) % n) for i in range(n)])  10.9 us
    ppermute x4, waiting for transfers between devices, neighbour(): return lax.ppermute(block, axis, [(i, i ^ mask) for i in range(4)])  9.81 us
    ppermute x4, starting transfers between devices, neighbour(): return lax.ppermute(block, axis, [(i, i ^ mask) for i in range(4)])  8.18 us
    all_to_all x1, waiting for transfers between devices, to_all(): lax.all_to_all(jnp.broadcast_to(block[None], (length, *block.shape)), axe...  7.84 us
    ppermute x12, waiting for transfers between devices, around(): lax.ppermute(block, axis, [(i, (i + k) % n) for i in range(n)])  6.3 us
  transfers between devices with their start and end apart: 22, of which 14 were waited for; matrix products, arithmetic and copies ran while one was open for 1% of the time, Pallas kernels for 2%

profile of v6, /device:TPU:1, one launch (start us, length us, event | category | flops | bytes accessed | tf_op | source)
XLA Modules:
  0.0 126.3 jit_solution(9848610261812460058)
XLA Ops:
  0.7 3.2 %dynamic-slice_bitcast_fusion = bf16[32,64,512]{2,1,0:T(8,128)(2,1)} fusion(bf16[32,2,64,512]{3,2,1,0:T(8,128)(2,1)} %bitcast.74, s32[]{:T(128)S(6)} %select_n.57), kind=kLoop, calls=%fused_computation.8 | loop fusion | bytes 4194308 | tf_op jit(solution)/shard_map/jit(dynamic_index_in_dim)/squeeze | solution.py:189
  3.9 3.2 %collective-permute-start = (bf16[32,64,512]{2,1,0:T(8,128)(2,1)}, bf16[32,64,512]{2,1,0:T(8,128)(2,1)}, u32[]{:S(2)}, u32[]{:S(2)}) collective-permute-start(bf16[32,64,512]{2,1,0:T(8,128)(2,1)} %dynamic-slice_bitcast_fusion), channel_id=1, source_target_pairs={{0,4},{4,0},{1,5},{5,1},{2,6},{6,2},{3,7},{7,3},{8,12},{12,8},{9,1... | collective-permute-start | bytes 6291464 | tf_op jit(solution)/shard_map/ppermute | solution.py:191
  7.2 1.3 %collective-permute-start.1 = (f32[1,3,16,512]{3,2,0,1:T(8,128)S(1)}, f32[1,3,16,512]{3,2,0,1:T(8,128)S(1)}, u32[]{:S(2)}, u32[]{:S(2)}) collective-permute-start(f32[1,3,16,512]{3,2,0,1:T(8,128)S(1)} %maximum_bitcast_fusion.3), channel_id=1, source_target_pairs={{0,64},{64,0},{128,192},{192,128},{1,65},{65,1},{129,193},{193,129... | collective-permute-start | bytes 294920 | tf_op jit(solution)/shard_map/ppermute | solution.py:27
  8.5 2.2 %copy-done = bf16[1,4096,512]{2,1,0:T(8,128)(2,1)S(1)} copy-done((bf16[1,4096,512]{2,1,0:T(8,128)(2,1)S(1)}, bf16[1,4096,512]{2,1,0:T(8,128)(2,1)}, u32[]{:S(2)}) %copy-start) | copy-done | bytes 4194328
  11.2 2.8 %shard_map.76 = bf16[32,64,512]{2,1,0:T(8,128)(2,1)S(1)} custom-call(bf16[32,64,512]{2,1,0:T(8,128)(2,1)S(1)} %shard_map.75.ours, bf16[32,64,512]{2,1,0:T(8,128)(2,1)} %collective-permute-done.theirs), custom_call_target="tpu_custom_call" | custom-call | tf_op jit(solution)/shard_map/pallas_call | solution.py:75
  14.8 33.6 %all_to_all.11 = bf16[32,64,512]{2,1,0:T(8,128)(2,1)S(1)} all-to-all(bf16[32,64,512]{2,1,0:T(8,128)(2,1)S(1)} %shard_map.76), channel_id=1, replica_groups=mesh['zh'=4,'zl'=2,'y'=4,'c'=2,'x'=4] {'zl','y','x'}, dimensions={0} | all-to-all | bytes 4194304 | tf_op jit(solution)/shard_map/all_to_all | solution.py:194
  48.4 1.4 %fusion.4 = f32[64,512]{1,0:T(8,128)S(1)} fusion(bf16[32,64,512]{2,1,0:T(8,128)(2,1)S(1)} %all_to_all.11), kind=kLoop, calls=%fused_computation.7 | loop fusion | flops 8355840 | bytes 2228224 | tf_op jit(solution)/shard_map/reduce_sum | solution.py:195
  49.8 2.1 %collective-permute-start.2 = (f32[64,512]{1,0:T(8,128)S(1)}, f32[64,512]{1,0:T(8,128)S(1)}, u32[]{:S(2)}, u32[]{:S(2)}) collective-permute-start(f32[64,512]{1,0:T(8,128)S(1)} %fusion.4), channel_id=1, source_target_pairs={{0,64},{64,0},{128,192},{192,128},{1,65},{65,1},{129,193},{193,129... | collective-permute-start | bytes 393224 | tf_op jit(solution)/shard_map/ppermute | solution.py:27
  51.9 2.6 %collective-permute-start.4 = (f32[2,3,16,512]{3,2,0,1:T(8,128)S(1)}, f32[2,3,16,512]{3,2,0,1:T(8,128)S(1)}, u32[]{:S(2)}, u32[]{:S(2)}) collective-permute-start(f32[2,3,16,512]{3,2,0,1:T(8,128)S(1)} %pad_maximum_fusion.3), channel_id=1, source_target_pairs={{0,192},{64,128},{128,64},{192,0},{1,193},{65,129},{129,65},{193,1... | collective-permute-start | bytes 589832 | tf_op jit(solution)/shard_map/ppermute | solution.py:27
  54.4 2.0 %collective-permute-done.2 = f32[64,512]{1,0:T(8,128)S(1)} collective-permute-done((f32[64,512]{1,0:T(8,128)S(1)}, f32[64,512]{1,0:T(8,128)S(1)}, u32[]{:S(2)}, u32[]{:S(2)}) %collective-permute-start.2) | collective-permute-done | bytes 131104 | tf_op jit(solution)/shard_map/ppermute | solution.py:27
  56.4 2.2 %collective-permute-start.3 = (f32[64,512]{1,0:T(8,128)S(1)}, f32[64,512]{1,0:T(8,128)S(1)}, u32[]{:S(2)}, u32[]{:S(2)}) collective-permute-start(f32[64,512]{1,0:T(8,128)S(1)} %add.103), channel_id=1, source_target_pairs={{0,192},{64,128},{128,64},{192,0},{1,193},{65,129},{129,65},{193,1... | collective-permute-start | bytes 393224 | tf_op jit(solution)/shard_map/ppermute | solution.py:27
  58.6 7.0 %collective-permute-done.3 = f32[64,512]{1,0:T(8,128)S(1)} collective-permute-done((f32[64,512]{1,0:T(8,128)S(1)}, f32[64,512]{1,0:T(8,128)S(1)}, u32[]{:S(2)}, u32[]{:S(2)}) %collective-permute-start.3) | collective-permute-done | bytes 131104 | tf_op jit(solution)/shard_map/ppermute | solution.py:27
  67.6 11.1 %all-to-all-start.1 = ((f32[64,1,1]{2,1,0:T(1,128)}), f32[64,1,1]{2,1,0:T(1,128)S(1)}, u32[]{:S(2)}, u32[]{:S(2)}) async-start(f32[64,1,1]{2,1,0:T(1,128)} %broadcast_in_dim.18), calls=%async_computation.1 | async-start | bytes 65536 | tf_op jit(solution)/shard_map/all_to_all | solution.py:21
  78.9 7.8 %all-to-all-done.1 = f32[64,1,1]{2,1,0:T(1,128)S(1)} async-done(((f32[64,1,1]{2,1,0:T(1,128)}), f32[64,1,1]{2,1,0:T(1,128)S(1)}, u32[]{:S(2)}, u32[]{:S(2)}) %all-to-all-start.1) | async-done | bytes 288 | tf_op jit(solution)/shard_map/all_to_all | solution.py:21
  88.4 3.0 %collective-permute-done.5 = bf16[4,16,512]{2,1,0:T(8,128)(2,1)S(1)} collective-permute-done((bf16[4,16,512]{2,1,0:T(8,128)(2,1)S(1)}, bf16[4,16,512]{2,1,0:T(8,128)(2,1)S(1)}, u32[]{:S(2)}, u32[]{:S(2)}) %collective-permute-start.5) | collective-permute-done | bytes 65568 | tf_op jit(solution)/shard_map/ppermute | solution.py:127
  92.1 1.5 %collective-permute-start.7 = (bf16[2,2,16,512]{3,2,1,0:T(8,128)(2,1)S(1)}, bf16[2,2,16,512]{3,2,1,0:T(8,128)(2,1)S(1)}, u32[]{:S(2)}, u32[]{:S(2)}) collective-permute-start(bf16[2,2,16,512]{3,2,1,0:T(8,128)(2,1)S(1)} %get-tuple-element.41), channel_id=1, source_target_pairs={{0,16},{8,24},{16,0},{24,8},{1,17},{9,25},{17,1},{25,9},{2,18},{10... | collective-permute-start | bytes 196616 | tf_op jit(solution)/shard_map/ppermute | solution.py:86
  94.4 1.5 %collective-permute-start.10 = (bf16[6,16,512]{2,1,0:T(8,128)(2,1)S(1)}, bf16[6,16,512]{2,1,0:T(8,128)(2,1)S(1)}, u32[]{:S(2)}, u32[]{:S(2)}) collective-permute-start(bf16[6,16,512]{2,1,0:T(8,128)(2,1)S(1)} %pad_maximum_fusion.4), channel_id=1, source_target_pairs={{0,2},{1,3},{2,0},{3,1},{4,6},{5,7},{6,4},{7,5},{8,10},{9,11},{10,... | collective-permute-start | bytes 294920 | tf_op jit(solution)/shard_map/ppermute | solution.py:86
  98.0 1.5 %collective-permute-done.10 = bf16[6,16,512]{2,1,0:T(8,128)(2,1)S(1)} collective-permute-done((bf16[6,16,512]{2,1,0:T(8,128)(2,1)S(1)}, bf16[6,16,512]{2,1,0:T(8,128)(2,1)S(1)}, u32[]{:S(2)}, u32[]{:S(2)}) %collective-permute-start.10) | collective-permute-done | bytes 98336 | tf_op jit(solution)/shard_map/ppermute | solution.py:86
  101.8 1.7 %collective-permute-start.13 = (bf16[4,2,2,16,512]{4,3,2,1,0:T(8,128)(2,1)S(1)}, bf16[4,2,2,16,512]{4,3,2,1,0:T(8,128)(2,1)S(1)}, u32[]{:S(2)}, u32[]{:S(2)}) collective-permute-start(bf16[4,2,2,16,512]{4,3,2,1,0:T(8,128)(2,1)S(1)} %get-tuple-element.33), channel_id=1, source_target_pairs={{0,2},{1,3},{2,0},{3,1},{4,6},{5,7},{6,4},{7,5},{8,10},{9,11},{10,... | collective-permute-start | bytes 786440 | tf_op jit(solution)/shard_map/ppermute | solution.py:86
  103.5 2.6 %collective-permute-start.17 = (bf16[4,2,2,16,512]{4,3,2,1,0:T(8,128)(2,1)S(1)}, bf16[4,2,2,16,512]{4,3,2,1,0:T(8,128)(2,1)S(1)}, u32[]{:S(2)}, u32[]{:S(2)}) collective-permute-start(bf16[4,2,2,16,512]{4,3,2,1,0:T(8,128)(2,1)S(1)} %get-tuple-element.32), channel_id=1, source_target_pairs={{0,24},{8,0},{16,8},{24,16},{1,25},{9,1},{17,9},{25,17},{2,26},{10... | collective-permute-start | bytes 786440 | tf_op jit(solution)/shard_map/ppermute | solution.py:86
  108.6 6.3 %collective-permute-start.18 = (bf16[2,4,2,2,16,512]{5,4,3,2,1,0:T(8,128)(2,1)S(1)}, bf16[2,4,2,2,16,512]{5,4,3,2,1,0:T(8,128)(2,1)S(1)}, u32[]{:S(2)}, u32[]{:S(2)}) collective-permute-start(bf16[2,4,2,2,16,512]{5,4,3,2,1,0:T(8,128)(2,1)S(1)} %pad_maximum_fusion.2.own), channel_id=1, source_target_pairs={{0,4},{4,0},{1,5},{5,1},{2,6},{6,2},{3,7},{7,3},{8,12},{12,8},{9,1... | collective-permute-start | bytes 1572872 | tf_op jit(solution)/shard_map/ppermute | solution.py:137
  115.2 2.5 %collective-permute-start.19 = (bf16[3,4,2,2,16,512]{5,4,3,2,1,0:T(8,128)(2,1)S(1)}, bf16[3,4,2,2,16,512]{5,4,3,2,1,0:T(8,128)(2,1)S(1)}, u32[]{:S(2)}, u32[]{:S(2)}) collective-permute-start(bf16[3,4,2,2,16,512]{5,4,3,2,1,0:T(8,128)(2,1)S(1)} %pad_maximum_fusion.xs_ref), channel_id=1, source_target_pairs={{0,4},{4,0},{1,5},{5,1},{2,6},{6,2},{3,7},{7,3},{8,12},{12,8},{9,1... | collective-permute-start | bytes 2359304 | tf_op jit(solution)/shard_map/ppermute | solution.py:137
  117.9 4.2 %collective-permute-start.20 = (bf16[3,4,2,2,16,512]{5,4,3,2,1,0:T(8,128)(2,1)S(1)}, bf16[3,4,2,2,16,512]{5,4,3,2,1,0:T(8,128)(2,1)S(1)}, u32[]{:S(2)}, u32[]{:S(2)}) collective-permute-start(bf16[3,4,2,2,16,512]{5,4,3,2,1,0:T(8,128)(2,1)S(1)} %pad_maximum_fusion.1.ys_ref), channel_id=1, source_target_pairs={{0,4},{4,0},{1,5},{5,1},{2,6},{6,2},{3,7},{7,3},{8,12},{12,8},{9,1... | collective-permute-start | bytes 2359304 | tf_op jit(solution)/shard_map/ppermute | solution.py:137
  124.1 2.1 %shard_map.77 = bf16[4,2,4,2,4,16,512]{6,5,4,3,2,1,0:T(8,128)(2,1)} custom-call(bf16[2,4,2,2,16,512]{5,4,3,2,1,0:T(8,128)(2,1)S(1)} %pad_maximum_fusion.2.own, bf16[3,4,2,2,16,512]{5,4,3,2,1,0:T(8,128)(2,1)S(1)} %pad_maximum_fusion.xs_ref, bf16[3,4,2,2,16,512]{5,4,3,2,1,0:T(8,128)(2,1)S(1)} %pad_maximum_fusion.1.ys_ref, ...), custom_call_target="tpu_custom_call" | custom-call | tf_op jit(solution)/shard_map/pallas_call | solution.py:139
  (65 shorter events, 15.0 us)
Async XLA Ops:
  0.6 6.5 %copy-start.1 = (f32[64,512]{1,0:T(8,128)S(1)}, f32[64,512]{1,0:T(8,128)}, u32[]{:S(2)}) copy-start(f32[64,512]{1,0:T(8,128)} %param.5) | copy-start | bytes 393220
  0.6 6.5 %copy-start.2 = (f32[64,512]{1,0:T(8,128)S(1)}, f32[64,512]{1,0:T(8,128)}, u32[]{:S(2)}) copy-start(f32[64,512]{1,0:T(8,128)} %param.7) | copy-start | bytes 393220
  3.9 7.4 %collective-permute-start = (bf16[32,64,512]{2,1,0:T(8,128)(2,1)}, bf16[32,64,512]{2,1,0:T(8,128)(2,1)}, u32[]{:S(2)}, u32[]{:S(2)}) collective-permute-start(bf16[32,64,512]{2,1,0:T(8,128)(2,1)} %dynamic-slice_bitcast_fusion), channel_id=1, source_target_pairs={{0,4},{4,0},{1,5},{5,1},{2,6},{6,2},{3,7},{7,3},{8,12},{12,8},{9,1... | collective-permute-start | bytes 6291464 | tf_op jit(solution)/shard_map/ppermute | solution.py:191
  7.2 7.6 %collective-permute-start.1 = (f32[1,3,16,512]{3,2,0,1:T(8,128)S(1)}, f32[1,3,16,512]{3,2,0,1:T(8,128)S(1)}, u32[]{:S(2)}, u32[]{:S(2)}) collective-permute-start(f32[1,3,16,512]{3,2,0,1:T(8,128)S(1)} %maximum_bitcast_fusion.3), channel_id=1, source_target_pairs={{0,64},{64,0},{128,192},{192,128},{1,65},{65,1},{129,193},{193,129... | collective-permute-start | bytes 294920 | tf_op jit(solution)/shard_map/ppermute | solution.py:27
  49.8 6.6 %collective-permute-start.2 = (f32[64,512]{1,0:T(8,128)S(1)}, f32[64,512]{1,0:T(8,128)S(1)}, u32[]{:S(2)}, u32[]{:S(2)}) collective-permute-start(f32[64,512]{1,0:T(8,128)S(1)} %fusion.4), channel_id=1, source_target_pairs={{0,64},{64,0},{128,192},{192,128},{1,65},{65,1},{129,193},{193,129... | collective-permute-start | bytes 393224 | tf_op jit(solution)/shard_map/ppermute | solution.py:27
  51.9 13.8 %collective-permute-start.4 = (f32[2,3,16,512]{3,2,0,1:T(8,128)S(1)}, f32[2,3,16,512]{3,2,0,1:T(8,128)S(1)}, u32[]{:S(2)}, u32[]{:S(2)}) collective-permute-start(f32[2,3,16,512]{3,2,0,1:T(8,128)S(1)} %pad_maximum_fusion.3), channel_id=1, source_target_pairs={{0,192},{64,128},{128,64},{192,0},{1,193},{65,129},{129,65},{193,1... | collective-permute-start | bytes 589832 | tf_op jit(solution)/shard_map/ppermute | solution.py:27
  56.4 9.2 %collective-permute-start.3 = (f32[64,512]{1,0:T(8,128)S(1)}, f32[64,512]{1,0:T(8,128)S(1)}, u32[]{:S(2)}, u32[]{:S(2)}) collective-permute-start(f32[64,512]{1,0:T(8,128)S(1)} %add.103), channel_id=1, source_target_pairs={{0,192},{64,128},{128,64},{192,0},{1,193},{65,129},{129,65},{193,1... | collective-permute-start | bytes 393224 | tf_op jit(solution)/shard_map/ppermute | solution.py:27
  67.6 19.1 %all-to-all-start.1 = ((f32[64,1,1]{2,1,0:T(1,128)}), f32[64,1,1]{2,1,0:T(1,128)S(1)}, u32[]{:S(2)}, u32[]{:S(2)}) async-start(f32[64,1,1]{2,1,0:T(1,128)} %broadcast_in_dim.18), calls=%async_computation.1 | async-start | bytes 65536 | tf_op jit(solution)/shard_map/all_to_all | solution.py:21
  88.2 3.2 %collective-permute-start.5 = (bf16[4,16,512]{2,1,0:T(8,128)(2,1)S(1)}, bf16[4,16,512]{2,1,0:T(8,128)(2,1)S(1)}, u32[]{:S(2)}, u32[]{:S(2)}) collective-permute-start(bf16[4,16,512]{2,1,0:T(8,128)(2,1)S(1)} %bitcast.79), channel_id=1, source_target_pairs={{0,32},{32,0},{1,33},{33,1},{2,34},{34,2},{3,35},{35,3},{4,36},{36... | collective-permute-start | bytes 196616 | tf_op jit(solution)/shard_map/ppermute | solution.py:127
  91.4 4.4 %collective-permute-start.8 = (bf16[2,2,16,512]{3,2,1,0:T(8,128)(2,1)S(1)}, bf16[2,2,16,512]{3,2,1,0:T(8,128)(2,1)S(1)}, u32[]{:S(2)}, u32[]{:S(2)}) collective-permute-start(bf16[2,2,16,512]{3,2,1,0:T(8,128)(2,1)S(1)} %get-tuple-element.41), channel_id=1, source_target_pairs={{0,24},{8,0},{16,8},{24,16},{1,25},{9,1},{17,9},{25,17},{2,26},{10... | collective-permute-start | bytes 196616 | tf_op jit(solution)/shard_map/ppermute | solution.py:86
  92.1 4.6 %collective-permute-start.7 = (bf16[2,2,16,512]{3,2,1,0:T(8,128)(2,1)S(1)}, bf16[2,2,16,512]{3,2,1,0:T(8,128)(2,1)S(1)}, u32[]{:S(2)}, u32[]{:S(2)}) collective-permute-start(bf16[2,2,16,512]{3,2,1,0:T(8,128)(2,1)S(1)} %get-tuple-element.41), channel_id=1, source_target_pairs={{0,16},{8,24},{16,0},{24,8},{1,17},{9,25},{17,1},{25,9},{2,18},{10... | collective-permute-start | bytes 196616 | tf_op jit(solution)/shard_map/ppermute | solution.py:86
  93.6 4.3 %collective-permute-start.6 = (bf16[2,2,16,512]{3,2,1,0:T(8,128)(2,1)S(1)}, bf16[2,2,16,512]{3,2,1,0:T(8,128)(2,1)S(1)}, u32[]{:S(2)}, u32[]{:S(2)}) collective-permute-start(bf16[2,2,16,512]{3,2,1,0:T(8,128)(2,1)S(1)} %get-tuple-element.41), channel_id=1, source_target_pairs={{0,8},{8,16},{16,24},{24,0},{1,9},{9,17},{17,25},{25,1},{2,10},{10... | collective-permute-start | bytes 196616 | tf_op jit(solution)/shard_map/ppermute | solution.py:86
  93.7 4.3 %collective-permute-start.11 = (bf16[6,16,512]{2,1,0:T(8,128)(2,1)S(1)}, bf16[6,16,512]{2,1,0:T(8,128)(2,1)S(1)}, u32[]{:S(2)}, u32[]{:S(2)}) collective-permute-start(bf16[6,16,512]{2,1,0:T(8,128)(2,1)S(1)} %pad_maximum_fusion.4), channel_id=1, source_target_pairs={{0,3},{1,0},{2,1},{3,2},{4,7},{5,4},{6,5},{7,6},{8,11},{9,8},{10,9... | collective-permute-start | bytes 294920 | tf_op jit(solution)/shard_map/ppermute | solution.py:86
  94.4 5.2 %collective-permute-start.10 = (bf16[6,16,512]{2,1,0:T(8,128)(2,1)S(1)}, bf16[6,16,512]{2,1,0:T(8,128)(2,1)S(1)}, u32[]{:S(2)}, u32[]{:S(2)}) collective-permute-start(bf16[6,16,512]{2,1,0:T(8,128)(2,1)S(1)} %pad_maximum_fusion.4), channel_id=1, source_target_pairs={{0,2},{1,3},{2,0},{3,1},{4,6},{5,7},{6,4},{7,5},{8,10},{9,11},{10,... | collective-permute-start | bytes 294920 | tf_op jit(solution)/shard_map/ppermute | solution.py:86
  95.8 5.0 %collective-permute-start.9 = (bf16[6,16,512]{2,1,0:T(8,128)(2,1)S(1)}, bf16[6,16,512]{2,1,0:T(8,128)(2,1)S(1)}, u32[]{:S(2)}, u32[]{:S(2)}) collective-permute-start(bf16[6,16,512]{2,1,0:T(8,128)(2,1)S(1)} %pad_maximum_fusion.4), channel_id=1, source_target_pairs={{0,1},{1,2},{2,3},{3,0},{4,5},{5,6},{6,7},{7,4},{8,9},{9,10},{10,1... | collective-permute-start | bytes 294920 | tf_op jit(solution)/shard_map/ppermute | solution.py:86
  100.9 5.5 %collective-permute-start.14 = (bf16[4,2,2,16,512]{4,3,2,1,0:T(8,128)(2,1)S(1)}, bf16[4,2,2,16,512]{4,3,2,1,0:T(8,128)(2,1)S(1)}, u32[]{:S(2)}, u32[]{:S(2)}) collective-permute-start(bf16[4,2,2,16,512]{4,3,2,1,0:T(8,128)(2,1)S(1)} %get-tuple-element.33), channel_id=1, source_target_pairs={{0,3},{1,0},{2,1},{3,2},{4,7},{5,4},{6,5},{7,6},{8,11},{9,8},{10,9... | collective-permute-start | bytes 786440 | tf_op jit(solution)/shard_map/ppermute | solution.py:86
  101.8 6.8 %collective-permute-start.13 = (bf16[4,2,2,16,512]{4,3,2,1,0:T(8,128)(2,1)S(1)}, bf16[4,2,2,16,512]{4,3,2,1,0:T(8,128)(2,1)S(1)}, u32[]{:S(2)}, u32[]{:S(2)}) collective-permute-start(bf16[4,2,2,16,512]{4,3,2,1,0:T(8,128)(2,1)S(1)} %get-tuple-element.33), channel_id=1, source_target_pairs={{0,2},{1,3},{2,0},{3,1},{4,6},{5,7},{6,4},{7,5},{8,10},{9,11},{10,... | collective-permute-start | bytes 786440 | tf_op jit(solution)/shard_map/ppermute | solution.py:86
  103.5 11.7 %collective-permute-start.12 = (bf16[4,2,2,16,512]{4,3,2,1,0:T(8,128)(2,1)S(1)}, bf16[4,2,2,16,512]{4,3,2,1,0:T(8,128)(2,1)S(1)}, u32[]{:S(2)}, u32[]{:S(2)}) collective-permute-start(bf16[4,2,2,16,512]{4,3,2,1,0:T(8,128)(2,1)S(1)} %get-tuple-element.33), channel_id=1, source_target_pairs={{0,1},{1,2},{2,3},{3,0},{4,5},{5,6},{6,7},{7,4},{8,9},{9,10},{10,1... | collective-permute-start | bytes 786440 | tf_op jit(solution)/shard_map/ppermute | solution.py:86
  103.5 14.3 %collective-permute-start.17 = (bf16[4,2,2,16,512]{4,3,2,1,0:T(8,128)(2,1)S(1)}, bf16[4,2,2,16,512]{4,3,2,1,0:T(8,128)(2,1)S(1)}, u32[]{:S(2)}, u32[]{:S(2)}) collective-permute-start(bf16[4,2,2,16,512]{4,3,2,1,0:T(8,128)(2,1)S(1)} %get-tuple-element.32), channel_id=1, source_target_pairs={{0,24},{8,0},{16,8},{24,16},{1,25},{9,1},{17,9},{25,17},{2,26},{10... | collective-permute-start | bytes 786440 | tf_op jit(solution)/shard_map/ppermute | solution.py:86
  106.1 11.7 %collective-permute-start.16 = (bf16[4,2,2,16,512]{4,3,2,1,0:T(8,128)(2,1)S(1)}, bf16[4,2,2,16,512]{4,3,2,1,0:T(8,128)(2,1)S(1)}, u32[]{:S(2)}, u32[]{:S(2)}) collective-permute-start(bf16[4,2,2,16,512]{4,3,2,1,0:T(8,128)(2,1)S(1)} %get-tuple-element.32), channel_id=1, source_target_pairs={{0,16},{8,24},{16,0},{24,8},{1,17},{9,25},{17,1},{25,9},{2,18},{10... | collective-permute-start | bytes 786440 | tf_op jit(solution)/shard_map/ppermute | solution.py:86
  106.4 11.4 %collective-permute-start.15 = (bf16[4,2,2,16,512]{4,3,2,1,0:T(8,128)(2,1)S(1)}, bf16[4,2,2,16,512]{4,3,2,1,0:T(8,128)(2,1)S(1)}, u32[]{:S(2)}, u32[]{:S(2)}) collective-permute-start(bf16[4,2,2,16,512]{4,3,2,1,0:T(8,128)(2,1)S(1)} %get-tuple-element.32), channel_id=1, source_target_pairs={{0,8},{8,16},{16,24},{24,0},{1,9},{9,17},{17,25},{25,1},{2,10},{10... | collective-permute-start | bytes 786440 | tf_op jit(solution)/shard_map/ppermute | solution.py:86
  108.6 14.4 %collective-permute-start.18 = (bf16[2,4,2,2,16,512]{5,4,3,2,1,0:T(8,128)(2,1)S(1)}, bf16[2,4,2,2,16,512]{5,4,3,2,1,0:T(8,128)(2,1)S(1)}, u32[]{:S(2)}, u32[]{:S(2)}) collective-permute-start(bf16[2,4,2,2,16,512]{5,4,3,2,1,0:T(8,128)(2,1)S(1)} %pad_maximum_fusion.2.own), channel_id=1, source_target_pairs={{0,4},{4,0},{1,5},{5,1},{2,6},{6,2},{3,7},{7,3},{8,12},{12,8},{9,1... | collective-permute-start | bytes 1572872 | tf_op jit(solution)/shard_map/ppermute | solution.py:137
  115.2 7.7 %collective-permute-start.19 = (bf16[3,4,2,2,16,512]{5,4,3,2,1,0:T(8,128)(2,1)S(1)}, bf16[3,4,2,2,16,512]{5,4,3,2,1,0:T(8,128)(2,1)S(1)}, u32[]{:S(2)}, u32[]{:S(2)}) collective-permute-start(bf16[3,4,2,2,16,512]{5,4,3,2,1,0:T(8,128)(2,1)S(1)} %pad_maximum_fusion.xs_ref), channel_id=1, source_target_pairs={{0,4},{4,0},{1,5},{5,1},{2,6},{6,2},{3,7},{7,3},{8,12},{12,8},{9,1... | collective-permute-start | bytes 2359304 | tf_op jit(solution)/shard_map/ppermute | solution.py:137
  117.9 6.1 %collective-permute-start.20 = (bf16[3,4,2,2,16,512]{5,4,3,2,1,0:T(8,128)(2,1)S(1)}, bf16[3,4,2,2,16,512]{5,4,3,2,1,0:T(8,128)(2,1)S(1)}, u32[]{:S(2)}, u32[]{:S(2)}) collective-permute-start(bf16[3,4,2,2,16,512]{5,4,3,2,1,0:T(8,128)(2,1)S(1)} %pad_maximum_fusion.1.ys_ref), channel_id=1, source_target_pairs={{0,4},{4,0},{1,5},{5,1},{2,6},{6,2},{3,7},{7,3},{8,12},{12,8},{9,1... | collective-permute-start | bytes 2359304 | tf_op jit(solution)/shard_map/ppermute | solution.py:137
  (2 other events, 8.7 us)
